TPU v7x, 32 devices: a whole 2x2x4 slice. The times are simulated.
32 devices in a mesh: groups: 2 (over y), blk: 4 (over x, core), layer: 4 (over z).
Axes of the slice: x: 2, y: 2, z: 4, core: 2. Of those that a mesh axis runs over, the one named last changes fastest.
Arguments:
- train_grads: bfloat16 [2048, 4, 4096], P(('groups', 'blk'), 'layer'), parts along dimension 0, may hold values from -6 to 6
- query_grads: bfloat16 [2048, 4, 4096], P(('groups', 'blk'), 'layer'), parts along dimension 0, may hold values from -6 to 6
- eigenvalues: float32 [4, 4096], P('layer'), may hold values from 0.02 to 2
- order: int32 [6, 256], P('groups'), parts along dimension 0, may hold values from 0 to 255, each once within a row
Outputs:
- scores: float32 [3, 256, 2048], P(None, 'layer', ('groups', 'blk')), parts along dimension 2
There are 2 independent parts, one for each index of `groups`. A program takes and returns all parts, laid end to end along the dimension named above; an argument that names none is the same for every part. Nothing has to cross between parts.
Inputs may be any that keep to these rules, and one draw needn't show every extreme that they name: Each row of order is a permutation of 0 .. 255.
All inputs are finite; a program needn't handle non-finite values.
Results may differ from a plain program's by a relative error of at most 0.0029.
Values may be sent and summed in bfloat16 or wider, within the bound.
No kernel may reach another device: no remote copies, remote signals or barrier semaphores. Data moves between devices by JAX's collectives and lax.ppermute only.
A program may use at most 64 MiB of HBM per device.

v0:
```python
import jax
import jax.numpy as jnp
from jax import lax
from jax.sharding import PartitionSpec as P

STEPS = 3


def from_behind(x, axis, by):
    length = lax.axis_size(axis)
    return lax.ppermute(x, axis, [(i, (i + by) % length) for i in range(length)])


def per_device(train_grads, query_grads, eigenvalues, order):
    weights = 1.0 / (eigenvalues + 0.05)
    scaled = (query_grads.astype(jnp.float32) * weights[None, :, :]).astype(jnp.bfloat16)
    tf = train_grads.astype(jnp.float32)
    local_self = jnp.sum(tf * tf * weights[None, :, :], axis=(1, 2))
    selfinf = lax.psum(local_self, "layer")
    inverse = 1.0 / jnp.sqrt(selfinf)
    rows = train_grads.shape[0]
    queries = scaled.shape[0]
    train_flat = train_grads.reshape(rows, -1)
    current = scaled
    outputs = []
    for step in range(STEPS):
        if step > 0:
            current = from_behind(current, "blk", 1)
        block_flat = current.reshape(queries, -1)
        partial_value = lax.dot_general(
            block_flat, train_flat, (((1,), (1,)), ((), ())), preferred_element_type=jnp.float32
        )
        partial_value = jnp.take(partial_value, order[step], axis=0)
        summed = lax.psum_scatter(partial_value, "layer", scatter_dimension=0, tiled=True)
        outputs.append(summed * inverse[None, :])
    return jnp.stack(outputs, axis=0)


def solution(mesh):
    return jax.shard_map(
        per_device,
        mesh=mesh,
        in_specs=(
            P(("groups", "blk"), "layer", None),
            P(("groups", "blk"), "layer", None),
            P("layer", None),
            P("groups", None),
        ),
        out_specs=P(None, "layer", ("groups", "blk")),
        check_vma=False,
    )
```

profile of v0, /device:TPU:0, one launch (start us, length us, event | category | flops | bytes accessed | tf_op | source)
XLA Modules:
  0.0 110.0 jit_solution(2437187728798118487)
XLA Ops:
  6.5 0.7 add_divide_fusion
  7.3 4.7 %multiply_reduce_fusion = (f32[256]{0:T(256)S(1)}, bf16[256,1,4096]{2,0,1:T(8,128)(2,1)}) fusion(bf16[256,1,4096]{2,0,1:T(8,128)(2,1)} %param.6, f32[4096]{0:T(1024)S(1)} %bitcast.26, bf16[256,1,4096]{2,0,1:T(8,128)(2,1)} %param.7), kind=kLoop, calls=%fused_computation.3 | loop fusion | flops 7339776 | bytes 6308864 | tf_op jit(solution)/shard_map/reduce_sum | solution.py:18
  12.0 0.5 collective-permute-start
  12.5 2.3 %fusion.6 = f32[256,256]{1,0:T(8,128)S(1)} fusion(bf16[256,1,4096]{2,0,1:T(8,128)(2,1)S(1)} %copy-done, bf16[256,1,4096]{2,0,1:T(8,128)(2,1)} %get-tuple-element.7), kind=kOutput, calls=%fused_computation.11 | convolution fusion | flops 536870912 | bytes 4456448 | tf_op jit(solution)/shard_map/dot_general | solution.py:30
  14.8 1.0 gather_fusion
  15.8 22.6 %collective-permute-done = bf16[256,1,4096]{2,0,1:T(8,128)(2,1)} collective-permute-done((bf16[256,1,4096]{2,0,1:T(8,128)(2,1)}, bf16[256,1,4096]{2,0,1:T(8,128)(2,1)}, u32[]{:S(2)}, u32[]{:S(2)}) %collective-permute-start) | collective-permute-done | bytes 2097184 | tf_op jit(solution)/shard_map/ppermute | solution.py:11
  38.4 0.8 broadcast_select_fusion.2
  39.2 0.0 reduce-scatter.4.cloned.1.call-update
  39.3 0.0 reduce-scatter.6.cloned.1.call-start
  39.4 2.3 %fusion.2 = f32[256,256]{1,0:T(8,128)S(1)} fusion(bf16[256,1,4096]{2,0,1:T(8,128)(2,1)} %collective-permute-done, bf16[256,1,4096]{2,0,1:T(8,128)(2,1)S(1)} %copy-done), kind=kOutput, calls=%fused_computation.7 | convolution fusion | flops 536870912 | bytes 4456448 | tf_op jit(solution)/shard_map/dot_general | solution.py:30
  41.7 1.0 gather_fusion.1
  42.7 0.8 broadcast_select_fusion.1
  43.5 0.0 reduce-scatter.6.cloned.1.call-update
  43.5 0.0 reduce-scatter.8.cloned.1.call-start
  43.6 20.6 %collective-permute-done.1 = bf16[256,1,4096]{2,0,1:T(8,128)(2,1)} collective-permute-done((bf16[256,1,4096]{2,0,1:T(8,128)(2,1)}, bf16[256,1,4096]{2,0,1:T(8,128)(2,1)}, u32[]{:S(2)}, u32[]{:S(2)}) %collective-permute-start.1) | collective-permute-done | bytes 2097184 | tf_op jit(solution)/shard_map/ppermute | solution.py:11
  64.2 2.3 %fusion = f32[256,256]{1,0:T(8,128)S(1)} fusion(bf16[256,1,4096]{2,0,1:T(8,128)(2,1)} %collective-permute-done.1, bf16[256,1,4096]{2,0,1:T(8,128)(2,1)S(1)} %copy-done), kind=kOutput, calls=%fused_computation.5 | convolution fusion | flops 536870912 | bytes 4456448 | tf_op jit(solution)/shard_map/dot_general | solution.py:30
  66.5 1.0 gather_fusion.2
  67.5 0.8 broadcast_select_fusion
  68.3 0.0 reduce-scatter.8.cloned.1.call-update
  68.3 12.8 %psum.7 = f32[256]{0:T(256)S(1)} all-reduce(f32[256]{0:T(256)S(1)} %get-tuple-element.6), channel_id=1, replica_groups=mesh['groups'=2,'blk'=4,'layer'=4] {'layer'}, use_global_device_ids=true, to_apply=%region_2.0 | all-reduce | flops 256 | bytes 2048 | tf_op jit(solution)/shard_map/psum | solution.py:19
  81.1 0.7 reduce-scatter.6.cloned.1.call-done
  81.8 20.1 %reduce-scatter.8.cloned.1.call-done = f32[64,256]{1,0:T(8,128)} async-done(((f32[256,256]{1,0:T(8,128)}), f32[64,256]{1,0:T(8,128)}) %reduce-scatter.8.cloned.1.call-update) | async-done | bytes 65552 | tf_op jit(solution)/shard_map/reduce_scatter | solution.py:34
  101.9 0.9 multiply_bitcast_fusion.2
  102.8 0.7 pad_maximum_fusion
  (18 shorter events, 0.1 us)
Async XLA Ops:
  6.5 74.6 %reduce-scatter.4.cloned.1.call-start = ((), (), s32[]{:S(2)}) async-start(), calls=%async_computation.3 | async-start | bytes 327680 | tf_op jit(solution)/shard_map/reduce_scatter | solution.py:34
  7.3 5.2 %copy-start.1 = (s32[3,256]{1,0:T(4,128)S(1)}, s32[3,256]{1,0:T(4,128)}, u32[]{:S(2)}) copy-start(s32[3,256]{1,0:T(4,128)} %param.9) | copy-start | bytes 9220
  7.3 5.2 %copy-start = (bf16[256,1,4096]{2,0,1:T(8,128)(2,1)S(1)}, bf16[256,1,4096]{2,0,1:T(8,128)(2,1)}, u32[]{:S(2)}) copy-start(bf16[256,1,4096]{2,0,1:T(8,128)(2,1)} %param.6) | copy-start | bytes 6291460
  12.0 26.4 %collective-permute-start = (bf16[256,1,4096]{2,0,1:T(8,128)(2,1)}, bf16[256,1,4096]{2,0,1:T(8,128)(2,1)}, u32[]{:S(2)}, u32[]{:S(2)}) collective-permute-start(bf16[256,1,4096]{2,0,1:T(8,128)(2,1)} %get-tuple-element.7), channel_id=1, source_target_pairs={{0,4},{4,8},{8,12},{12,0},{1,5},{5,9},{9,13},{13,1},{2,6},{6,10},{... | collective-permute-start | bytes 6291464 | tf_op jit(solution)/shard_map/ppermute | solution.py:11
  38.4 25.8 %collective-permute-start.1 = (bf16[256,1,4096]{2,0,1:T(8,128)(2,1)}, bf16[256,1,4096]{2,0,1:T(8,128)(2,1)}, u32[]{:S(2)}, u32[]{:S(2)}) collective-permute-start(bf16[256,1,4096]{2,0,1:T(8,128)(2,1)} %collective-permute-done), channel_id=1, source_target_pairs={{0,4},{4,8},{8,12},{12,0},{1,5},{5,9},{9,13},{13,1},{2,6},{6,10},{... | collective-permute-start | bytes 6291464 | tf_op jit(solution)/shard_map/ppermute | solution.py:11
  39.3 42.5 %reduce-scatter.6.cloned.1.call-start = ((), (), s32[]{:S(2)}) async-start(), calls=%async_computation.4 | async-start | bytes 327680 | tf_op jit(solution)/shard_map/reduce_scatter | solution.py:34
  43.5 58.3 %reduce-scatter.8.cloned.1.call-start = ((), (), s32[]{:S(2)}) async-start(), calls=%async_computation.5 | async-start | bytes 327680 | tf_op jit(solution)/shard_map/reduce_scatter | solution.py:34
Sparse Core Ops, SparseCore 0:
  39.4 22.0 reduce-scatter.3
  63.8 17.9 reduce-scatter.5
  84.1 17.7 reduce-scatter.7
where the time goes:
time: 110 us
  waiting for transfers between devices  64 us (58%)
  between operations  13.2 us (12%)
  blocking collectives  12.8 us (12%)
  other arithmetic  9.51 us (9%)
  matrix products  6.99 us (6%)
  local copies, waits for them, and re-layouts  2.93 us (3%)
    ppermute x2, waiting for transfers between devices, from_behind(): lax.ppermute(x, axis, [(i, (i + by) % length) for i in range(length)])  43.2 us
    reduce_scatter x3, waiting for transfers between devices, per_device(): lax.psum_scatter(partial_value, 'layer', scatter_dimension=0, tiled=True)  20.7 us
    psum x1, blocking collectives, per_device(): selfinf = lax.psum(local_self, 'layer')  12.8 us
    dot_general x3, matrix products, per_device(): lax.dot_general(block_flat, train_flat, (((1,), (1,)), ((), ())), preferr...  6.99 us
    reduce_sum x1, other arithmetic, per_device(): local_self = jnp.sum(tf * tf * weights[None, :, :], axis=(1, 2))  4.7 us
    gather x3, local copies, waits for them, and re-layouts, per_device(): partial_value = jnp.take(partial_value, order[step], axis=0)  2.91 us
    select_n x6, other arithmetic, per_device(): partial_value = jnp.take(partial_value, order[step], axis=0)  2.41 us
  transfers between devices with their start and end apart: 5, of which 4 were waited for; matrix products, arithmetic and copies ran while one was open for 11% of the time, Pallas kernels for 0%

commit v1 on v0

v1 whole, which is shorter than its diff:
```python
import functools

import jax
import jax.numpy as jnp
from jax import lax
from jax.experimental import pallas as pl
from jax.experimental.pallas import tpu as pltpu
from jax.sharding import PartitionSpec as P

STEPS = 3
TAIL = 64
DEPTH = 512
EXTRA = 8
F32, BF16 = jnp.float32, jnp.bfloat16


def after(x, *earlier):
    return lax.optimization_barrier((x,) + earlier)[0]


def scaled(x, weights):
    return (x.astype(F32) * weights).astype(BF16)


def dot_rows(x, t):
    return lax.dot_general(x, t, (((1,), (1,)), ((), ())), preferred_element_type=F32)


def choose(order_row, p):
    queries = p.shape[0]
    hot = (lax.broadcasted_iota(jnp.int32, (queries, order_row.shape[1]), 0) == order_row).astype(F32).astype(BF16)
    total = None
    for _ in range(3):
        term = p.astype(BF16)
        p = p - term.astype(F32)
        part = lax.dot_general(hot, term, (((0,), (0,)), ((), ())), preferred_element_type=F32)
        total = part if total is None else total + part
    return total


def block_kernel(kind, layers, *refs):
    place, x_refs = refs[0], refs[1 : 1 + (2 if kind == "mixed" else 1)]
    refs = refs[1 + len(x_refs) :]
    t_ref, eig_ref, order_ref = refs[:3]
    outs, (acc, self_acc) = refs[3 : 3 + layers], refs[3 + layers :]
    step, steps = pl.program_id(0), pl.num_programs(0)
    me, odd = place[0], place[1]

    @pl.when(step == 0)
    def _():
        acc[...] = jnp.zeros_like(acc)
        self_acc[...] = jnp.zeros_like(self_acc)

    weights = 1.0 / (eig_ref[...] + 0.05)
    t = t_ref[...]
    if kind == "mixed":

        @pl.when(odd == 1)
        def _():
            acc[...] += dot_rows(scaled(x_refs[0][...], weights), t)

        @pl.when(odd == 0)
        def _():
            head = x_refs[1].shape[0]
            acc[:head] += dot_rows(scaled(x_refs[1][...], weights), t)

    else:
        acc[...] += dot_rows(scaled(x_refs[0][...], weights), t)
    if kind == "first":
        tf = t.astype(F32)
        square = tf * tf * weights
        part = square[:, :128]
        for k in range(128, square.shape[1], 128):
            part = part + square[:, k : k + 128]
        self_acc[...] += part

    @pl.when(step == steps - 1)
    def _():
        acc[...] = choose(order_ref[...], acc[...])
        own = acc.shape[0] // layers
        if kind == "first":
            row = jnp.sum(self_acc[...].T, axis=0, keepdims=True)
            extra = jnp.broadcast_to(row, (EXTRA, row.shape[1]))
        for by in range(layers):
            start = pl.multiple_of(lax.rem(me + by, layers) * own, own)
            outs[by][:own] = acc[pl.ds(start, own)]
            if kind == "first":
                outs[by][own:] = extra


def block_call(kind, layers, place, xs, t, eig, order_row):
    rows, depth = t.shape
    queries = order_row.shape[1]
    own = queries // layers + (EXTRA if kind == "first" else 0)
    x_specs = [pl.BlockSpec((x.shape[0], DEPTH), lambda k, place: (0, k)) for x in xs]
    if kind == "mixed":
        x_specs[0] = pl.BlockSpec((queries, DEPTH), lambda k, place: (0, k * place[1]))
        x_specs[1] = pl.BlockSpec((xs[1].shape[0], DEPTH), lambda k, place: (0, k * (1 - place[1])))
    return pl.pallas_call(
        functools.partial(block_kernel, kind, layers),
        grid_spec=pltpu.PrefetchScalarGridSpec(
            num_scalar_prefetch=1,
            grid=(depth // DEPTH,),
            in_specs=x_specs
            + [
                pl.BlockSpec((rows, DEPTH), lambda k, place: (0, k)),
                pl.BlockSpec((1, DEPTH), lambda k, place: (0, k)),
                pl.BlockSpec((1, queries), lambda k, place: (0, 0)),
            ],
            out_specs=[pl.BlockSpec((own, rows), lambda k, place: (0, 0))] * layers,
            scratch_shapes=[pltpu.VMEM((queries, rows), F32), pltpu.VMEM((rows, 128), F32)],
        ),
        out_shape=[jax.ShapeDtypeStruct((own, rows), F32)] * layers,
        compiler_params=pltpu.CompilerParams(vmem_limit_bytes=24 << 20),
        cost_estimate=pl.CostEstimate(
            flops=2 * queries * rows * depth, bytes_accessed=4 * queries * depth, transcendentals=0
        ),
        name="block_" + kind,
    )(place, *xs, t, eig, order_row)


def tail_kernel(x_ref, t_ref, eig_ref, out_ref):
    @pl.when(pl.program_id(0) == 0)
    def _():
        out_ref[...] = jnp.zeros_like(out_ref)

    out_ref[...] += dot_rows(scaled(x_ref[...], 1.0 / (eig_ref[...] + 0.05)), t_ref[...])


def tail_call(x, t, eig):
    rows, depth = t.shape
    tail = x.shape[0]
    return pl.pallas_call(
        tail_kernel,
        grid=(depth // DEPTH,),
        in_specs=[
            pl.BlockSpec((tail, DEPTH), lambda k: (0, k)),
            pl.BlockSpec((rows, DEPTH), lambda k: (0, k)),
            pl.BlockSpec((1, DEPTH), lambda k: (0, k)),
        ],
        out_specs=pl.BlockSpec((tail, rows), lambda k: (0, 0)),
        out_shape=jax.ShapeDtypeStruct((tail, rows), F32),
        compiler_params=pltpu.CompilerParams(vmem_limit_bytes=24 << 20),
        cost_estimate=pl.CostEstimate(flops=2 * tail * rows * depth, bytes_accessed=2 * rows * depth, transcendentals=0),
        name="tail_product",
    )(x, t, eig)


def added(refs):
    total = refs[0][...]
    for ref in refs[1:]:
        total = total + ref[...]
    return total


def base_kernel(layers, *refs):
    ins, (out_ref, inverse_ref) = refs[:-2], refs[-2:]
    own = out_ref.shape[1]
    first, second = added(ins[:layers]), added(ins[layers:])
    inverse = 1.0 / jnp.sqrt(first[own : own + 1])
    inverse_ref[...] = inverse
    out_ref[0] = first[:own] * inverse
    out_ref[1] = second * inverse
    out_ref[2] = jnp.zeros_like(second)


def base_call(layers, sums0, sums1):
    own, rows = sums1[0].shape
    return pl.pallas_call(
        functools.partial(base_kernel, layers),
        out_shape=[jax.ShapeDtypeStruct((STEPS, own, rows), F32), jax.ShapeDtypeStruct((1, rows), F32)],
        name="base",
    )(*sums0, *sums1)


def final_kernel(layers, first_row, base_ref, inverse_ref, order_ref, *refs):
    sums, terms, out_ref = refs[:layers], refs[layers:-1], refs[-1]
    chosen = choose(order_ref[...] - first_row, added(terms))
    out_ref[0] = (added(sums) + chosen) * inverse_ref[...]


def final_call(layers, first_row, base, inverse, order_row, sums, terms):
    _, own, rows = base.shape
    last = pl.BlockSpec((1, own, rows), lambda i: (STEPS - 1, 0, 0))

    def whole(x):
        return pl.BlockSpec(x.shape, lambda i: (0, 0))

    return pl.pallas_call(
        functools.partial(final_kernel, layers, first_row),
        grid=(1,),
        in_specs=[pl.BlockSpec(memory_space=pl.ANY), whole(inverse), whole(order_row)]
        + [whole(x) for x in (*sums, *terms)],
        out_specs=last,
        out_shape=jax.ShapeDtypeStruct(base.shape, F32),
        input_output_aliases={0: 0},
        name="final",
    )(base, inverse, order_row, *sums, *terms)


def per_device(train_grads, query_grads, eigenvalues, order):
    rows, queries = train_grads.shape[0], query_grads.shape[0]
    blks, layers = lax.axis_size("blk"), lax.axis_size("layer")
    own = queries // layers
    head = queries - TAIL
    me = lax.axis_index("layer")
    place = jnp.stack([me, lax.axis_index("blk") % 2]).astype(jnp.int32)
    evens = range(0, blks, 2)
    t = train_grads.reshape(rows, -1)
    q = query_grads.reshape(queries, -1)
    order_rows = [order[s : s + 1] for s in range(STEPS)]
    own_order = lax.dynamic_slice(order_rows[2], (0, me * own), (1, own))

    odd_on = [(i + 1, (i + 3) % blks) for i in evens]
    even_on = [(i, (i + 2) % blks) for i in evens]
    to_odd = [(i, i + 1) for i in evens]
    to_even = [(i + 1, i) for i in evens]

    def exchange(pieces):
        got = [pieces[0]]
        for by in range(1, layers):
            got.append(lax.ppermute(pieces[by], "layer", [(i, (i + by) % layers) for i in range(layers)]))
        return got

    odd_two = lax.ppermute(q, "blk", odd_on)
    odd_one = lax.ppermute(q, "blk", to_odd)
    sums0 = exchange(block_call("first", layers, place, [q], t, eigenvalues, order_rows[0]))
    main, last = lax.optimization_barrier((q[:head], q[head:], *sums0))[:2]
    even_one = lax.ppermute(after(odd_two, main, last), "blk", to_even)
    main = lax.ppermute(main, "blk", even_on)
    last = lax.ppermute(last, "blk", even_on)

    sums1 = exchange(block_call("mixed", layers, place, [odd_one, even_one], t, eigenvalues, order_rows[1]))
    base, inverse = base_call(layers, sums0, sums1)

    main = after(main, inverse)
    pieces2 = block_call("mixed", layers, place, [odd_two, main], t, eigenvalues, order_rows[2])
    sums2 = exchange(pieces2)
    tail = tail_call(after(last, *pieces2), t, eigenvalues)
    terms = [tail]
    for by in range(1, layers):
        pairs = [(i * layers + k, i * layers + (k + by) % layers) for i in evens for k in range(layers)]
        terms.append(lax.ppermute(tail, ("blk", "layer"), pairs))
    return final_call(layers, head, base, inverse, own_order, sums2, terms)


def solution(mesh):
    return jax.shard_map(
        per_device,
        mesh=mesh,
        in_specs=(
            P(("groups", "blk"), "layer", None),
            P(("groups", "blk"), "layer", None),
            P("layer", None),
            P("groups", None),
        ),
        out_specs=P(None, "layer", ("groups", "blk")),
        check_vma=False,
    )
```

time: 110 us -> 80.4 us (0.73)
  waiting for transfers between devices: 64 us -> 10.5 us
  starting transfers between devices: 0.54 us -> 40.1 us
  Pallas kernels: 0 us -> 20.2 us
  between operations: 13.2 us -> 0.26 us
  blocking collectives: 12.8 us -> 0 us
  other arithmetic: 9.51 us -> 0.07 us
  matrix products: 6.99 us -> 0 us
  local copies, waits for them, and re-layouts: 2.93 us -> 8.57 us
    ppermute x2 -> x17, starting transfers between devices: 0.46 us -> 40.1 us  [the longest x9 16.7 us: exchange(): lax.ppermute(pieces[by], 'layer', [(i, (i + by) % layers) for i in range(...]
    ppermute x2 -> x17, waiting for transfers between devices: 43.2 us -> 10.5 us  [the longest x9 9.09 us: exchange(): lax.ppermute(pieces[by], 'layer', [(i, (i + by) % layers) for i in range(...]
    reduce_scatter x3 -> x0, waiting for transfers between devices: 20.7 us -> none  [per_device(): lax.psum_scatter(partial_value, 'layer', scatter_dimension=0, tiled=True)]
    pallas_call x0 -> x6, Pallas kernels: none -> 20.2 us  [the longest x3 14.6 us: block_call(): pl.pallas_call(functools.partial(block_kernel, kind, layers), grid_spec=p...]
    psum x1 -> x0, blocking collectives: 12.8 us -> none  [per_device(): selfinf = lax.psum(local_self, 'layer')]
    dot_general x3 -> x0, matrix products: 6.99 us -> none  [per_device(): lax.dot_general(block_flat, train_flat, (((1,), (1,)), ((), ())), preferr...]
    unnamed x4 -> x42, local copies, waits for them, and re-layouts: 0.01 us -> 5.8 us
    reduce_sum x1 -> x0, other arithmetic: 4.7 us -> none  [per_device(): local_self = jnp.sum(tf * tf * weights[None, :, :], axis=(1, 2))]
  transfers between devices with their start and end apart: 5 -> 17, of which waited for: 4 -> 9; matrix products, arithmetic and copies ran while one was open for 11% -> 4% of each run, Pallas kernels for 0% -> 21%
where the time goes in v1:
time: 80.4 us; the launch traced here: 79.7 us
  starting transfers between devices  40.1 us (50%)
  Pallas kernels  20.2 us (25%)
  waiting for transfers between devices  10.5 us (13%)
  local copies, waits for them, and re-layouts  8.57 us (11%)
    ppermute x9, starting transfers between devices, exchange(): lax.ppermute(pieces[by], 'layer', [(i, (i + by) % layers) for i in range(...  16.7 us
    pallas_call x3, Pallas kernels, block_call(): pl.pallas_call(functools.partial(block_kernel, kind, layers), grid_spec=p...  14.6 us
    ppermute x9, waiting for transfers between devices, exchange(): lax.ppermute(pieces[by], 'layer', [(i, (i + by) % layers) for i in range(...  9.09 us
    ppermute x3, starting transfers between devices, per_device(): terms.append(lax.ppermute(tail, ('blk', 'layer'), pairs))  8.65 us
    unnamed x42, local copies, waits for them, and re-layouts  5.8 us
    ppermute x1, starting transfers between devices, per_device(): odd_one = lax.ppermute(q, 'blk', to_odd)  5.62 us
    ppermute x1, starting transfers between devices, per_device(): last = lax.ppermute(last, 'blk', even_on)  3.4 us
    ppermute x1, starting transfers between devices, per_device(): main = lax.ppermute(main, 'blk', even_on)  2.44 us
  transfers between devices with their start and end apart: 17, of which 9 were waited for; matrix products, arithmetic and copies ran while one was open for 4% of the time, Pallas kernels for 21%

profile of v1, /device:TPU:0, one launch (start us, length us, event | category | flops | bytes accessed | tf_op | source)
XLA Modules:
  0.0 79.7 jit_solution(10400227799768692485)
XLA Ops:
  0.0 2.0 %collective-permute-start.4 = (bf16[256,4096]{1,0:T(8,128)(2,1)}, bf16[256,4096]{1,0:T(8,128)(2,1)}, u32[]{:S(2)}, u32[]{:S(2)}) collective-permute-start(bf16[256,4096]{1,0:T(8,128)(2,1)} %bitcast.12), channel_id=1, source_target_pairs={{4,12},{12,4},{5,13},{13,5},{6,14},{14,6},{7,15},{15,7},{20,28},{2... | collective-permute-start | bytes 6291464 | tf_op jit(solution)/shard_map/ppermute | solution.py:225
  2.0 5.6 %collective-permute-start.3 = (bf16[256,4096]{1,0:T(8,128)(2,1)}, bf16[256,4096]{1,0:T(8,128)(2,1)}, u32[]{:S(2)}, u32[]{:S(2)}) collective-permute-start(bf16[256,4096]{1,0:T(8,128)(2,1)} %bitcast.13), channel_id=1, source_target_pairs={{0,4},{8,12},{1,5},{9,13},{2,6},{10,14},{3,7},{11,15},{16,20},{24,... | collective-permute-start | bytes 6291464 | tf_op jit(solution)/shard_map/ppermute | solution.py:226
  8.5 1.6 %copy-done = bf16[256,1,4096]{2,0,1:T(8,128)(2,1)S(1)} copy-done((bf16[256,1,4096]{2,0,1:T(8,128)(2,1)S(1)}, bf16[256,1,4096]{2,0,1:T(8,128)(2,1)}, u32[]{:S(2)}) %copy-start) | copy-done | bytes 2097176
  10.1 1.6 %copy-done.2 = bf16[256,1,4096]{2,0,1:T(8,128)(2,1)S(1)} copy-done((bf16[256,1,4096]{2,0,1:T(8,128)(2,1)S(1)}, bf16[256,1,4096]{2,0,1:T(8,128)(2,1)}, u32[]{:S(2)}) %copy-start.2) | copy-done | bytes 2097176
  12.4 3.6 %block_first.1 = (f32[72,256]{1,0:T(8,128)S(1)}, f32[72,256]{1,0:T(8,128)S(1)}, f32[72,256]{1,0:T(8,128)S(1)}, f32[72,256]{1,0:T(8,128)S(1)}) custom-call(s32[2]{0:T(128)S(1)} %pad_add_fusion.refs_0_, bf16[256,4096]{1,0:T(8,128)(2,1)S(1)} %bitcast.14, bf16[256,4096]{1,0:T(8,128)(2,1)S(1)} %bitcast.8, f32[1,4096]{1,0:T(1,128)S(1)} %copy-done.3, ...), custom_call_target="tpu_custom_call" | custom-call | flops 536870912 | bytes 4194304 | tf_op jit(solution)/shard_map/block_first/pallas_call | solution.py:99
  16.1 1.6 %collective-permute-start = (f32[72,256]{1,0:T(8,128)S(1)}, f32[72,256]{1,0:T(8,128)S(1)}, u32[]{:S(2)}, u32[]{:S(2)}) collective-permute-start(f32[72,256]{1,0:T(8,128)S(1)} %get-tuple-element.25), channel_id=1, source_target_pairs={{0,1},{1,2},{2,3},{3,0},{4,5},{5,6},{6,7},{7,4},{8,9},{9,10},{10,1... | collective-permute-start | bytes 221192 | tf_op jit(solution)/shard_map/ppermute | solution.py:222
  17.7 2.6 %collective-permute-start.1 = (f32[72,256]{1,0:T(8,128)S(1)}, f32[72,256]{1,0:T(8,128)S(1)}, u32[]{:S(2)}, u32[]{:S(2)}) collective-permute-start(f32[72,256]{1,0:T(8,128)S(1)} %get-tuple-element.26), channel_id=1, source_target_pairs={{0,2},{1,3},{2,0},{3,1},{4,6},{5,7},{6,4},{7,5},{8,10},{9,11},{10,... | collective-permute-start | bytes 221192 | tf_op jit(solution)/shard_map/ppermute | solution.py:222
  26.0 2.4 %collective-permute-start.9 = (bf16[192,4096]{1,0:T(8,128)(2,1)}, bf16[192,4096]{1,0:T(8,128)(2,1)}, u32[]{:S(2)}, u32[]{:S(2)}) collective-permute-start(bf16[192,4096]{1,0:T(8,128)(2,1)} %slice_bitcast_fusion), channel_id=1, source_target_pairs={{0,8},{8,0},{1,9},{9,1},{2,10},{10,2},{3,11},{11,3},{16,24},{24,16... | collective-permute-start | bytes 4718600 | tf_op jit(solution)/shard_map/ppermute | solution.py:230
  28.5 3.4 %collective-permute-start.13 = (bf16[64,4096]{1,0:T(8,128)(2,1)S(1)}, bf16[64,4096]{1,0:T(8,128)(2,1)S(1)}, u32[]{:S(2)}, u32[]{:S(2)}) collective-permute-start(bf16[64,4096]{1,0:T(8,128)(2,1)S(1)} %slice_bitcast_fusion.1), channel_id=1, source_target_pairs={{0,8},{8,0},{1,9},{9,1},{2,10},{10,2},{3,11},{11,3},{16,24},{24,16... | collective-permute-start | bytes 1572872 | tf_op jit(solution)/shard_map/ppermute | solution.py:231
  31.9 1.4 %collective-permute-done.5.refs_2_ = bf16[256,4096]{1,0:T(8,128)(2,1)S(1)} collective-permute-done((bf16[256,4096]{1,0:T(8,128)(2,1)}, bf16[256,4096]{1,0:T(8,128)(2,1)S(1)}, u32[]{:S(2)}, u32[]{:S(2)}) %collective-permute-start.5) | collective-permute-done | bytes 2097184 | tf_op jit(solution)/shard_map/ppermute | solution.py:229
  33.3 4.7 %block_mixed.2 = (f32[64,256]{1,0:T(8,128)S(1)}, f32[64,256]{1,0:T(8,128)S(1)}, f32[64,256]{1,0:T(8,128)S(1)}, f32[64,256]{1,0:T(8,128)S(1)}) custom-call(s32[2]{0:T(128)S(1)} %pad_add_fusion.refs_0_, bf16[256,4096]{1,0:T(8,128)(2,1)} %collective-permute-done.3.refs_1_, bf16[256,4096]{1,0:T(8,128)(2,1)S(1)} %collective-permute-done.5.refs_2_, ...), custom_call_target="tpu_custom_call" | custom-call | flops 536870912 | bytes 4194304 | tf_op jit(solution)/shard_map/block_mixed/pallas_call | solution.py:99
  38.6 1.8 %collective-permute-start.6 = (f32[64,256]{1,0:T(8,128)S(1)}, f32[64,256]{1,0:T(8,128)S(1)}, u32[]{:S(2)}, u32[]{:S(2)}) collective-permute-start(f32[64,256]{1,0:T(8,128)S(1)} %get-tuple-element.32), channel_id=1, source_target_pairs={{0,1},{1,2},{2,3},{3,0},{4,5},{5,6},{6,7},{7,4},{8,9},{9,10},{10,1... | collective-permute-start | bytes 196616 | tf_op jit(solution)/shard_map/ppermute | solution.py:222
  40.4 2.6 %collective-permute-start.7 = (f32[64,256]{1,0:T(8,128)S(1)}, f32[64,256]{1,0:T(8,128)S(1)}, u32[]{:S(2)}, u32[]{:S(2)}) collective-permute-start(f32[64,256]{1,0:T(8,128)S(1)} %get-tuple-element.33), channel_id=1, source_target_pairs={{0,2},{1,3},{2,0},{3,1},{4,6},{5,7},{6,4},{7,5},{8,10},{9,11},{10,... | collective-permute-start | bytes 196616 | tf_op jit(solution)/shard_map/ppermute | solution.py:222
  44.7 3.5 %collective-permute-done.7.refs_6_ = f32[64,256]{1,0:T(8,128)S(1)} collective-permute-done((f32[64,256]{1,0:T(8,128)S(1)}, f32[64,256]{1,0:T(8,128)S(1)}, u32[]{:S(2)}, u32[]{:S(2)}) %collective-permute-start.7) | collective-permute-done | bytes 65568 | tf_op jit(solution)/shard_map/ppermute | solution.py:222
  49.4 1.8 %base.1 = (f32[3,64,256]{2,1,0:T(8,128)}, f32[1,256]{1,0:T(1,128)}) custom-call(f32[72,256]{1,0:T(8,128)} %copy-done.6, f32[72,256]{1,0:T(8,128)} %copy-done.9, f32[72,256]{1,0:T(8,128)} %copy-done.10, f32[72,256]{1,0:T(8,128)} %copy-done.11, f32[64,256]{1,0:T(8,128)} %copy-done.7, f32[64,256]{1,0:T(8,128)} %copy-done.12, f32[64,256]{1,0:T(8,128)} %copy-done.13, ...), custom_call_target="tpu_custom_call" | custom-call | tf_op jit(solution)/shard_map/base/pallas_call | solution.py:169
  51.2 6.3 %block_mixed.3 = (f32[64,256]{1,0:T(8,128)S(1)}, f32[64,256]{1,0:T(8,128)S(1)}, f32[64,256]{1,0:T(8,128)S(1)}, f32[64,256]{1,0:T(8,128)S(1)}) custom-call(s32[2]{0:T(128)S(1)} %pad_add_fusion.refs_0_, bf16[256,4096]{1,0:T(8,128)(2,1)} %collective-permute-done.4.refs_1_, bf16[192,4096]{1,0:T(8,128)(2,1)} %collective-permute-done.9.refs_2_, ...), custom_call_target="tpu_custom_call" | custom-call | flops 536870912 | bytes 4194304 | tf_op jit(solution)/shard_map/block_mixed/pallas_call | solution.py:99
  57.5 1.9 %tail_product.1.refs_4_ = f32[64,256]{1,0:T(8,128)S(1)} custom-call(bf16[64,4096]{1,0:T(8,128)(2,1)S(1)} %collective-permute-done.13.x_ref, bf16[256,4096]{1,0:T(8,128)(2,1)S(1)} %bitcast.11, f32[1,4096]{1,0:T(1,128)S(1)} %copy-done.4), custom_call_target="tpu_custom_call" | custom-call | flops 134217728 | bytes 2097152 | tf_op jit(solution)/shard_map/tail_product/pallas_call | solution.py:133
  59.4 4.3 %collective-permute-start.16 = (f32[64,256]{1,0:T(8,128)S(1)}, f32[64,256]{1,0:T(8,128)S(1)}, u32[]{:S(2)}, u32[]{:S(2)}) collective-permute-start(f32[64,256]{1,0:T(8,128)S(1)} %tail_product.1.refs_4_), channel_id=1, source_target_pairs={{0,3},{1,0},{2,1},{3,2},{8,11},{9,8},{10,9},{11,10},{16,19},{17,16... | collective-permute-start | bytes 196616 | tf_op jit(solution)/shard_map/ppermute | solution.py:243
  63.7 2.4 %collective-permute-start.15 = (f32[64,256]{1,0:T(8,128)S(1)}, f32[64,256]{1,0:T(8,128)S(1)}, u32[]{:S(2)}, u32[]{:S(2)}) collective-permute-start(f32[64,256]{1,0:T(8,128)S(1)} %tail_product.1.refs_4_), channel_id=1, source_target_pairs={{0,2},{1,3},{2,0},{3,1},{8,10},{9,11},{10,8},{11,9},{16,18},{17,19... | collective-permute-start | bytes 196616 | tf_op jit(solution)/shard_map/ppermute | solution.py:243
  66.1 2.0 %collective-permute-start.14 = (f32[64,256]{1,0:T(8,128)S(1)}, f32[64,256]{1,0:T(8,128)S(1)}, u32[]{:S(2)}, u32[]{:S(2)}) collective-permute-start(f32[64,256]{1,0:T(8,128)S(1)} %tail_product.1.refs_4_), channel_id=1, source_target_pairs={{0,1},{1,2},{2,3},{3,0},{8,9},{9,10},{10,11},{11,8},{16,17},{17,18... | collective-permute-start | bytes 196616 | tf_op jit(solution)/shard_map/ppermute | solution.py:243
  68.1 3.0 %collective-permute-start.10 = (f32[64,256]{1,0:T(8,128)S(1)}, f32[64,256]{1,0:T(8,128)S(1)}, u32[]{:S(2)}, u32[]{:S(2)}) collective-permute-start(f32[64,256]{1,0:T(8,128)S(1)} %get-tuple-element.39), channel_id=1, source_target_pairs={{0,1},{1,2},{2,3},{3,0},{4,5},{5,6},{6,7},{7,4},{8,9},{9,10},{10,1... | collective-permute-start | bytes 196616 | tf_op jit(solution)/shard_map/ppermute | solution.py:222
  71.1 1.4 %collective-permute-start.11 = (f32[64,256]{1,0:T(8,128)S(1)}, f32[64,256]{1,0:T(8,128)S(1)}, u32[]{:S(2)}, u32[]{:S(2)}) collective-permute-start(f32[64,256]{1,0:T(8,128)S(1)} %get-tuple-element.40), channel_id=1, source_target_pairs={{0,2},{1,3},{2,0},{3,1},{4,6},{5,7},{6,4},{7,5},{8,10},{9,11},{10,... | collective-permute-start | bytes 196616 | tf_op jit(solution)/shard_map/ppermute | solution.py:222
  74.7 1.8 %collective-permute-done.11.refs_2_ = f32[64,256]{1,0:T(8,128)S(1)} collective-permute-done((f32[64,256]{1,0:T(8,128)S(1)}, f32[64,256]{1,0:T(8,128)S(1)}, u32[]{:S(2)}, u32[]{:S(2)}) %collective-permute-start.11) | collective-permute-done | bytes 65568 | tf_op jit(solution)/shard_map/ppermute | solution.py:222
  77.8 1.9 %final.1 = f32[3,64,256]{2,1,0:T(8,128)} custom-call(f32[3,64,256]{2,1,0:T(8,128)} %get-tuple-element.35.base_ref, f32[1,256]{1,0:T(1,128)} %get-tuple-element.36.inverse_ref, s32[1,64]{1,0:T(1,128)} %constant_dynamic-slice_fusion.order_ref, f32[64,256]{1,0:T(8,128)} %copy-done.8, f32[64,256]{1,0:T(8,128)} %copy-done.18, ...), custom_call_target="tpu_custom_call", output_to_operand_aliasing={{}: (0, {})} | custom-call | tf_op jit(solution)/shard_map/final/pallas_call | solution.py:189
  (63 shorter events, 14.4 us)
Async XLA Ops:
  0.0 24.7 %collective-permute-start.4 = (bf16[256,4096]{1,0:T(8,128)(2,1)}, bf16[256,4096]{1,0:T(8,128)(2,1)}, u32[]{:S(2)}, u32[]{:S(2)}) collective-permute-start(bf16[256,4096]{1,0:T(8,128)(2,1)} %bitcast.12), channel_id=1, source_target_pairs={{4,12},{12,4},{5,13},{13,5},{6,14},{14,6},{7,15},{15,7},{20,28},{2... | collective-permute-start | bytes 6291464 | tf_op jit(solution)/shard_map/ppermute | solution.py:225
  2.0 29.9 %collective-permute-start.3 = (bf16[256,4096]{1,0:T(8,128)(2,1)}, bf16[256,4096]{1,0:T(8,128)(2,1)}, u32[]{:S(2)}, u32[]{:S(2)}) collective-permute-start(bf16[256,4096]{1,0:T(8,128)(2,1)} %bitcast.13), channel_id=1, source_target_pairs={{0,4},{8,12},{1,5},{9,13},{2,6},{10,14},{3,7},{11,15},{16,20},{24,... | collective-permute-start | bytes 6291464 | tf_op jit(solution)/shard_map/ppermute | solution.py:226
  16.0 6.9 %copy-start.6 = (f32[72,256]{1,0:T(8,128)}, f32[72,256]{1,0:T(8,128)S(1)}, u32[]{:S(2)}) copy-start(f32[72,256]{1,0:T(8,128)S(1)} %get-tuple-element.24.refs_0_) | copy-start | bytes 221188
  16.1 6.9 %collective-permute-start = (f32[72,256]{1,0:T(8,128)S(1)}, f32[72,256]{1,0:T(8,128)S(1)}, u32[]{:S(2)}, u32[]{:S(2)}) collective-permute-start(f32[72,256]{1,0:T(8,128)S(1)} %get-tuple-element.25), channel_id=1, source_target_pairs={{0,1},{1,2},{2,3},{3,0},{4,5},{5,6},{6,7},{7,4},{8,9},{9,10},{10,1... | collective-permute-start | bytes 221192 | tf_op jit(solution)/shard_map/ppermute | solution.py:222
  17.7 6.6 %collective-permute-start.1 = (f32[72,256]{1,0:T(8,128)S(1)}, f32[72,256]{1,0:T(8,128)S(1)}, u32[]{:S(2)}, u32[]{:S(2)}) collective-permute-start(f32[72,256]{1,0:T(8,128)S(1)} %get-tuple-element.26), channel_id=1, source_target_pairs={{0,2},{1,3},{2,0},{3,1},{4,6},{5,7},{6,4},{7,5},{8,10},{9,11},{10,... | collective-permute-start | bytes 221192 | tf_op jit(solution)/shard_map/ppermute | solution.py:222
  20.3 13.0 %copy-start.1 = (bf16[256,1,4096]{2,0,1:T(8,128)(2,1)S(1)}, bf16[256,1,4096]{2,0,1:T(8,128)(2,1)}, u32[]{:S(2)}) copy-start(bf16[256,1,4096]{2,0,1:T(8,128)(2,1)} %param.4) | copy-start | bytes 6291460
  20.3 13.0 %copy-start.4 = (f32[1,4096]{1,0:T(1,128)S(1)}, f32[1,4096]{1,0:T(1,128)}, u32[]{:S(2)}) copy-start(f32[1,4096]{1,0:T(1,128)} %eig_ref.1) | copy-start | bytes 49156
  20.3 4.5 %collective-permute-start.2 = (f32[72,256]{1,0:T(8,128)S(1)}, f32[72,256]{1,0:T(8,128)S(1)}, u32[]{:S(2)}, u32[]{:S(2)}) collective-permute-start(f32[72,256]{1,0:T(8,128)S(1)} %get-tuple-element.27), channel_id=1, source_target_pairs={{0,3},{1,0},{2,1},{3,2},{4,7},{5,4},{6,5},{7,6},{8,11},{9,8},{10,9... | collective-permute-start | bytes 221192 | tf_op jit(solution)/shard_map/ppermute | solution.py:222
  23.0 14.9 %copy-start.9 = (f32[72,256]{1,0:T(8,128)}, f32[72,256]{1,0:T(8,128)S(1)}, u32[]{:S(2)}) copy-start(f32[72,256]{1,0:T(8,128)S(1)} %collective-permute-done.refs_1_) | copy-start | bytes 221188
  24.3 13.7 %copy-start.10 = (f32[72,256]{1,0:T(8,128)}, f32[72,256]{1,0:T(8,128)S(1)}, u32[]{:S(2)}) copy-start(f32[72,256]{1,0:T(8,128)S(1)} %collective-permute-done.1.refs_2_) | copy-start | bytes 221188
  24.7 13.2 %copy-start.11 = (f32[72,256]{1,0:T(8,128)}, f32[72,256]{1,0:T(8,128)S(1)}, u32[]{:S(2)}) copy-start(f32[72,256]{1,0:T(8,128)S(1)} %collective-permute-done.2.refs_3_) | copy-start | bytes 221188
  24.7 8.5 %collective-permute-start.5 = (bf16[256,4096]{1,0:T(8,128)(2,1)}, bf16[256,4096]{1,0:T(8,128)(2,1)S(1)}, u32[]{:S(2)}, u32[]{:S(2)}) collective-permute-start(bf16[256,4096]{1,0:T(8,128)(2,1)} %collective-permute-done.4.refs_1_), channel_id=1, source_target_pairs={{4,0},{12,8},{5,1},{13,9},{6,2},{14,10},{7,3},{15,11},{20,16},{28,... | collective-permute-start | bytes 6291464 | tf_op jit(solution)/shard_map/ppermute | solution.py:229
  26.0 25.1 %collective-permute-start.9 = (bf16[192,4096]{1,0:T(8,128)(2,1)}, bf16[192,4096]{1,0:T(8,128)(2,1)}, u32[]{:S(2)}, u32[]{:S(2)}) collective-permute-start(bf16[192,4096]{1,0:T(8,128)(2,1)} %slice_bitcast_fusion), channel_id=1, source_target_pairs={{0,8},{8,0},{1,9},{9,1},{2,10},{10,2},{3,11},{11,3},{16,24},{24,16... | collective-permute-start | bytes 4718600 | tf_op jit(solution)/shard_map/ppermute | solution.py:230
  28.5 29.0 %collective-permute-start.13 = (bf16[64,4096]{1,0:T(8,128)(2,1)S(1)}, bf16[64,4096]{1,0:T(8,128)(2,1)S(1)}, u32[]{:S(2)}, u32[]{:S(2)}) collective-permute-start(bf16[64,4096]{1,0:T(8,128)(2,1)S(1)} %slice_bitcast_fusion.1), channel_id=1, source_target_pairs={{0,8},{8,0},{1,9},{9,1},{2,10},{10,2},{3,11},{11,3},{16,24},{24,16... | collective-permute-start | bytes 1572872 | tf_op jit(solution)/shard_map/ppermute | solution.py:231
  38.6 6.1 %collective-permute-start.6 = (f32[64,256]{1,0:T(8,128)S(1)}, f32[64,256]{1,0:T(8,128)S(1)}, u32[]{:S(2)}, u32[]{:S(2)}) collective-permute-start(f32[64,256]{1,0:T(8,128)S(1)} %get-tuple-element.32), channel_id=1, source_target_pairs={{0,1},{1,2},{2,3},{3,0},{4,5},{5,6},{6,7},{7,4},{8,9},{9,10},{10,1... | collective-permute-start | bytes 196616 | tf_op jit(solution)/shard_map/ppermute | solution.py:222
  40.4 7.8 %collective-permute-start.7 = (f32[64,256]{1,0:T(8,128)S(1)}, f32[64,256]{1,0:T(8,128)S(1)}, u32[]{:S(2)}, u32[]{:S(2)}) collective-permute-start(f32[64,256]{1,0:T(8,128)S(1)} %get-tuple-element.33), channel_id=1, source_target_pairs={{0,2},{1,3},{2,0},{3,1},{4,6},{5,7},{6,4},{7,5},{8,10},{9,11},{10,... | collective-permute-start | bytes 196616 | tf_op jit(solution)/shard_map/ppermute | solution.py:222
  43.0 5.7 %collective-permute-start.8 = (f32[64,256]{1,0:T(8,128)S(1)}, f32[64,256]{1,0:T(8,128)S(1)}, u32[]{:S(2)}, u32[]{:S(2)}) collective-permute-start(f32[64,256]{1,0:T(8,128)S(1)} %get-tuple-element.34), channel_id=1, source_target_pairs={{0,3},{1,0},{2,1},{3,2},{4,7},{5,4},{6,5},{7,6},{8,11},{9,8},{10,9... | collective-permute-start | bytes 196616 | tf_op jit(solution)/shard_map/ppermute | solution.py:222
  59.4 17.7 %copy-start.5 = (f32[64,256]{1,0:T(8,128)}, f32[64,256]{1,0:T(8,128)S(1)}, u32[]{:S(2)}) copy-start(f32[64,256]{1,0:T(8,128)S(1)} %tail_product.1.refs_4_) | copy-start | bytes 196612
  59.4 13.0 %collective-permute-start.16 = (f32[64,256]{1,0:T(8,128)S(1)}, f32[64,256]{1,0:T(8,128)S(1)}, u32[]{:S(2)}, u32[]{:S(2)}) collective-permute-start(f32[64,256]{1,0:T(8,128)S(1)} %tail_product.1.refs_4_), channel_id=1, source_target_pairs={{0,3},{1,0},{2,1},{3,2},{8,11},{9,8},{10,9},{11,10},{16,19},{17,16... | collective-permute-start | bytes 196616 | tf_op jit(solution)/shard_map/ppermute | solution.py:243
  63.7 10.4 %collective-permute-start.15 = (f32[64,256]{1,0:T(8,128)S(1)}, f32[64,256]{1,0:T(8,128)S(1)}, u32[]{:S(2)}, u32[]{:S(2)}) collective-permute-start(f32[64,256]{1,0:T(8,128)S(1)} %tail_product.1.refs_4_), channel_id=1, source_target_pairs={{0,2},{1,3},{2,0},{3,1},{8,10},{9,11},{10,8},{11,9},{16,18},{17,19... | collective-permute-start | bytes 196616 | tf_op jit(solution)/shard_map/ppermute | solution.py:243
  66.1 8.1 %collective-permute-start.14 = (f32[64,256]{1,0:T(8,128)S(1)}, f32[64,256]{1,0:T(8,128)S(1)}, u32[]{:S(2)}, u32[]{:S(2)}) collective-permute-start(f32[64,256]{1,0:T(8,128)S(1)} %tail_product.1.refs_4_), channel_id=1, source_target_pairs={{0,1},{1,2},{2,3},{3,0},{8,9},{9,10},{10,11},{11,8},{16,17},{17,18... | collective-permute-start | bytes 196616 | tf_op jit(solution)/shard_map/ppermute | solution.py:243
  68.1 6.6 %collective-permute-start.10 = (f32[64,256]{1,0:T(8,128)S(1)}, f32[64,256]{1,0:T(8,128)S(1)}, u32[]{:S(2)}, u32[]{:S(2)}) collective-permute-start(f32[64,256]{1,0:T(8,128)S(1)} %get-tuple-element.39), channel_id=1, source_target_pairs={{0,1},{1,2},{2,3},{3,0},{4,5},{5,6},{6,7},{7,4},{8,9},{9,10},{10,1... | collective-permute-start | bytes 196616 | tf_op jit(solution)/shard_map/ppermute | solution.py:222
  71.1 5.4 %collective-permute-start.11 = (f32[64,256]{1,0:T(8,128)S(1)}, f32[64,256]{1,0:T(8,128)S(1)}, u32[]{:S(2)}, u32[]{:S(2)}) collective-permute-start(f32[64,256]{1,0:T(8,128)S(1)} %get-tuple-element.40), channel_id=1, source_target_pairs={{0,2},{1,3},{2,0},{3,1},{4,6},{5,7},{6,4},{7,5},{8,10},{9,11},{10,... | collective-permute-start | bytes 196616 | tf_op jit(solution)/shard_map/ppermute | solution.py:222
  72.4 4.7 %collective-permute-start.12 = (f32[64,256]{1,0:T(8,128)S(1)}, f32[64,256]{1,0:T(8,128)S(1)}, u32[]{:S(2)}, u32[]{:S(2)}) collective-permute-start(f32[64,256]{1,0:T(8,128)S(1)} %get-tuple-element.41), channel_id=1, source_target_pairs={{0,3},{1,0},{2,1},{3,2},{4,7},{5,4},{6,5},{7,6},{8,11},{9,8},{10,9... | collective-permute-start | bytes 196616 | tf_op jit(solution)/shard_map/ppermute | solution.py:222
  (14 other events, 26.4 us)

commit v2 on v0

v2 whole, which is shorter than its diff:
```python
import functools

import jax
import jax.numpy as jnp
from jax import lax
from jax.experimental import pallas as pl
from jax.experimental.pallas import tpu as pltpu
from jax.sharding import PartitionSpec as P

STEPS = 3
PART = 1024
EXTRA = 8
F32, BF16 = jnp.float32, jnp.bfloat16
VMEM = pl.BlockSpec(memory_space=pltpu.VMEM)
SMEM = pl.BlockSpec(memory_space=pltpu.SMEM)


def after(x, *earlier):
    return lax.optimization_barrier((x,) + earlier)[0]


def dot(x, y, contract):
    return lax.dot_general(x, y, (contract, ((), ())), preferred_element_type=F32)


def added(refs):
    total = refs[0][...].astype(F32)
    for ref in refs[1:]:
        total = total + ref[...].astype(F32)
    return total


def choose(column, p):
    shape = (column.shape[0], p.shape[0])
    hot = (lax.broadcasted_iota(jnp.int32, shape, 1) == column).astype(F32).astype(BF16)
    total = None
    for _ in range(3):
        term = p.astype(BF16)
        p = p - term.astype(F32)
        part = dot(hot, term, ((1,), (0,)))
        total = part if total is None else total + part
    return total


def scores_kernel(step, first, layers, me_ref, x_ref, t_ref, eig_ref, order_ref, *refs):
    outs, acc = refs[:layers], refs[layers]
    p, squares = None, None
    for c in range(0, t_ref.shape[1], PART):
        columns = slice(c, c + PART)
        weights = 1.0 / (eig_ref[:, columns] + 0.05)
        t = t_ref[:, columns]
        x = (x_ref[:, columns].astype(F32) * weights).astype(BF16)
        part = dot(x, t, ((1,), (1,)))
        p = part if p is None else p + part
        if first:
            tf = t.astype(F32)
            square = tf * tf * weights
            for k in range(0, PART, 128):
                part = square[:, k : k + 128]
                squares = part if squares is None else squares + part
    acc[...] = choose(order_ref[:, step : step + 1], p)
    own = p.shape[0] // layers
    if first:
        extra = jnp.broadcast_to(jnp.sum(squares.T, axis=0, keepdims=True), (EXTRA, p.shape[1]))
    for by in range(layers):
        start = pl.multiple_of(lax.rem(me_ref[0] + by, layers) * own, own)
        outs[by][:own] = acc[pl.ds(start, own)].astype(outs[by].dtype)
        if first:
            outs[by][own:] = extra


def scores_call(step, first, layers, me, x, t, eig, order, sent):
    rows, depth = t.shape
    queries = x.shape[0]
    own = queries // layers + (EXTRA if first else 0)
    return pl.pallas_call(
        functools.partial(scores_kernel, step, first, layers),
        in_specs=[SMEM] + [VMEM] * 4,
        out_specs=[VMEM] * layers,
        scratch_shapes=[pltpu.VMEM((queries, rows), F32)],
        out_shape=[jax.ShapeDtypeStruct((own, rows), F32 if by == 0 else sent) for by in range(layers)],
        compiler_params=pltpu.CompilerParams(vmem_limit_bytes=24 << 20),
        cost_estimate=pl.CostEstimate(
            flops=2 * queries * rows * depth, bytes_accessed=4 * queries * depth, transcendentals=0
        ),
        name="scores_step_" + str(step),
    )(me, x, t, eig, order)


def base_kernel(layers, *refs):
    ins, (out_ref, inverse_ref) = refs[:-2], refs[-2:]
    own = out_ref.shape[1]
    first, second = added(ins[:layers]), added(ins[layers:])
    inverse = 1.0 / jnp.sqrt(first[own : own + 1])
    inverse_ref[...] = inverse
    out_ref[0] = first[:own] * inverse
    out_ref[1] = second * inverse
    out_ref[2] = jnp.zeros_like(second)


def base_call(layers, sums0, sums1):
    own, rows = sums1[0].shape
    return pl.pallas_call(
        functools.partial(base_kernel, layers),
        out_shape=[jax.ShapeDtypeStruct((STEPS, own, rows), F32), jax.ShapeDtypeStruct((1, rows), F32)],
        name="base",
    )(*sums0, *sums1)


def final_kernel(base_ref, inverse_ref, *refs):
    refs[-1][0] = added(refs[:-1]) * inverse_ref[...]


def final_call(base, inverse, sums):
    _, own, rows = base.shape
    whole = lambda i: (0, 0)
    return pl.pallas_call(
        final_kernel,
        grid=(1,),
        in_specs=[pl.BlockSpec(memory_space=pl.ANY)] + [pl.BlockSpec(x.shape, whole) for x in (inverse, *sums)],
        out_specs=pl.BlockSpec((1, own, rows), lambda i: (STEPS - 1, 0, 0)),
        out_shape=jax.ShapeDtypeStruct(base.shape, F32),
        input_output_aliases={0: 0},
        name="final",
    )(base, inverse, *sums)


def per_device(train_grads, query_grads, eigenvalues, order):
    rows, queries = train_grads.shape[0], query_grads.shape[0]
    layers = lax.axis_size("layer")
    me = lax.axis_index("layer").astype(jnp.int32).reshape(1)
    t = train_grads.reshape(rows, -1)
    q = query_grads.reshape(queries, -1)
    columns = order.T

    def shifted(x, axis, by):
        length = lax.axis_size(axis)
        return lax.ppermute(x, axis, [(i, (i + by) % length) for i in range(length)])

    def exchange(pieces):
        return [pieces[0]] + [shifted(pieces[by], "layer", by) for by in range(1, layers)]

    one_back = shifted(q, "blk", 1)
    sums0 = exchange(scores_call(0, True, layers, me, q, t, eigenvalues, columns, F32))
    one_back = after(one_back, *sums0)
    two_back = shifted(one_back, "blk", 1)
    sums1 = exchange(scores_call(1, False, layers, me, one_back, t, eigenvalues, columns, F32))
    base, inverse = base_call(layers, sums0, sums1)
    t2 = after(t, inverse)
    sums2 = exchange(scores_call(2, False, layers, me, two_back, t2, eigenvalues, columns, BF16))
    return final_call(base, inverse, sums2)


def solution(mesh):
    return jax.shard_map(
        per_device,
        mesh=mesh,
        in_specs=(
            P(("groups", "blk"), "layer", None),
            P(("groups", "blk"), "layer", None),
            P("layer", None),
            P("groups", None),
        ),
        out_specs=P(None, "layer", ("groups", "blk")),
        check_vma=False,
    )
```

time: 110 us -> 67 us (0.61)
  waiting for transfers between devices: 64 us -> 28.7 us
  starting transfers between devices: 0.54 us -> 19.6 us
  between operations: 13.2 us -> 0.11 us
  blocking collectives: 12.8 us -> 0 us
  Pallas kernels: 0 us -> 10.4 us
  other arithmetic: 9.51 us -> 0 us
  matrix products: 6.99 us -> 0 us
  local copies, waits for them, and re-layouts: 2.93 us -> 7.8 us
    reduce_scatter x3 -> x0, waiting for transfers between devices: 20.7 us -> none  [per_device(): lax.psum_scatter(partial_value, 'layer', scatter_dimension=0, tiled=True)]
    ppermute x2 -> x11, starting transfers between devices: 0.46 us -> 19.6 us  [shifted(): lax.ppermute(x, axis, [(i, (i + by) % length) for i in range(length)])]
    ppermute x2 -> x11, waiting for transfers between devices: 43.2 us -> 28.7 us  [shifted(): lax.ppermute(x, axis, [(i, (i + by) % length) for i in range(length)])]
    psum x1 -> x0, blocking collectives: 12.8 us -> none  [per_device(): selfinf = lax.psum(local_self, 'layer')]
    pallas_call x0 -> x5, Pallas kernels: none -> 10.4 us  [the longest x3 7.15 us: scores_call(): pl.pallas_call(functools.partial(scores_kernel, step, first, layers), in_...]
    unnamed x4 -> x35, local copies, waits for them, and re-layouts: 0.01 us -> 7.8 us
    dot_general x3 -> x0, matrix products: 6.99 us -> none  [per_device(): lax.dot_general(block_flat, train_flat, (((1,), (1,)), ((), ())), preferr...]
    reduce_sum x1 -> x0, other arithmetic: 4.7 us -> none  [per_device(): local_self = jnp.sum(tf * tf * weights[None, :, :], axis=(1, 2))]
  transfers between devices with their start and end apart: 5 -> 11, of which waited for: 4 -> 11; matrix products, arithmetic and copies ran while one was open for 11% -> 1% of each run, Pallas kernels for 0% -> 9%
where the time goes in v2:
time: 67 us; the launch traced here: 66.6 us
  waiting for transfers between devices  28.7 us (43%)
  starting transfers between devices  19.6 us (29%)
  Pallas kernels  10.4 us (16%)
  local copies, waits for them, and re-layouts  7.8 us (12%)
    ppermute x11, waiting for transfers between devices, shifted(): lax.ppermute(x, axis, [(i, (i + by) % length) for i in range(length)])  28.7 us
    ppermute x11, starting transfers between devices, shifted(): lax.ppermute(x, axis, [(i, (i + by) % length) for i in range(length)])  19.6 us
    unnamed x35, local copies, waits for them, and re-layouts  7.8 us
    pallas_call x3, Pallas kernels, scores_call(): pl.pallas_call(functools.partial(scores_kernel, step, first, layers), in_...  7.15 us
    pallas_call x1, Pallas kernels, base_call(): pl.pallas_call(functools.partial(base_kernel, layers), out_shape=[jax.Sha...  1.79 us
    pallas_call x1, Pallas kernels, final_call(): pl.pallas_call(final_kernel, grid=(1,), in_specs=[pl.BlockSpec(memory_spa...  1.49 us
  transfers between devices with their start and end apart: 11, of which 11 were waited for; matrix products, arithmetic and copies ran while one was open for 1% of the time, Pallas kernels for 9%

profile of v2, /device:TPU:0, one launch (start us, length us, event | category | flops | bytes accessed | tf_op | source)
XLA Modules:
  0.0 66.6 jit_solution(2943416679719360284)
XLA Ops:
  0.5 0.8 %copy.6 = s32[3,256]{0,1:T(8,128)S(1)} copy(s32[3,256]{1,0:T(4,128)} %param.7) | data formatting | bytes 6144 | tf_op args[3]
  1.3 1.6 %copy-done = bf16[256,1,4096]{2,0,1:T(8,128)(2,1)S(1)} copy-done((bf16[256,1,4096]{2,0,1:T(8,128)(2,1)S(1)}, bf16[256,1,4096]{2,0,1:T(8,128)(2,1)}, u32[]{:S(2)}) %copy-start) | copy-done | bytes 2097176
  2.9 1.6 %copy-done.2 = bf16[256,1,4096]{2,0,1:T(8,128)(2,1)S(1)} copy-done((bf16[256,1,4096]{2,0,1:T(8,128)(2,1)S(1)}, bf16[256,1,4096]{2,0,1:T(8,128)(2,1)}, u32[]{:S(2)}) %copy-start.2) | copy-done | bytes 2097176
  4.5 0.7 %copy-done.3 = f32[1,4096]{1,0:T(1,128)S(1)} copy-done((f32[1,4096]{1,0:T(1,128)S(1)}, f32[1,4096]{1,0:T(1,128)}, u32[]{:S(2)}) %copy-start.3) | copy-done | bytes 16408
  5.2 1.5 %scores_step_0.1 = (f32[72,256]{1,0:T(8,128)S(1)}, f32[72,256]{1,0:T(8,128)S(1)}, f32[72,256]{1,0:T(8,128)S(1)}, f32[72,256]{1,0:T(8,128)S(1)}) custom-call(s32[1]{0:T(128)} %bitcast.me_ref, bf16[256,4096]{1,0:T(8,128)(2,1)S(1)} %bitcast.11, bf16[256,4096]{1,0:T(8,128)(2,1)S(1)} %bitcast.4, f32[1,4096]{1,0:T(1,128)S(1)} %copy-done.3, s32[256,3]{1,0:T(8,128)S(1)} %bitcast.7), custom_call_target="tpu_custom_call" | custom-call | flops 536870912 | bytes 4194304 | tf_op jit(solution)/shard_map/scores_step_0/pallas_call | solution.py:76
  6.7 0.6 copy-done.5
  7.4 2.6 %collective-permute-start = (f32[72,256]{1,0:T(8,128)S(1)}, f32[72,256]{1,0:T(8,128)S(1)}, u32[]{:S(2)}, u32[]{:S(2)}) collective-permute-start(f32[72,256]{1,0:T(8,128)S(1)} %get-tuple-element.22), channel_id=1, source_target_pairs={{0,1},{1,2},{2,3},{3,0},{4,5},{5,6},{6,7},{7,4},{8,9},{9,10},{10,1... | collective-permute-start | bytes 221192 | tf_op jit(solution)/shard_map/ppermute | solution.py:138
  9.9 2.6 %collective-permute-start.1 = (f32[72,256]{1,0:T(8,128)S(1)}, f32[72,256]{1,0:T(8,128)S(1)}, u32[]{:S(2)}, u32[]{:S(2)}) collective-permute-start(f32[72,256]{1,0:T(8,128)S(1)} %get-tuple-element.23), channel_id=1, source_target_pairs={{0,2},{1,3},{2,0},{3,1},{4,6},{5,7},{6,4},{7,5},{8,10},{9,11},{10,... | collective-permute-start | bytes 221192 | tf_op jit(solution)/shard_map/ppermute | solution.py:138
  12.5 1.3 %collective-permute-start.2 = (f32[72,256]{1,0:T(8,128)S(1)}, f32[72,256]{1,0:T(8,128)S(1)}, u32[]{:S(2)}, u32[]{:S(2)}) collective-permute-start(f32[72,256]{1,0:T(8,128)S(1)} %get-tuple-element.24), channel_id=1, source_target_pairs={{0,3},{1,0},{2,1},{3,2},{4,7},{5,4},{6,5},{7,6},{8,11},{9,8},{10,9... | collective-permute-start | bytes 221192 | tf_op jit(solution)/shard_map/ppermute | solution.py:138
  14.3 4.0 %collective-permute-done.1.refs_2_ = f32[72,256]{1,0:T(8,128)S(1)} collective-permute-done((f32[72,256]{1,0:T(8,128)S(1)}, f32[72,256]{1,0:T(8,128)S(1)}, u32[]{:S(2)}, u32[]{:S(2)}) %collective-permute-start.1) | collective-permute-done | bytes 73760 | tf_op jit(solution)/shard_map/ppermute | solution.py:138
  18.9 7.5 %collective-permute-done.3.x_ref = bf16[256,4096]{1,0:T(8,128)(2,1)} collective-permute-done((bf16[256,4096]{1,0:T(8,128)(2,1)}, bf16[256,4096]{1,0:T(8,128)(2,1)}, u32[]{:S(2)}, u32[]{:S(2)}) %collective-permute-start.3) | collective-permute-done | bytes 2097184 | tf_op jit(solution)/shard_map/ppermute | solution.py:138
  26.4 2.8 %scores_step_1.1 = (f32[64,256]{1,0:T(8,128)S(1)}, f32[64,256]{1,0:T(8,128)S(1)}, f32[64,256]{1,0:T(8,128)S(1)}, f32[64,256]{1,0:T(8,128)S(1)}) custom-call(s32[1]{0:T(128)} %bitcast.me_ref, bf16[256,4096]{1,0:T(8,128)(2,1)} %collective-permute-done.3.x_ref, bf16[256,4096]{1,0:T(8,128)(2,1)S(1)} %bitcast.5, f32[1,4096]{1,0:T(1,128)S(1)} %copy-done.4, ...), custom_call_target="tpu_custom_call" | custom-call | flops 536870912 | bytes 4194304 | tf_op jit(solution)/shard_map/scores_step_1/pallas_call | solution.py:76
  29.9 2.4 %collective-permute-start.4 = (f32[64,256]{1,0:T(8,128)S(1)}, f32[64,256]{1,0:T(8,128)S(1)}, u32[]{:S(2)}, u32[]{:S(2)}) collective-permute-start(f32[64,256]{1,0:T(8,128)S(1)} %get-tuple-element.27), channel_id=1, source_target_pairs={{0,1},{1,2},{2,3},{3,0},{4,5},{5,6},{6,7},{7,4},{8,9},{9,10},{10,1... | collective-permute-start | bytes 196616 | tf_op jit(solution)/shard_map/ppermute | solution.py:138
  32.3 2.6 %collective-permute-start.5 = (f32[64,256]{1,0:T(8,128)S(1)}, f32[64,256]{1,0:T(8,128)S(1)}, u32[]{:S(2)}, u32[]{:S(2)}) collective-permute-start(f32[64,256]{1,0:T(8,128)S(1)} %get-tuple-element.28), channel_id=1, source_target_pairs={{0,2},{1,3},{2,0},{3,1},{4,6},{5,7},{6,4},{7,5},{8,10},{9,11},{10,... | collective-permute-start | bytes 196616 | tf_op jit(solution)/shard_map/ppermute | solution.py:138
  34.9 1.3 %collective-permute-start.6 = (f32[64,256]{1,0:T(8,128)S(1)}, f32[64,256]{1,0:T(8,128)S(1)}, u32[]{:S(2)}, u32[]{:S(2)}) collective-permute-start(f32[64,256]{1,0:T(8,128)S(1)} %get-tuple-element.29), channel_id=1, source_target_pairs={{0,3},{1,0},{2,1},{3,2},{4,7},{5,4},{6,5},{7,6},{8,11},{9,8},{10,9... | collective-permute-start | bytes 196616 | tf_op jit(solution)/shard_map/ppermute | solution.py:138
  36.5 3.7 %collective-permute-done.5.refs_6_ = f32[64,256]{1,0:T(8,128)S(1)} collective-permute-done((f32[64,256]{1,0:T(8,128)S(1)}, f32[64,256]{1,0:T(8,128)S(1)}, u32[]{:S(2)}, u32[]{:S(2)}) %collective-permute-start.5) | collective-permute-done | bytes 65568 | tf_op jit(solution)/shard_map/ppermute | solution.py:138
  41.5 1.8 %base.1 = (f32[3,64,256]{2,1,0:T(8,128)}, f32[1,256]{1,0:T(1,128)}) custom-call(f32[72,256]{1,0:T(8,128)} %copy-done.5, f32[72,256]{1,0:T(8,128)} %copy-done.8, f32[72,256]{1,0:T(8,128)} %copy-done.9, f32[72,256]{1,0:T(8,128)} %copy-done.10, f32[64,256]{1,0:T(8,128)} %copy-done.6, f32[64,256]{1,0:T(8,128)} %copy-done.11, f32[64,256]{1,0:T(8,128)} %copy-done.12, ...), custom_call_target="tpu_custom_call" | custom-call | tf_op jit(solution)/shard_map/base/pallas_call | solution.py:103
  43.2 8.9 %collective-permute-done.7.x_ref = bf16[256,4096]{1,0:T(8,128)(2,1)} collective-permute-done((bf16[256,4096]{1,0:T(8,128)(2,1)}, bf16[256,4096]{1,0:T(8,128)(2,1)}, u32[]{:S(2)}, u32[]{:S(2)}) %collective-permute-start.7) | collective-permute-done | bytes 2097184 | tf_op jit(solution)/shard_map/ppermute | solution.py:138
  52.2 2.8 %scores_step_2.1 = (f32[64,256]{1,0:T(8,128)S(1)}, bf16[64,256]{1,0:T(8,128)(2,1)S(1)}, bf16[64,256]{1,0:T(8,128)(2,1)S(1)}, bf16[64,256]{1,0:T(8,128)(2,1)S(1)}) custom-call(s32[1]{0:T(128)} %bitcast.me_ref, bf16[256,4096]{1,0:T(8,128)(2,1)} %collective-permute-done.7.x_ref, bf16[256,4096]{1,0:T(8,128)(2,1)S(1)} %bitcast.6, f32[1,4096]{1,0:T(1,128)S(1)} %copy-done.4, ...), custom_call_target="tpu_custom_call" | custom-call | flops 536870912 | bytes 4194304 | tf_op jit(solution)/shard_map/scores_step_2/pallas_call | solution.py:76
  55.6 2.4 %collective-permute-start.8 = (bf16[64,256]{1,0:T(8,128)(2,1)S(1)}, bf16[64,256]{1,0:T(8,128)(2,1)S(1)}, u32[]{:S(2)}, u32[]{:S(2)}) collective-permute-start(bf16[64,256]{1,0:T(8,128)(2,1)S(1)} %get-tuple-element.34), channel_id=1, source_target_pairs={{0,1},{1,2},{2,3},{3,0},{4,5},{5,6},{6,7},{7,4},{8,9},{9,10},{10,1... | collective-permute-start | bytes 98312 | tf_op jit(solution)/shard_map/ppermute | solution.py:138
  58.0 2.6 %collective-permute-start.9 = (bf16[64,256]{1,0:T(8,128)(2,1)S(1)}, bf16[64,256]{1,0:T(8,128)(2,1)S(1)}, u32[]{:S(2)}, u32[]{:S(2)}) collective-permute-start(bf16[64,256]{1,0:T(8,128)(2,1)S(1)} %get-tuple-element.35), channel_id=1, source_target_pairs={{0,2},{1,3},{2,0},{3,1},{4,6},{5,7},{6,4},{7,5},{8,10},{9,11},{10,... | collective-permute-start | bytes 98312 | tf_op jit(solution)/shard_map/ppermute | solution.py:138
  60.6 1.3 %collective-permute-start.10 = (bf16[64,256]{1,0:T(8,128)(2,1)S(1)}, bf16[64,256]{1,0:T(8,128)(2,1)S(1)}, u32[]{:S(2)}, u32[]{:S(2)}) collective-permute-start(bf16[64,256]{1,0:T(8,128)(2,1)S(1)} %get-tuple-element.36), channel_id=1, source_target_pairs={{0,3},{1,0},{2,1},{3,2},{4,7},{5,4},{6,5},{7,6},{8,11},{9,8},{10,9... | collective-permute-start | bytes 98312 | tf_op jit(solution)/shard_map/ppermute | solution.py:138
  62.8 1.7 %collective-permute-done.10.refs_3_ = bf16[64,256]{1,0:T(8,128)(2,1)S(1)} collective-permute-done((bf16[64,256]{1,0:T(8,128)(2,1)S(1)}, bf16[64,256]{1,0:T(8,128)(2,1)S(1)}, u32[]{:S(2)}, u32[]{:S(2)}) %collective-permute-start.10) | collective-permute-done | bytes 32800 | tf_op jit(solution)/shard_map/ppermute | solution.py:138
  65.1 1.5 %final.1 = f32[3,64,256]{2,1,0:T(8,128)} custom-call(f32[3,64,256]{2,1,0:T(8,128)} %get-tuple-element.30.base_ref, f32[1,256]{1,0:T(1,128)} %get-tuple-element.31.inverse_ref, f32[64,256]{1,0:T(8,128)} %copy-done.7, bf16[64,256]{1,0:T(8,128)(2,1)} %copy-done.14, bf16[64,256]{1,0:T(8,128)(2,1)} %copy-done.15, ...), custom_call_target="tpu_custom_call", output_to_operand_aliasing={{}: (0, {})} | custom-call | tf_op jit(solution)/shard_map/final/pallas_call | solution.py:117
  (38 shorter events, 5.8 us)
Async XLA Ops:
  0.0 26.4 %collective-permute-start.3 = (bf16[256,4096]{1,0:T(8,128)(2,1)}, bf16[256,4096]{1,0:T(8,128)(2,1)}, u32[]{:S(2)}, u32[]{:S(2)}) collective-permute-start(bf16[256,4096]{1,0:T(8,128)(2,1)} %bitcast.10), channel_id=1, source_target_pairs={{0,4},{4,8},{8,12},{12,0},{1,5},{5,9},{9,13},{13,1},{2,6},{6,10},{... | collective-permute-start | bytes 6291464 | tf_op jit(solution)/shard_map/ppermute | solution.py:138
  1.3 1.6 %copy-start = (bf16[256,1,4096]{2,0,1:T(8,128)(2,1)S(1)}, bf16[256,1,4096]{2,0,1:T(8,128)(2,1)}, u32[]{:S(2)}) copy-start(bf16[256,1,4096]{2,0,1:T(8,128)(2,1)} %param.4) | copy-start | bytes 6291460
  2.9 1.6 %copy-start.2 = (bf16[256,1,4096]{2,0,1:T(8,128)(2,1)S(1)}, bf16[256,1,4096]{2,0,1:T(8,128)(2,1)}, u32[]{:S(2)}) copy-start(bf16[256,1,4096]{2,0,1:T(8,128)(2,1)} %param.5) | copy-start | bytes 6291460
  4.5 0.7 %copy-start.3 = (f32[1,4096]{1,0:T(1,128)S(1)}, f32[1,4096]{1,0:T(1,128)}, u32[]{:S(2)}) copy-start(f32[1,4096]{1,0:T(1,128)} %eig_ref.5) | copy-start | bytes 49156
  5.2 21.2 %copy-start.1 = (bf16[256,1,4096]{2,0,1:T(8,128)(2,1)S(1)}, bf16[256,1,4096]{2,0,1:T(8,128)(2,1)}, u32[]{:S(2)}) copy-start(bf16[256,1,4096]{2,0,1:T(8,128)(2,1)} %param.4) | copy-start | bytes 6291460
  5.2 21.2 %copy-start.4 = (f32[1,4096]{1,0:T(1,128)S(1)}, f32[1,4096]{1,0:T(1,128)}, u32[]{:S(2)}) copy-start(f32[1,4096]{1,0:T(1,128)} %eig_ref.5) | copy-start | bytes 49156
  6.7 0.6 copy-start.5
  7.4 6.9 %collective-permute-start = (f32[72,256]{1,0:T(8,128)S(1)}, f32[72,256]{1,0:T(8,128)S(1)}, u32[]{:S(2)}, u32[]{:S(2)}) collective-permute-start(f32[72,256]{1,0:T(8,128)S(1)} %get-tuple-element.22), channel_id=1, source_target_pairs={{0,1},{1,2},{2,3},{3,0},{4,5},{5,6},{6,7},{7,4},{8,9},{9,10},{10,1... | collective-permute-start | bytes 221192 | tf_op jit(solution)/shard_map/ppermute | solution.py:138
  9.9 8.4 %collective-permute-start.1 = (f32[72,256]{1,0:T(8,128)S(1)}, f32[72,256]{1,0:T(8,128)S(1)}, u32[]{:S(2)}, u32[]{:S(2)}) collective-permute-start(f32[72,256]{1,0:T(8,128)S(1)} %get-tuple-element.23), channel_id=1, source_target_pairs={{0,2},{1,3},{2,0},{3,1},{4,6},{5,7},{6,4},{7,5},{8,10},{9,11},{10,... | collective-permute-start | bytes 221192 | tf_op jit(solution)/shard_map/ppermute | solution.py:138
  12.5 6.4 %collective-permute-start.2 = (f32[72,256]{1,0:T(8,128)S(1)}, f32[72,256]{1,0:T(8,128)S(1)}, u32[]{:S(2)}, u32[]{:S(2)}) collective-permute-start(f32[72,256]{1,0:T(8,128)S(1)} %get-tuple-element.24), channel_id=1, source_target_pairs={{0,3},{1,0},{2,1},{3,2},{4,7},{5,4},{6,5},{7,6},{8,11},{9,8},{10,9... | collective-permute-start | bytes 221192 | tf_op jit(solution)/shard_map/ppermute | solution.py:138
  14.3 15.0 %copy-start.8 = (f32[72,256]{1,0:T(8,128)}, f32[72,256]{1,0:T(8,128)S(1)}, u32[]{:S(2)}) copy-start(f32[72,256]{1,0:T(8,128)S(1)} %collective-permute-done.refs_1_) | copy-start | bytes 221188
  18.3 10.9 %copy-start.9 = (f32[72,256]{1,0:T(8,128)}, f32[72,256]{1,0:T(8,128)S(1)}, u32[]{:S(2)}) copy-start(f32[72,256]{1,0:T(8,128)S(1)} %collective-permute-done.1.refs_2_) | copy-start | bytes 221188
  18.9 10.3 %copy-start.10 = (f32[72,256]{1,0:T(8,128)}, f32[72,256]{1,0:T(8,128)S(1)}, u32[]{:S(2)}) copy-start(f32[72,256]{1,0:T(8,128)S(1)} %collective-permute-done.2.refs_3_) | copy-start | bytes 221188
  26.4 25.8 %collective-permute-start.7 = (bf16[256,4096]{1,0:T(8,128)(2,1)}, bf16[256,4096]{1,0:T(8,128)(2,1)}, u32[]{:S(2)}, u32[]{:S(2)}) collective-permute-start(bf16[256,4096]{1,0:T(8,128)(2,1)} %collective-permute-done.3.x_ref), channel_id=1, source_target_pairs={{0,4},{4,8},{8,12},{12,0},{1,5},{5,9},{9,13},{13,1},{2,6},{6,10},{... | collective-permute-start | bytes 6291464 | tf_op jit(solution)/shard_map/ppermute | solution.py:138
  29.9 6.7 %collective-permute-start.4 = (f32[64,256]{1,0:T(8,128)S(1)}, f32[64,256]{1,0:T(8,128)S(1)}, u32[]{:S(2)}, u32[]{:S(2)}) collective-permute-start(f32[64,256]{1,0:T(8,128)S(1)} %get-tuple-element.27), channel_id=1, source_target_pairs={{0,1},{1,2},{2,3},{3,0},{4,5},{5,6},{6,7},{7,4},{8,9},{9,10},{10,1... | collective-permute-start | bytes 196616 | tf_op jit(solution)/shard_map/ppermute | solution.py:138
  32.3 7.9 %collective-permute-start.5 = (f32[64,256]{1,0:T(8,128)S(1)}, f32[64,256]{1,0:T(8,128)S(1)}, u32[]{:S(2)}, u32[]{:S(2)}) collective-permute-start(f32[64,256]{1,0:T(8,128)S(1)} %get-tuple-element.28), channel_id=1, source_target_pairs={{0,2},{1,3},{2,0},{3,1},{4,6},{5,7},{6,4},{7,5},{8,10},{9,11},{10,... | collective-permute-start | bytes 196616 | tf_op jit(solution)/shard_map/ppermute | solution.py:138
  34.9 6.0 %collective-permute-start.6 = (f32[64,256]{1,0:T(8,128)S(1)}, f32[64,256]{1,0:T(8,128)S(1)}, u32[]{:S(2)}, u32[]{:S(2)}) collective-permute-start(f32[64,256]{1,0:T(8,128)S(1)} %get-tuple-element.29), channel_id=1, source_target_pairs={{0,3},{1,0},{2,1},{3,2},{4,7},{5,4},{6,5},{7,6},{8,11},{9,8},{10,9... | collective-permute-start | bytes 196616 | tf_op jit(solution)/shard_map/ppermute | solution.py:138
  36.5 4.3 %copy-start.11 = (f32[64,256]{1,0:T(8,128)}, f32[64,256]{1,0:T(8,128)S(1)}, u32[]{:S(2)}) copy-start(f32[64,256]{1,0:T(8,128)S(1)} %collective-permute-done.4.refs_5_) | copy-start | bytes 196612
  40.2 0.6 copy-start.12
  55.6 6.7 %collective-permute-start.8 = (bf16[64,256]{1,0:T(8,128)(2,1)S(1)}, bf16[64,256]{1,0:T(8,128)(2,1)S(1)}, u32[]{:S(2)}, u32[]{:S(2)}) collective-permute-start(bf16[64,256]{1,0:T(8,128)(2,1)S(1)} %get-tuple-element.34), channel_id=1, source_target_pairs={{0,1},{1,2},{2,3},{3,0},{4,5},{5,6},{6,7},{7,4},{8,9},{9,10},{10,1... | collective-permute-start | bytes 98312 | tf_op jit(solution)/shard_map/ppermute | solution.py:138
  58.0 4.8 %collective-permute-start.9 = (bf16[64,256]{1,0:T(8,128)(2,1)S(1)}, bf16[64,256]{1,0:T(8,128)(2,1)S(1)}, u32[]{:S(2)}, u32[]{:S(2)}) collective-permute-start(bf16[64,256]{1,0:T(8,128)(2,1)S(1)} %get-tuple-element.35), channel_id=1, source_target_pairs={{0,2},{1,3},{2,0},{3,1},{4,6},{5,7},{6,4},{7,5},{8,10},{9,11},{10,... | collective-permute-start | bytes 98312 | tf_op jit(solution)/shard_map/ppermute | solution.py:138
  60.6 3.9 %collective-permute-start.10 = (bf16[64,256]{1,0:T(8,128)(2,1)S(1)}, bf16[64,256]{1,0:T(8,128)(2,1)S(1)}, u32[]{:S(2)}, u32[]{:S(2)}) collective-permute-start(bf16[64,256]{1,0:T(8,128)(2,1)S(1)} %get-tuple-element.36), channel_id=1, source_target_pairs={{0,3},{1,0},{2,1},{3,2},{4,7},{5,4},{6,5},{7,6},{8,11},{9,8},{10,9... | collective-permute-start | bytes 98312 | tf_op jit(solution)/shard_map/ppermute | solution.py:138
  62.3 2.2 %copy-start.14 = (bf16[64,256]{1,0:T(8,128)(2,1)}, bf16[64,256]{1,0:T(8,128)(2,1)S(1)}, u32[]{:S(2)}) copy-start(bf16[64,256]{1,0:T(8,128)(2,1)S(1)} %collective-permute-done.8.refs_1_) | copy-start | bytes 98308
  62.8 1.7 %copy-start.15 = (bf16[64,256]{1,0:T(8,128)(2,1)}, bf16[64,256]{1,0:T(8,128)(2,1)S(1)}, u32[]{:S(2)}) copy-start(bf16[64,256]{1,0:T(8,128)(2,1)S(1)} %collective-permute-done.9.refs_2_) | copy-start | bytes 98308
  (4 other events, 2.5 us)

commit v3 on v2

--- a/solution.py
+++ b/solution.py
@@ -79,7 +79,7 @@
         out_specs=[VMEM] * layers,
         scratch_shapes=[pltpu.VMEM((queries, rows), F32)],
         out_shape=[jax.ShapeDtypeStruct((own, rows), F32 if by == 0 else sent) for by in range(layers)],
-        compiler_params=pltpu.CompilerParams(vmem_limit_bytes=24 << 20),
+        compiler_params=pltpu.CompilerParams(vmem_limit_bytes=12 << 20),
         cost_estimate=pl.CostEstimate(
             flops=2 * queries * rows * depth, bytes_accessed=4 * queries * depth, transcendentals=0
         ),
@@ -103,26 +103,9 @@
     return pl.pallas_call(
         functools.partial(base_kernel, layers),
         out_shape=[jax.ShapeDtypeStruct((STEPS, own, rows), F32), jax.ShapeDtypeStruct((1, rows), F32)],
+        compiler_params=pltpu.CompilerParams(vmem_limit_bytes=4 << 20),
         name="base",
     )(*sums0, *sums1)
-
-
-def final_kernel(base_ref, inverse_ref, *refs):
-    refs[-1][0] = added(refs[:-1]) * inverse_ref[...]
-
-
-def final_call(base, inverse, sums):
-    _, own, rows = base.shape
-    whole = lambda i: (0, 0)
-    return pl.pallas_call(
-        final_kernel,
-        grid=(1,),
-        in_specs=[pl.BlockSpec(memory_space=pl.ANY)] + [pl.BlockSpec(x.shape, whole) for x in (inverse, *sums)],
-        out_specs=pl.BlockSpec((1, own, rows), lambda i: (STEPS - 1, 0, 0)),
-        out_shape=jax.ShapeDtypeStruct(base.shape, F32),
-        input_output_aliases={0: 0},
-        name="final",
-    )(base, inverse, *sums)
 
 
 def per_device(train_grads, query_grads, eigenvalues, order):
@@ -148,7 +131,10 @@
     base, inverse = base_call(layers, sums0, sums1)
     t2 = after(t, inverse)
     sums2 = exchange(scores_call(2, False, layers, me, two_back, t2, eigenvalues, columns, BF16))
-    return final_call(base, inverse, sums2)
+    total = sums2[0]
+    for piece in sums2[1:]:
+        total = total + piece.astype(F32)
+    return lax.dynamic_update_slice(base, (total * inverse)[None], (STEPS - 1, 0, 0))
 
 
 def solution(mesh):

time: 67 us -> 62.9 us (0.939)
  Pallas kernels: 10.4 us -> 4.71 us
  waiting for transfers between devices: 28.7 us -> 32.7 us
  local copies, waits for them, and re-layouts: 7.8 us -> 4.71 us
    ppermute x11, waiting for transfers between devices: 28.7 us -> 32.7 us  [shifted(): lax.ppermute(x, axis, [(i, (i + by) % length) for i in range(length)])]
    pallas_call x3, Pallas kernels: 7.15 us -> 3.99 us  [scores_call(): pl.pallas_call(functools.partial(scores_kernel, step, first, layers), in_...]
    unnamed x35 -> x9, local copies, waits for them, and re-layouts: 7.8 us -> 4.71 us
    pallas_call x1 -> x0, Pallas kernels: 1.49 us -> none  [final_call(): pl.pallas_call(final_kernel, grid=(1,), in_specs=[pl.BlockSpec(memory_spa...]
    pallas_call x1, Pallas kernels: 1.79 us -> 0.72 us  [base_call(): pl.pallas_call(functools.partial(base_kernel, layers), out_shape=[jax.Sha...]
  transfers between devices with their start and end apart: 11 -> 11, of which waited for: 11 -> 11; matrix products, arithmetic and copies ran while one was open for 1% -> 1% of each run, Pallas kernels for 9% -> 6%
where the time goes in v3:
time: 62.9 us; the launch traced here: 62.6 us
  waiting for transfers between devices  32.7 us (52%)
  starting transfers between devices  19.8 us (31%)
  local copies, waits for them, and re-layouts  4.71 us (7%)
  Pallas kernels  4.71 us (7%)
  other arithmetic  0.65 us (1%)
    ppermute x11, waiting for transfers between devices, shifted(): lax.ppermute(x, axis, [(i, (i + by) % length) for i in range(length)])  32.7 us
    ppermute x11, starting transfers between devices, shifted(): lax.ppermute(x, axis, [(i, (i + by) % length) for i in range(length)])  19.8 us
    unnamed x9, local copies, waits for them, and re-layouts  4.71 us
    pallas_call x3, Pallas kernels, scores_call(): pl.pallas_call(functools.partial(scores_kernel, step, first, layers), in_...  3.99 us
  transfers between devices with their start and end apart: 11, of which 11 were waited for; matrix products, arithmetic and copies ran while one was open for 1% of the time, Pallas kernels for 6%

profile of v3, /device:TPU:0, one launch (start us, length us, event | category | flops | bytes accessed | tf_op | source)
XLA Modules:
  0.0 62.6 jit_solution(3300397925085221452)
XLA Ops:
  0.5 0.8 %copy.5 = s32[3,256]{0,1:T(8,128)S(1)} copy(s32[3,256]{1,0:T(4,128)} %param.7) | data formatting | bytes 6144 | tf_op args[3]
  1.3 1.6 %copy-done = bf16[256,1,4096]{2,0,1:T(8,128)(2,1)S(1)} copy-done((bf16[256,1,4096]{2,0,1:T(8,128)(2,1)S(1)}, bf16[256,1,4096]{2,0,1:T(8,128)(2,1)}, u32[]{:S(2)}) %copy-start) | copy-done | bytes 2097176
  2.9 1.6 %copy-done.2 = bf16[256,1,4096]{2,0,1:T(8,128)(2,1)S(1)} copy-done((bf16[256,1,4096]{2,0,1:T(8,128)(2,1)S(1)}, bf16[256,1,4096]{2,0,1:T(8,128)(2,1)}, u32[]{:S(2)}) %copy-start.2) | copy-done | bytes 2097176
  4.5 0.7 %copy-done.3 = f32[1,4096]{1,0:T(1,128)S(1)} copy-done((f32[1,4096]{1,0:T(1,128)S(1)}, f32[1,4096]{1,0:T(1,128)}, u32[]{:S(2)}) %copy-start.3) | copy-done | bytes 16408
  5.2 1.5 %scores_step_0.1 = (f32[72,256]{1,0:T(8,128)S(1)}, f32[72,256]{1,0:T(8,128)S(1)}, f32[72,256]{1,0:T(8,128)S(1)}, f32[72,256]{1,0:T(8,128)S(1)}) custom-call(s32[1]{0:T(128)} %bitcast.me_ref, bf16[256,4096]{1,0:T(8,128)(2,1)S(1)} %bitcast.14, bf16[256,4096]{1,0:T(8,128)(2,1)S(1)} %bitcast.7, f32[1,4096]{1,0:T(1,128)S(1)} %copy-done.3, s32[256,3]{1,0:T(8,128)S(1)} %bitcast.10), custom_call_target="tpu_custom_call" | custom-call | flops 536870912 | bytes 4194304 | tf_op jit(solution)/shard_map/scores_step_0/pallas_call | solution.py:76
  6.7 2.6 %collective-permute-start = (f32[72,256]{1,0:T(8,128)S(1)}, f32[72,256]{1,0:T(8,128)S(1)}, u32[]{:S(2)}, u32[]{:S(2)}) collective-permute-start(f32[72,256]{1,0:T(8,128)S(1)} %get-tuple-element.22), channel_id=1, source_target_pairs={{0,1},{1,2},{2,3},{3,0},{4,5},{5,6},{6,7},{7,4},{8,9},{9,10},{10,1... | collective-permute-start | bytes 221192 | tf_op jit(solution)/shard_map/ppermute | solution.py:121
  9.3 2.6 %collective-permute-start.1 = (f32[72,256]{1,0:T(8,128)S(1)}, f32[72,256]{1,0:T(8,128)S(1)}, u32[]{:S(2)}, u32[]{:S(2)}) collective-permute-start(f32[72,256]{1,0:T(8,128)S(1)} %get-tuple-element.23), channel_id=1, source_target_pairs={{0,2},{1,3},{2,0},{3,1},{4,6},{5,7},{6,4},{7,5},{8,10},{9,11},{10,... | collective-permute-start | bytes 221192 | tf_op jit(solution)/shard_map/ppermute | solution.py:121
  11.9 1.3 %collective-permute-start.2 = (f32[72,256]{1,0:T(8,128)S(1)}, f32[72,256]{1,0:T(8,128)S(1)}, u32[]{:S(2)}, u32[]{:S(2)}) collective-permute-start(f32[72,256]{1,0:T(8,128)S(1)} %get-tuple-element.24), channel_id=1, source_target_pairs={{0,3},{1,0},{2,1},{3,2},{4,7},{5,4},{6,5},{7,6},{8,11},{9,8},{10,9... | collective-permute-start | bytes 221192 | tf_op jit(solution)/shard_map/ppermute | solution.py:121
  13.7 4.0 %collective-permute-done.1.refs_2_ = f32[72,256]{1,0:T(8,128)S(1)} collective-permute-done((f32[72,256]{1,0:T(8,128)S(1)}, f32[72,256]{1,0:T(8,128)S(1)}, u32[]{:S(2)}, u32[]{:S(2)}) %collective-permute-start.1) | collective-permute-done | bytes 73760 | tf_op jit(solution)/shard_map/ppermute | solution.py:121
  18.4 7.9 %collective-permute-done.3.x_ref = bf16[256,4096]{1,0:T(8,128)(2,1)S(1)} collective-permute-done((bf16[256,4096]{1,0:T(8,128)(2,1)}, bf16[256,4096]{1,0:T(8,128)(2,1)S(1)}, u32[]{:S(2)}, u32[]{:S(2)}) %collective-permute-start.3) | collective-permute-done | bytes 2097184 | tf_op jit(solution)/shard_map/ppermute | solution.py:121
  26.4 1.2 %scores_step_1.1 = (f32[64,256]{1,0:T(8,128)S(1)}, f32[64,256]{1,0:T(8,128)S(1)}, f32[64,256]{1,0:T(8,128)S(1)}, f32[64,256]{1,0:T(8,128)S(1)}) custom-call(s32[1]{0:T(128)} %bitcast.me_ref, bf16[256,4096]{1,0:T(8,128)(2,1)S(1)} %collective-permute-done.3.x_ref, bf16[256,4096]{1,0:T(8,128)(2,1)S(1)} %bitcast.8, f32[1,4096]{1,0:T(1,128)S(1)} %copy-done.3, ...), custom_call_target="tpu_custom_call" | custom-call | flops 536870912 | bytes 4194304 | tf_op jit(solution)/shard_map/scores_step_1/pallas_call | solution.py:76
  27.6 2.4 %collective-permute-start.4 = (f32[64,256]{1,0:T(8,128)S(1)}, f32[64,256]{1,0:T(8,128)S(1)}, u32[]{:S(2)}, u32[]{:S(2)}) collective-permute-start(f32[64,256]{1,0:T(8,128)S(1)} %get-tuple-element.27), channel_id=1, source_target_pairs={{0,1},{1,2},{2,3},{3,0},{4,5},{5,6},{6,7},{7,4},{8,9},{9,10},{10,1... | collective-permute-start | bytes 196616 | tf_op jit(solution)/shard_map/ppermute | solution.py:121
  30.0 2.6 %collective-permute-start.5 = (f32[64,256]{1,0:T(8,128)S(1)}, f32[64,256]{1,0:T(8,128)S(1)}, u32[]{:S(2)}, u32[]{:S(2)}) collective-permute-start(f32[64,256]{1,0:T(8,128)S(1)} %get-tuple-element.28), channel_id=1, source_target_pairs={{0,2},{1,3},{2,0},{3,1},{4,6},{5,7},{6,4},{7,5},{8,10},{9,11},{10,... | collective-permute-start | bytes 196616 | tf_op jit(solution)/shard_map/ppermute | solution.py:121
  32.6 1.3 %collective-permute-start.6 = (f32[64,256]{1,0:T(8,128)S(1)}, f32[64,256]{1,0:T(8,128)S(1)}, u32[]{:S(2)}, u32[]{:S(2)}) collective-permute-start(f32[64,256]{1,0:T(8,128)S(1)} %get-tuple-element.29), channel_id=1, source_target_pairs={{0,3},{1,0},{2,1},{3,2},{4,7},{5,4},{6,5},{7,6},{8,11},{9,8},{10,9... | collective-permute-start | bytes 196616 | tf_op jit(solution)/shard_map/ppermute | solution.py:121
  34.3 3.7 %collective-permute-done.5.refs_6_ = f32[64,256]{1,0:T(8,128)S(1)} collective-permute-done((f32[64,256]{1,0:T(8,128)S(1)}, f32[64,256]{1,0:T(8,128)S(1)}, u32[]{:S(2)}, u32[]{:S(2)}) %collective-permute-start.5) | collective-permute-done | bytes 65568 | tf_op jit(solution)/shard_map/ppermute | solution.py:121
  38.0 0.7 %collective-permute-done.6.refs_7_ = f32[64,256]{1,0:T(8,128)S(1)} collective-permute-done((f32[64,256]{1,0:T(8,128)S(1)}, f32[64,256]{1,0:T(8,128)S(1)}, u32[]{:S(2)}, u32[]{:S(2)}) %collective-permute-start.6) | collective-permute-done | bytes 65568 | tf_op jit(solution)/shard_map/ppermute | solution.py:121
  38.6 0.7 %base.1 = (f32[3,64,256]{2,1,0:T(8,128)}, f32[1,256]{1,0:T(1,128)S(1)}) custom-call(f32[72,256]{1,0:T(8,128)S(1)} %get-tuple-element.21.refs_0_, f32[72,256]{1,0:T(8,128)S(1)} %collective-permute-done.refs_1_, f32[72,256]{1,0:T(8,128)S(1)} %collective-permute-done.1.refs_2_, f32[72,256]{1,0:T(8,128)S(1)} %collective-permute-done.2.refs_3_, ...), custom_call_target="tpu_custom_call" | custom-call | tf_op jit(solution)/shard_map/base/pallas_call | solution.py:103
  39.3 12.4 %collective-permute-done.7.x_ref = bf16[256,4096]{1,0:T(8,128)(2,1)S(1)} collective-permute-done((bf16[256,4096]{1,0:T(8,128)(2,1)S(1)}, bf16[256,4096]{1,0:T(8,128)(2,1)S(1)}, u32[]{:S(2)}, u32[]{:S(2)}) %collective-permute-start.7) | collective-permute-done | bytes 2097184 | tf_op jit(solution)/shard_map/ppermute | solution.py:121
  51.8 1.2 %scores_step_2.1 = (f32[64,256]{1,0:T(8,128)S(1)}, bf16[64,256]{1,0:T(8,128)(2,1)S(1)}, bf16[64,256]{1,0:T(8,128)(2,1)S(1)}, bf16[64,256]{1,0:T(8,128)(2,1)S(1)}) custom-call(s32[1]{0:T(128)} %bitcast.me_ref, bf16[256,4096]{1,0:T(8,128)(2,1)S(1)} %collective-permute-done.7.x_ref, bf16[256,4096]{1,0:T(8,128)(2,1)S(1)} %bitcast.9, f32[1,4096]{1,0:T(1,128)S(1)} %copy-done.3, ...), custom_call_target="tpu_custom_call" | custom-call | flops 536870912 | bytes 4194304 | tf_op jit(solution)/shard_map/scores_step_2/pallas_call | solution.py:76
  53.0 2.4 %collective-permute-start.8 = (bf16[64,256]{1,0:T(8,128)(2,1)S(1)}, bf16[64,256]{1,0:T(8,128)(2,1)S(1)}, u32[]{:S(2)}, u32[]{:S(2)}) collective-permute-start(bf16[64,256]{1,0:T(8,128)(2,1)S(1)} %get-tuple-element.34), channel_id=1, source_target_pairs={{0,1},{1,2},{2,3},{3,0},{4,5},{5,6},{6,7},{7,4},{8,9},{9,10},{10,1... | collective-permute-start | bytes 98312 | tf_op jit(solution)/shard_map/ppermute | solution.py:121
  55.4 2.6 %collective-permute-start.9 = (bf16[64,256]{1,0:T(8,128)(2,1)S(1)}, bf16[64,256]{1,0:T(8,128)(2,1)S(1)}, u32[]{:S(2)}, u32[]{:S(2)}) collective-permute-start(bf16[64,256]{1,0:T(8,128)(2,1)S(1)} %get-tuple-element.35), channel_id=1, source_target_pairs={{0,2},{1,3},{2,0},{3,1},{4,6},{5,7},{6,4},{7,5},{8,10},{9,11},{10,... | collective-permute-start | bytes 98312 | tf_op jit(solution)/shard_map/ppermute | solution.py:121
  58.0 1.3 %collective-permute-start.10 = (bf16[64,256]{1,0:T(8,128)(2,1)S(1)}, bf16[64,256]{1,0:T(8,128)(2,1)S(1)}, u32[]{:S(2)}, u32[]{:S(2)}) collective-permute-start(bf16[64,256]{1,0:T(8,128)(2,1)S(1)} %get-tuple-element.36), channel_id=1, source_target_pairs={{0,3},{1,0},{2,1},{3,2},{4,7},{5,4},{6,5},{7,6},{8,11},{9,8},{10,9... | collective-permute-start | bytes 98312 | tf_op jit(solution)/shard_map/ppermute | solution.py:121
  60.2 1.7 %collective-permute-done.10 = bf16[64,256]{1,0:T(8,128)(2,1)S(1)} collective-permute-done((bf16[64,256]{1,0:T(8,128)(2,1)S(1)}, bf16[64,256]{1,0:T(8,128)(2,1)S(1)}, u32[]{:S(2)}, u32[]{:S(2)}) %collective-permute-start.10) | collective-permute-done | bytes 32800 | tf_op jit(solution)/shard_map/ppermute | solution.py:121
  61.9 0.6 %bitcast_dynamic-update-slice_fusion = f32[3,64,256]{2,1,0:T(8,128)} fusion(f32[3,64,256]{2,1,0:T(8,128)} %get-tuple-element.30, bf16[64,256]{1,0:T(8,128)(2,1)S(1)} %collective-permute-done.10, bf16[64,256]{1,0:T(8,128)(2,1)S(1)} %collective-permute-done.9, f32[64,256]{1,0:T(8,128)S(1)} %get-tuple-element.33, bf16[64,256]{1,0:T(8,128)(2,1)S(1)} %collective-permute-done.8, ...), kind=kLoop, calls=%fused_computation | loop fusion | flops 114688 | bytes 230400 | tf_op jit(solution)/shard_map/dynamic_update_slice | solution.py:137
  (12 shorter events, 2.8 us)
Async XLA Ops:
  0.0 26.3 %collective-permute-start.3 = (bf16[256,4096]{1,0:T(8,128)(2,1)}, bf16[256,4096]{1,0:T(8,128)(2,1)S(1)}, u32[]{:S(2)}, u32[]{:S(2)}) collective-permute-start(bf16[256,4096]{1,0:T(8,128)(2,1)} %bitcast.13), channel_id=1, source_target_pairs={{0,4},{4,8},{8,12},{12,0},{1,5},{5,9},{9,13},{13,1},{2,6},{6,10},{... | collective-permute-start | bytes 6291464 | tf_op jit(solution)/shard_map/ppermute | solution.py:121
  1.3 1.6 %copy-start = (bf16[256,1,4096]{2,0,1:T(8,128)(2,1)S(1)}, bf16[256,1,4096]{2,0,1:T(8,128)(2,1)}, u32[]{:S(2)}) copy-start(bf16[256,1,4096]{2,0,1:T(8,128)(2,1)} %param.4) | copy-start | bytes 6291460
  2.9 1.6 %copy-start.2 = (bf16[256,1,4096]{2,0,1:T(8,128)(2,1)S(1)}, bf16[256,1,4096]{2,0,1:T(8,128)(2,1)}, u32[]{:S(2)}) copy-start(bf16[256,1,4096]{2,0,1:T(8,128)(2,1)} %param.5) | copy-start | bytes 6291460
  4.5 0.7 %copy-start.3 = (f32[1,4096]{1,0:T(1,128)S(1)}, f32[1,4096]{1,0:T(1,128)}, u32[]{:S(2)}) copy-start(f32[1,4096]{1,0:T(1,128)} %eig_ref.5) | copy-start | bytes 49156
  5.2 21.2 %copy-start.1 = (bf16[256,1,4096]{2,0,1:T(8,128)(2,1)S(1)}, bf16[256,1,4096]{2,0,1:T(8,128)(2,1)}, u32[]{:S(2)}) copy-start(bf16[256,1,4096]{2,0,1:T(8,128)(2,1)} %param.4) | copy-start | bytes 6291460
  6.7 7.0 %collective-permute-start = (f32[72,256]{1,0:T(8,128)S(1)}, f32[72,256]{1,0:T(8,128)S(1)}, u32[]{:S(2)}, u32[]{:S(2)}) collective-permute-start(f32[72,256]{1,0:T(8,128)S(1)} %get-tuple-element.22), channel_id=1, source_target_pairs={{0,1},{1,2},{2,3},{3,0},{4,5},{5,6},{6,7},{7,4},{8,9},{9,10},{10,1... | collective-permute-start | bytes 221192 | tf_op jit(solution)/shard_map/ppermute | solution.py:121
  9.3 8.4 %collective-permute-start.1 = (f32[72,256]{1,0:T(8,128)S(1)}, f32[72,256]{1,0:T(8,128)S(1)}, u32[]{:S(2)}, u32[]{:S(2)}) collective-permute-start(f32[72,256]{1,0:T(8,128)S(1)} %get-tuple-element.23), channel_id=1, source_target_pairs={{0,2},{1,3},{2,0},{3,1},{4,6},{5,7},{6,4},{7,5},{8,10},{9,11},{10,... | collective-permute-start | bytes 221192 | tf_op jit(solution)/shard_map/ppermute | solution.py:121
  11.9 6.4 %collective-permute-start.2 = (f32[72,256]{1,0:T(8,128)S(1)}, f32[72,256]{1,0:T(8,128)S(1)}, u32[]{:S(2)}, u32[]{:S(2)}) collective-permute-start(f32[72,256]{1,0:T(8,128)S(1)} %get-tuple-element.24), channel_id=1, source_target_pairs={{0,3},{1,0},{2,1},{3,2},{4,7},{5,4},{6,5},{7,6},{8,11},{9,8},{10,9... | collective-permute-start | bytes 221192 | tf_op jit(solution)/shard_map/ppermute | solution.py:121
  26.3 25.5 %collective-permute-start.7 = (bf16[256,4096]{1,0:T(8,128)(2,1)S(1)}, bf16[256,4096]{1,0:T(8,128)(2,1)S(1)}, u32[]{:S(2)}, u32[]{:S(2)}) collective-permute-start(bf16[256,4096]{1,0:T(8,128)(2,1)S(1)} %collective-permute-done.3.x_ref), channel_id=1, source_target_pairs={{0,4},{4,8},{8,12},{12,0},{1,5},{5,9},{9,13},{13,1},{2,6},{6,10},{... | collective-permute-start | bytes 6291464 | tf_op jit(solution)/shard_map/ppermute | solution.py:121
  27.6 6.7 %collective-permute-start.4 = (f32[64,256]{1,0:T(8,128)S(1)}, f32[64,256]{1,0:T(8,128)S(1)}, u32[]{:S(2)}, u32[]{:S(2)}) collective-permute-start(f32[64,256]{1,0:T(8,128)S(1)} %get-tuple-element.27), channel_id=1, source_target_pairs={{0,1},{1,2},{2,3},{3,0},{4,5},{5,6},{6,7},{7,4},{8,9},{9,10},{10,1... | collective-permute-start | bytes 196616 | tf_op jit(solution)/shard_map/ppermute | solution.py:121
  30.0 8.0 %collective-permute-start.5 = (f32[64,256]{1,0:T(8,128)S(1)}, f32[64,256]{1,0:T(8,128)S(1)}, u32[]{:S(2)}, u32[]{:S(2)}) collective-permute-start(f32[64,256]{1,0:T(8,128)S(1)} %get-tuple-element.28), channel_id=1, source_target_pairs={{0,2},{1,3},{2,0},{3,1},{4,6},{5,7},{6,4},{7,5},{8,10},{9,11},{10,... | collective-permute-start | bytes 196616 | tf_op jit(solution)/shard_map/ppermute | solution.py:121
  32.6 6.0 %collective-permute-start.6 = (f32[64,256]{1,0:T(8,128)S(1)}, f32[64,256]{1,0:T(8,128)S(1)}, u32[]{:S(2)}, u32[]{:S(2)}) collective-permute-start(f32[64,256]{1,0:T(8,128)S(1)} %get-tuple-element.29), channel_id=1, source_target_pairs={{0,3},{1,0},{2,1},{3,2},{4,7},{5,4},{6,5},{7,6},{8,11},{9,8},{10,9... | collective-permute-start | bytes 196616 | tf_op jit(solution)/shard_map/ppermute | solution.py:121
  53.0 6.7 %collective-permute-start.8 = (bf16[64,256]{1,0:T(8,128)(2,1)S(1)}, bf16[64,256]{1,0:T(8,128)(2,1)S(1)}, u32[]{:S(2)}, u32[]{:S(2)}) collective-permute-start(bf16[64,256]{1,0:T(8,128)(2,1)S(1)} %get-tuple-element.34), channel_id=1, source_target_pairs={{0,1},{1,2},{2,3},{3,0},{4,5},{5,6},{6,7},{7,4},{8,9},{9,10},{10,1... | collective-permute-start | bytes 98312 | tf_op jit(solution)/shard_map/ppermute | solution.py:121
  55.4 4.8 %collective-permute-start.9 = (bf16[64,256]{1,0:T(8,128)(2,1)S(1)}, bf16[64,256]{1,0:T(8,128)(2,1)S(1)}, u32[]{:S(2)}, u32[]{:S(2)}) collective-permute-start(bf16[64,256]{1,0:T(8,128)(2,1)S(1)} %get-tuple-element.35), channel_id=1, source_target_pairs={{0,2},{1,3},{2,0},{3,1},{4,6},{5,7},{6,4},{7,5},{8,10},{9,11},{10,... | collective-permute-start | bytes 98312 | tf_op jit(solution)/shard_map/ppermute | solution.py:121
  58.0 3.9 %collective-permute-start.10 = (bf16[64,256]{1,0:T(8,128)(2,1)S(1)}, bf16[64,256]{1,0:T(8,128)(2,1)S(1)}, u32[]{:S(2)}, u32[]{:S(2)}) collective-permute-start(bf16[64,256]{1,0:T(8,128)(2,1)S(1)} %get-tuple-element.36), channel_id=1, source_target_pairs={{0,3},{1,0},{2,1},{3,2},{4,7},{5,4},{6,5},{7,6},{8,11},{9,8},{10,9... | collective-permute-start | bytes 98312 | tf_op jit(solution)/shard_map/ppermute | solution.py:121

commit v4 on v3

--- a/solution.py
+++ b/solution.py
@@ -42,14 +42,18 @@
     return total
 
 
-def scores_kernel(step, first, layers, me_ref, x_ref, t_ref, eig_ref, order_ref, *refs):
+def scores_kernel(step, first, layers, n_x, me_ref, *refs):
+    x_refs, (t_ref, eig_ref, order_ref), refs = refs[:n_x], refs[n_x : n_x + 3], refs[n_x + 3 :]
     outs, acc = refs[:layers], refs[layers]
     p, squares = None, None
     for c in range(0, t_ref.shape[1], PART):
         columns = slice(c, c + PART)
         weights = 1.0 / (eig_ref[:, columns] + 0.05)
         t = t_ref[:, columns]
-        x = (x_ref[:, columns].astype(F32) * weights).astype(BF16)
+        x = x_refs[0][:, columns].astype(F32)
+        for ref in x_refs[1:]:
+            x = x + ref[:, columns].astype(F32)
+        x = (x * weights).astype(BF16)
         part = dot(x, t, ((1,), (1,)))
         p = part if p is None else p + part
         if first:
@@ -63,19 +67,19 @@
     if first:
         extra = jnp.broadcast_to(jnp.sum(squares.T, axis=0, keepdims=True), (EXTRA, p.shape[1]))
     for by in range(layers):
-        start = pl.multiple_of(lax.rem(me_ref[0] + by, layers) * own, own)
+        start = pl.multiple_of((me_ref[0] ^ by) * own, own)
         outs[by][:own] = acc[pl.ds(start, own)].astype(outs[by].dtype)
         if first:
             outs[by][own:] = extra
 
 
-def scores_call(step, first, layers, me, x, t, eig, order, sent):
+def scores_call(step, first, layers, me, xs, t, eig, order, sent):
     rows, depth = t.shape
-    queries = x.shape[0]
+    queries = xs[0].shape[0]
     own = queries // layers + (EXTRA if first else 0)
     return pl.pallas_call(
-        functools.partial(scores_kernel, step, first, layers),
-        in_specs=[SMEM] + [VMEM] * 4,
+        functools.partial(scores_kernel, step, first, layers, len(xs)),
+        in_specs=[SMEM] + [VMEM] * (len(xs) + 3),
         out_specs=[VMEM] * layers,
         scratch_shapes=[pltpu.VMEM((queries, rows), F32)],
         out_shape=[jax.ShapeDtypeStruct((own, rows), F32 if by == 0 else sent) for by in range(layers)],
@@ -84,7 +88,7 @@
             flops=2 * queries * rows * depth, bytes_accessed=4 * queries * depth, transcendentals=0
         ),
         name="scores_step_" + str(step),
-    )(me, x, t, eig, order)
+    )(me, *xs, t, eig, order)
 
 
 def base_kernel(layers, *refs):
@@ -110,27 +114,27 @@
 
 def per_device(train_grads, query_grads, eigenvalues, order):
     rows, queries = train_grads.shape[0], query_grads.shape[0]
-    layers = lax.axis_size("layer")
+    layers, blks = lax.axis_size("layer"), lax.axis_size("blk")
     me = lax.axis_index("layer").astype(jnp.int32).reshape(1)
     t = train_grads.reshape(rows, -1)
     q = query_grads.reshape(queries, -1)
     columns = order.T
 
-    def shifted(x, axis, by):
-        length = lax.axis_size(axis)
-        return lax.ppermute(x, axis, [(i, (i + by) % length) for i in range(length)])
+    def exchange(pieces):
+        order = [1, *range(layers - 1, 1, -1)]
+        got = [lax.ppermute(pieces[by], "layer", [(i, i ^ by) for i in range(layers)]) for by in order]
+        return [pieces[0]] + got
 
-    def exchange(pieces):
-        return [pieces[0]] + [shifted(pieces[by], "layer", by) for by in range(1, layers)]
-
-    one_back = shifted(q, "blk", 1)
-    sums0 = exchange(scores_call(0, True, layers, me, q, t, eigenvalues, columns, F32))
-    one_back = after(one_back, *sums0)
-    two_back = shifted(one_back, "blk", 1)
-    sums1 = exchange(scores_call(1, False, layers, me, one_back, t, eigenvalues, columns, F32))
+    one_back = lax.ppermute(q, "blk", [(i, (i + 1) % blks) for i in range(blks)])
+    sums0 = exchange(scores_call(0, True, layers, me, [q], t, eigenvalues, columns, F32))
+    later = after(q, *sums0)
+    even_two = lax.ppermute(later, "blk", [(i, (i + 2) % blks) for i in range(0, blks, 2)])
+    one_back = after(one_back, later)
+    odd_two = lax.ppermute(one_back, "blk", [(i, i + 1) for i in range(0, blks, 2)])
+    sums1 = exchange(scores_call(1, False, layers, me, [one_back], t, eigenvalues, columns, F32))
     base, inverse = base_call(layers, sums0, sums1)
     t2 = after(t, inverse)
-    sums2 = exchange(scores_call(2, False, layers, me, two_back, t2, eigenvalues, columns, BF16))
+    sums2 = exchange(scores_call(2, False, layers, me, [even_two, odd_two], t2, eigenvalues, columns, BF16))
     total = sums2[0]
     for piece in sums2[1:]:
         total = total + piece.astype(F32)

time: 62.9 us -> 60.4 us (0.960)
  waiting for transfers between devices: 32.7 us -> 26.4 us
  starting transfers between devices: 19.8 us -> 23.4 us
    ppermute x11 -> x12, waiting for transfers between devices: 32.7 us -> 26.4 us  [the longest x9 17.3 us: exchange(): lax.ppermute(pieces[by], 'layer', [(i, i ^ by) for i in range(layers)])]
    ppermute x11 -> x12, starting transfers between devices: 19.8 us -> 23.4 us  [the longest x9 16.7 us: exchange(): lax.ppermute(pieces[by], 'layer', [(i, i ^ by) for i in range(layers)])]
    unnamed x9 -> x11, local copies, waits for them, and re-layouts: 4.71 us -> 4.71 us
  transfers between devices with their start and end apart: 11 -> 12, of which waited for: 11 -> 8; matrix products, arithmetic and copies ran while one was open for 1% -> 1% of each run, Pallas kernels for 6% -> 6%
where the time goes in v4:
time: 60.4 us; the launch traced here: 60.1 us
  waiting for transfers between devices  26.4 us (44%)
  starting transfers between devices  23.4 us (39%)
  Pallas kernels  4.79 us (8%)
  local copies, waits for them, and re-layouts  4.71 us (8%)
  other arithmetic  0.65 us (1%)
    ppermute x9, waiting for transfers between devices, exchange(): lax.ppermute(pieces[by], 'layer', [(i, i ^ by) for i in range(layers)])  17.3 us
    ppermute x9, starting transfers between devices, exchange(): lax.ppermute(pieces[by], 'layer', [(i, i ^ by) for i in range(layers)])  16.7 us
    unnamed x11, local copies, waits for them, and re-layouts  4.71 us
    ppermute x1, waiting for transfers between devices, per_device(): lax.ppermute(later, 'blk', [(i, (i + 2) % blks) for i in range(0, blks, 2)])  4.65 us
    ppermute x1, waiting for transfers between devices, per_device(): lax.ppermute(q, 'blk', [(i, (i + 1) % blks) for i in range(blks)])  4.47 us
    pallas_call x3, Pallas kernels, scores_call(): pl.pallas_call(functools.partial(scores_kernel, step, first, layers, len(...  4.08 us
    ppermute x1, starting transfers between devices, per_device(): lax.ppermute(one_back, 'blk', [(i, i + 1) for i in range(0, blks, 2)])  3.24 us
    ppermute x1, starting transfers between devices, per_device(): lax.ppermute(later, 'blk', [(i, (i + 2) % blks) for i in range(0, blks, 2)])  3.02 us
  transfers between devices with their start and end apart: 12, of which 8 were waited for; matrix products, arithmetic and copies ran while one was open for 1% of the time, Pallas kernels for 6%

profile of v4, /device:TPU:0, one launch (start us, length us, event | category | flops | bytes accessed | tf_op | source)
XLA Modules:
  0.0 60.1 jit_solution(12811304293034136536)
XLA Ops:
  0.5 0.8 %copy.5 = s32[3,256]{0,1:T(8,128)S(1)} copy(s32[3,256]{1,0:T(4,128)} %param.7) | data formatting | bytes 6144 | tf_op args[3]
  1.3 1.6 %copy-done = bf16[256,1,4096]{2,0,1:T(8,128)(2,1)S(1)} copy-done((bf16[256,1,4096]{2,0,1:T(8,128)(2,1)S(1)}, bf16[256,1,4096]{2,0,1:T(8,128)(2,1)}, u32[]{:S(2)}) %copy-start) | copy-done | bytes 2097176
  2.9 1.6 %copy-done.2 = bf16[256,1,4096]{2,0,1:T(8,128)(2,1)S(1)} copy-done((bf16[256,1,4096]{2,0,1:T(8,128)(2,1)S(1)}, bf16[256,1,4096]{2,0,1:T(8,128)(2,1)}, u32[]{:S(2)}) %copy-start.2) | copy-done | bytes 2097176
  4.5 0.7 %copy-done.4 = f32[1,4096]{1,0:T(1,128)S(1)} copy-done((f32[1,4096]{1,0:T(1,128)S(1)}, f32[1,4096]{1,0:T(1,128)}, u32[]{:S(2)}) %copy-start.4) | copy-done | bytes 16408
  5.2 1.5 %scores_step_0.1 = (f32[72,256]{1,0:T(8,128)S(1)}, f32[72,256]{1,0:T(8,128)S(1)}, f32[72,256]{1,0:T(8,128)S(1)}, f32[72,256]{1,0:T(8,128)S(1)}) custom-call(s32[1]{0:T(128)} %bitcast.me_ref, bf16[256,4096]{1,0:T(8,128)(2,1)S(1)} %bitcast.14, bf16[256,4096]{1,0:T(8,128)(2,1)S(1)} %bitcast.7, f32[1,4096]{1,0:T(1,128)S(1)} %copy-done.4, s32[256,3]{1,0:T(8,128)S(1)} %bitcast.10), custom_call_target="tpu_custom_call" | custom-call | flops 536870912 | bytes 4194304 | tf_op jit(solution)/shard_map/scores_step_0/pallas_call | solution.py:80
  6.7 2.6 %collective-permute-start = (f32[72,256]{1,0:T(8,128)S(1)}, f32[72,256]{1,0:T(8,128)S(1)}, u32[]{:S(2)}, u32[]{:S(2)}) collective-permute-start(f32[72,256]{1,0:T(8,128)S(1)} %get-tuple-element.23), channel_id=1, source_target_pairs={{0,1},{1,0},{2,3},{3,2},{4,5},{5,4},{6,7},{7,6},{8,9},{9,8},{10,11... | collective-permute-start | bytes 221192 | tf_op jit(solution)/shard_map/ppermute | solution.py:125
  9.4 2.5 %collective-permute-start.1 = (f32[72,256]{1,0:T(8,128)S(1)}, f32[72,256]{1,0:T(8,128)S(1)}, u32[]{:S(2)}, u32[]{:S(2)}) collective-permute-start(f32[72,256]{1,0:T(8,128)S(1)} %get-tuple-element.24), channel_id=1, source_target_pairs={{0,3},{1,2},{2,1},{3,0},{4,7},{5,6},{6,5},{7,4},{8,11},{9,10},{10,... | collective-permute-start | bytes 221192 | tf_op jit(solution)/shard_map/ppermute | solution.py:125
  11.9 4.4 %collective-permute-done.1.refs_2_ = f32[72,256]{1,0:T(8,128)S(1)} collective-permute-done((f32[72,256]{1,0:T(8,128)S(1)}, f32[72,256]{1,0:T(8,128)S(1)}, u32[]{:S(2)}, u32[]{:S(2)}) %collective-permute-start.1) | collective-permute-done | bytes 73760 | tf_op jit(solution)/shard_map/ppermute | solution.py:125
  16.3 3.5 %collective-permute-done.2.refs_3_ = f32[72,256]{1,0:T(8,128)S(1)} collective-permute-done((f32[72,256]{1,0:T(8,128)S(1)}, f32[72,256]{1,0:T(8,128)S(1)}, u32[]{:S(2)}, u32[]{:S(2)}) %collective-permute-start.2) | collective-permute-done | bytes 73760 | tf_op jit(solution)/shard_map/ppermute | solution.py:125
  19.8 3.0 %collective-permute-start.7 = (bf16[256,4096]{1,0:T(8,128)(2,1)S(1)}, bf16[256,4096]{1,0:T(8,128)(2,1)S(1)}, u32[]{:S(2)}, u32[]{:S(2)}) collective-permute-start(bf16[256,4096]{1,0:T(8,128)(2,1)S(1)} %bitcast.15), channel_id=1, source_target_pairs={{0,8},{8,0},{1,9},{9,1},{2,10},{10,2},{3,11},{11,3},{16,24},{24,16... | collective-permute-start | bytes 6291464 | tf_op jit(solution)/shard_map/ppermute | solution.py:131
  22.8 4.5 %collective-permute-done.3.refs_0_ = bf16[256,4096]{1,0:T(8,128)(2,1)S(1)} collective-permute-done((bf16[256,4096]{1,0:T(8,128)(2,1)}, bf16[256,4096]{1,0:T(8,128)(2,1)S(1)}, u32[]{:S(2)}, u32[]{:S(2)}) %collective-permute-start.3) | collective-permute-done | bytes 2097184 | tf_op jit(solution)/shard_map/ppermute | solution.py:128
  27.3 3.2 %collective-permute-start.8 = (bf16[256,4096]{1,0:T(8,128)(2,1)S(1)}, bf16[256,4096]{1,0:T(8,128)(2,1)S(1)}, u32[]{:S(2)}, u32[]{:S(2)}) collective-permute-start(bf16[256,4096]{1,0:T(8,128)(2,1)S(1)} %collective-permute-done.3.refs_0_), channel_id=1, source_target_pairs={{0,4},{8,12},{1,5},{9,13},{2,6},{10,14},{3,7},{11,15},{16,20},{24,... | collective-permute-start | bytes 6291464 | tf_op jit(solution)/shard_map/ppermute | solution.py:133
  30.6 1.2 %scores_step_1.1 = (f32[64,256]{1,0:T(8,128)S(1)}, f32[64,256]{1,0:T(8,128)S(1)}, f32[64,256]{1,0:T(8,128)S(1)}, f32[64,256]{1,0:T(8,128)S(1)}) custom-call(s32[1]{0:T(128)} %bitcast.me_ref, bf16[256,4096]{1,0:T(8,128)(2,1)S(1)} %collective-permute-done.3.refs_0_, bf16[256,4096]{1,0:T(8,128)(2,1)S(1)} %bitcast.8, f32[1,4096]{1,0:T(1,128)S(1)} %copy-done.4, ...), custom_call_target="tpu_custom_call" | custom-call | flops 536870912 | bytes 4194304 | tf_op jit(solution)/shard_map/scores_step_1/pallas_call | solution.py:80
  31.8 3.3 %collective-permute-start.4 = (f32[64,256]{1,0:T(8,128)S(1)}, f32[64,256]{1,0:T(8,128)S(1)}, u32[]{:S(2)}, u32[]{:S(2)}) collective-permute-start(f32[64,256]{1,0:T(8,128)S(1)} %get-tuple-element.29), channel_id=1, source_target_pairs={{0,1},{1,0},{2,3},{3,2},{4,5},{5,4},{6,7},{7,6},{8,9},{9,8},{10,11... | collective-permute-start | bytes 196616 | tf_op jit(solution)/shard_map/ppermute | solution.py:125
  35.2 3.0 %collective-permute-start.5 = (f32[64,256]{1,0:T(8,128)S(1)}, f32[64,256]{1,0:T(8,128)S(1)}, u32[]{:S(2)}, u32[]{:S(2)}) collective-permute-start(f32[64,256]{1,0:T(8,128)S(1)} %get-tuple-element.30), channel_id=1, source_target_pairs={{0,3},{1,2},{2,1},{3,0},{4,7},{5,6},{6,5},{7,4},{8,11},{9,10},{10,... | collective-permute-start | bytes 196616 | tf_op jit(solution)/shard_map/ppermute | solution.py:125
  38.1 3.3 %collective-permute-done.5.refs_6_ = f32[64,256]{1,0:T(8,128)S(1)} collective-permute-done((f32[64,256]{1,0:T(8,128)S(1)}, f32[64,256]{1,0:T(8,128)S(1)}, u32[]{:S(2)}, u32[]{:S(2)}) %collective-permute-start.5) | collective-permute-done | bytes 65568 | tf_op jit(solution)/shard_map/ppermute | solution.py:125
  41.4 2.0 %collective-permute-done.6.refs_7_ = f32[64,256]{1,0:T(8,128)S(1)} collective-permute-done((f32[64,256]{1,0:T(8,128)S(1)}, f32[64,256]{1,0:T(8,128)S(1)}, u32[]{:S(2)}, u32[]{:S(2)}) %collective-permute-start.6) | collective-permute-done | bytes 65568 | tf_op jit(solution)/shard_map/ppermute | solution.py:125
  43.4 0.7 %base.1 = (f32[3,64,256]{2,1,0:T(8,128)}, f32[1,256]{1,0:T(1,128)S(1)}) custom-call(f32[72,256]{1,0:T(8,128)S(1)} %get-tuple-element.22.refs_0_, f32[72,256]{1,0:T(8,128)S(1)} %collective-permute-done.refs_1_, f32[72,256]{1,0:T(8,128)S(1)} %collective-permute-done.1.refs_2_, f32[72,256]{1,0:T(8,128)S(1)} %collective-permute-done.2.refs_3_, ...), custom_call_target="tpu_custom_call" | custom-call | tf_op jit(solution)/shard_map/base/pallas_call | solution.py:107
  44.1 4.7 %collective-permute-done.7.refs_0_ = bf16[256,4096]{1,0:T(8,128)(2,1)S(1)} collective-permute-done((bf16[256,4096]{1,0:T(8,128)(2,1)S(1)}, bf16[256,4096]{1,0:T(8,128)(2,1)S(1)}, u32[]{:S(2)}, u32[]{:S(2)}) %collective-permute-start.7) | collective-permute-done | bytes 2097184 | tf_op jit(solution)/shard_map/ppermute | solution.py:131
  48.8 1.3 %scores_step_2.1 = (f32[64,256]{1,0:T(8,128)S(1)}, bf16[64,256]{1,0:T(8,128)(2,1)S(1)}, bf16[64,256]{1,0:T(8,128)(2,1)S(1)}, bf16[64,256]{1,0:T(8,128)(2,1)S(1)}) custom-call(s32[1]{0:T(128)} %bitcast.me_ref, bf16[256,4096]{1,0:T(8,128)(2,1)S(1)} %collective-permute-done.7.refs_0_, bf16[256,4096]{1,0:T(8,128)(2,1)S(1)} %collective-permute-done.8.refs_1_, ...), custom_call_target="tpu_custom_call" | custom-call | flops 536870912 | bytes 4194304 | tf_op jit(solution)/shard_map/scores_step_2/pallas_call | solution.py:80
  50.1 4.5 %collective-permute-start.10 = (bf16[64,256]{1,0:T(8,128)(2,1)S(1)}, bf16[64,256]{1,0:T(8,128)(2,1)S(1)}, u32[]{:S(2)}, u32[]{:S(2)}) collective-permute-start(bf16[64,256]{1,0:T(8,128)(2,1)S(1)} %get-tuple-element.37), channel_id=1, source_target_pairs={{0,3},{1,2},{2,1},{3,0},{4,7},{5,6},{6,5},{7,4},{8,11},{9,10},{10,... | collective-permute-start | bytes 98312 | tf_op jit(solution)/shard_map/ppermute | solution.py:125
  55.2 1.3 %collective-permute-done.10 = bf16[64,256]{1,0:T(8,128)(2,1)S(1)} collective-permute-done((bf16[64,256]{1,0:T(8,128)(2,1)S(1)}, bf16[64,256]{1,0:T(8,128)(2,1)S(1)}, u32[]{:S(2)}, u32[]{:S(2)}) %collective-permute-start.10) | collective-permute-done | bytes 32800 | tf_op jit(solution)/shard_map/ppermute | solution.py:125
  56.5 2.9 %collective-permute-done.11 = bf16[64,256]{1,0:T(8,128)(2,1)S(1)} collective-permute-done((bf16[64,256]{1,0:T(8,128)(2,1)S(1)}, bf16[64,256]{1,0:T(8,128)(2,1)S(1)}, u32[]{:S(2)}, u32[]{:S(2)}) %collective-permute-start.11) | collective-permute-done | bytes 32800 | tf_op jit(solution)/shard_map/ppermute | solution.py:125
  59.4 0.6 %bitcast_dynamic-update-slice_fusion = f32[3,64,256]{2,1,0:T(8,128)} fusion(f32[3,64,256]{2,1,0:T(8,128)} %get-tuple-element.32, bf16[64,256]{1,0:T(8,128)(2,1)S(1)} %collective-permute-done.11, bf16[64,256]{1,0:T(8,128)(2,1)S(1)} %collective-permute-done.10, f32[64,256]{1,0:T(8,128)S(1)} %get-tuple-element.35, bf16[64,256]{1,0:T(8,128)(2,1)S(1)} %collective-permute-done.9, ...), kind=kLoop, calls=%fused_computation | loop fusion | flops 114688 | bytes 230400 | tf_op jit(solution)/shard_map/dynamic_update_slice | solution.py:141
  (16 shorter events, 1.2 us)
Async XLA Ops:
  0.0 27.3 %collective-permute-start.3 = (bf16[256,4096]{1,0:T(8,128)(2,1)}, bf16[256,4096]{1,0:T(8,128)(2,1)S(1)}, u32[]{:S(2)}, u32[]{:S(2)}) collective-permute-start(bf16[256,4096]{1,0:T(8,128)(2,1)} %bitcast.13), channel_id=1, source_target_pairs={{0,4},{4,8},{8,12},{12,0},{1,5},{5,9},{9,13},{13,1},{2,6},{6,10},{... | collective-permute-start | bytes 6291464 | tf_op jit(solution)/shard_map/ppermute | solution.py:128
  1.3 1.6 %copy-start = (bf16[256,1,4096]{2,0,1:T(8,128)(2,1)S(1)}, bf16[256,1,4096]{2,0,1:T(8,128)(2,1)}, u32[]{:S(2)}) copy-start(bf16[256,1,4096]{2,0,1:T(8,128)(2,1)} %param.4) | copy-start | bytes 6291460
  2.9 1.6 %copy-start.2 = (bf16[256,1,4096]{2,0,1:T(8,128)(2,1)S(1)}, bf16[256,1,4096]{2,0,1:T(8,128)(2,1)}, u32[]{:S(2)}) copy-start(bf16[256,1,4096]{2,0,1:T(8,128)(2,1)} %param.5) | copy-start | bytes 6291460
  4.5 0.7 %copy-start.4 = (f32[1,4096]{1,0:T(1,128)S(1)}, f32[1,4096]{1,0:T(1,128)}, u32[]{:S(2)}) copy-start(f32[1,4096]{1,0:T(1,128)} %refs_3_.1) | copy-start | bytes 49156
  5.2 14.6 %copy-start.3 = (bf16[256,1,4096]{2,0,1:T(8,128)(2,1)S(1)}, bf16[256,1,4096]{2,0,1:T(8,128)(2,1)}, u32[]{:S(2)}) copy-start(bf16[256,1,4096]{2,0,1:T(8,128)(2,1)} %param.5) | copy-start | bytes 6291460
  5.2 25.4 %copy-start.1 = (bf16[256,1,4096]{2,0,1:T(8,128)(2,1)S(1)}, bf16[256,1,4096]{2,0,1:T(8,128)(2,1)}, u32[]{:S(2)}) copy-start(bf16[256,1,4096]{2,0,1:T(8,128)(2,1)} %param.4) | copy-start | bytes 6291460
  6.7 5.2 %collective-permute-start = (f32[72,256]{1,0:T(8,128)S(1)}, f32[72,256]{1,0:T(8,128)S(1)}, u32[]{:S(2)}, u32[]{:S(2)}) collective-permute-start(f32[72,256]{1,0:T(8,128)S(1)} %get-tuple-element.23), channel_id=1, source_target_pairs={{0,1},{1,0},{2,3},{3,2},{4,5},{5,4},{6,7},{7,6},{8,9},{9,8},{10,11... | collective-permute-start | bytes 221192 | tf_op jit(solution)/shard_map/ppermute | solution.py:125
  9.4 6.9 %collective-permute-start.1 = (f32[72,256]{1,0:T(8,128)S(1)}, f32[72,256]{1,0:T(8,128)S(1)}, u32[]{:S(2)}, u32[]{:S(2)}) collective-permute-start(f32[72,256]{1,0:T(8,128)S(1)} %get-tuple-element.24), channel_id=1, source_target_pairs={{0,3},{1,2},{2,1},{3,0},{4,7},{5,6},{6,5},{7,4},{8,11},{9,10},{10,... | collective-permute-start | bytes 221192 | tf_op jit(solution)/shard_map/ppermute | solution.py:125
  11.8 8.0 %collective-permute-start.2 = (f32[72,256]{1,0:T(8,128)S(1)}, f32[72,256]{1,0:T(8,128)S(1)}, u32[]{:S(2)}, u32[]{:S(2)}) collective-permute-start(f32[72,256]{1,0:T(8,128)S(1)} %get-tuple-element.25), channel_id=1, source_target_pairs={{0,2},{1,3},{2,0},{3,1},{4,6},{5,7},{6,4},{7,5},{8,10},{9,11},{10,... | collective-permute-start | bytes 221192 | tf_op jit(solution)/shard_map/ppermute | solution.py:125
  19.8 29.0 %collective-permute-start.7 = (bf16[256,4096]{1,0:T(8,128)(2,1)S(1)}, bf16[256,4096]{1,0:T(8,128)(2,1)S(1)}, u32[]{:S(2)}, u32[]{:S(2)}) collective-permute-start(bf16[256,4096]{1,0:T(8,128)(2,1)S(1)} %bitcast.15), channel_id=1, source_target_pairs={{0,8},{8,0},{1,9},{9,1},{2,10},{10,2},{3,11},{11,3},{16,24},{24,16... | collective-permute-start | bytes 6291464 | tf_op jit(solution)/shard_map/ppermute | solution.py:131
  27.3 21.5 %collective-permute-start.8 = (bf16[256,4096]{1,0:T(8,128)(2,1)S(1)}, bf16[256,4096]{1,0:T(8,128)(2,1)S(1)}, u32[]{:S(2)}, u32[]{:S(2)}) collective-permute-start(bf16[256,4096]{1,0:T(8,128)(2,1)S(1)} %collective-permute-done.3.refs_0_), channel_id=1, source_target_pairs={{0,4},{8,12},{1,5},{9,13},{2,6},{10,14},{3,7},{11,15},{16,20},{24,... | collective-permute-start | bytes 6291464 | tf_op jit(solution)/shard_map/ppermute | solution.py:133
  31.8 6.3 %collective-permute-start.4 = (f32[64,256]{1,0:T(8,128)S(1)}, f32[64,256]{1,0:T(8,128)S(1)}, u32[]{:S(2)}, u32[]{:S(2)}) collective-permute-start(f32[64,256]{1,0:T(8,128)S(1)} %get-tuple-element.29), channel_id=1, source_target_pairs={{0,1},{1,0},{2,3},{3,2},{4,5},{5,4},{6,7},{7,6},{8,9},{9,8},{10,11... | collective-permute-start | bytes 196616 | tf_op jit(solution)/shard_map/ppermute | solution.py:125
  35.2 6.2 %collective-permute-start.5 = (f32[64,256]{1,0:T(8,128)S(1)}, f32[64,256]{1,0:T(8,128)S(1)}, u32[]{:S(2)}, u32[]{:S(2)}) collective-permute-start(f32[64,256]{1,0:T(8,128)S(1)} %get-tuple-element.30), channel_id=1, source_target_pairs={{0,3},{1,2},{2,1},{3,0},{4,7},{5,6},{6,5},{7,4},{8,11},{9,10},{10,... | collective-permute-start | bytes 196616 | tf_op jit(solution)/shard_map/ppermute | solution.py:125
  38.1 5.3 %collective-permute-start.6 = (f32[64,256]{1,0:T(8,128)S(1)}, f32[64,256]{1,0:T(8,128)S(1)}, u32[]{:S(2)}, u32[]{:S(2)}) collective-permute-start(f32[64,256]{1,0:T(8,128)S(1)} %get-tuple-element.31), channel_id=1, source_target_pairs={{0,2},{1,3},{2,0},{3,1},{4,6},{5,7},{6,4},{7,5},{8,10},{9,11},{10,... | collective-permute-start | bytes 196616 | tf_op jit(solution)/shard_map/ppermute | solution.py:125
  50.1 6.4 %collective-permute-start.10 = (bf16[64,256]{1,0:T(8,128)(2,1)S(1)}, bf16[64,256]{1,0:T(8,128)(2,1)S(1)}, u32[]{:S(2)}, u32[]{:S(2)}) collective-permute-start(bf16[64,256]{1,0:T(8,128)(2,1)S(1)} %get-tuple-element.37), channel_id=1, source_target_pairs={{0,3},{1,2},{2,1},{3,0},{4,7},{5,6},{6,5},{7,4},{8,11},{9,10},{10,... | collective-permute-start | bytes 98312 | tf_op jit(solution)/shard_map/ppermute | solution.py:125
  54.6 4.8 %collective-permute-start.11 = (bf16[64,256]{1,0:T(8,128)(2,1)S(1)}, bf16[64,256]{1,0:T(8,128)(2,1)S(1)}, u32[]{:S(2)}, u32[]{:S(2)}) collective-permute-start(bf16[64,256]{1,0:T(8,128)(2,1)S(1)} %get-tuple-element.38), channel_id=1, source_target_pairs={{0,2},{1,3},{2,0},{3,1},{4,6},{5,7},{6,4},{7,5},{8,10},{9,11},{10,... | collective-permute-start | bytes 98312 | tf_op jit(solution)/shard_map/ppermute | solution.py:125
  54.6 4.8 %collective-permute-start.9 = (bf16[64,256]{1,0:T(8,128)(2,1)S(1)}, bf16[64,256]{1,0:T(8,128)(2,1)S(1)}, u32[]{:S(2)}, u32[]{:S(2)}) collective-permute-start(bf16[64,256]{1,0:T(8,128)(2,1)S(1)} %get-tuple-element.36), channel_id=1, source_target_pairs={{0,1},{1,0},{2,3},{3,2},{4,5},{5,4},{6,7},{7,6},{8,9},{9,8},{10,11... | collective-permute-start | bytes 98312 | tf_op jit(solution)/shard_map/ppermute | solution.py:125

commit v5 on v4

v5 whole, which is shorter than its diff:
```python
import functools

import jax
import jax.numpy as jnp
from jax import lax
from jax.experimental import pallas as pl
from jax.experimental.pallas import tpu as pltpu
from jax.sharding import PartitionSpec as P

STEPS = 3
PART = 1024
EXTRA = 8
F32, BF16 = jnp.float32, jnp.bfloat16
VMEM = pl.BlockSpec(memory_space=pltpu.VMEM)
SMEM = pl.BlockSpec(memory_space=pltpu.SMEM)


def after(x, *earlier):
    return lax.optimization_barrier((x,) + earlier)[0]


def dot(x, y, contract):
    return lax.dot_general(x, y, (contract, ((), ())), preferred_element_type=F32)


def added(refs):
    total = refs[0][...].astype(F32)
    for ref in refs[1:]:
        total = total + ref[...].astype(F32)
    return total


def choose(column, p):
    hot = one_hot(column, p.shape[0])
    total = None
    for _ in range(3):
        term = p.astype(BF16)
        p = p - term.astype(F32)
        part = dot(hot, term, ((1,), (0,)))
        total = part if total is None else total + part
    return total


def weights_of(eig_ref, columns):
    return 1.0 / (eig_ref[:, columns] + 0.05)


def one_hot(column, length):
    shape = (column.shape[0], length)
    return (lax.broadcasted_iota(jnp.int32, shape, 1) == column).astype(F32).astype(BF16)


def scores_kernel(steps, first, layers, me_ref, *refs):
    x_refs, refs = [], refs
    for _, n in steps:
        x_refs.append(refs[:n])
        refs = refs[n:]
    (t_ref, eig_ref, order_ref), refs = refs[:3], refs[3:]
    outs, acc = refs[:layers], refs[layers]
    p, squares = [None] * len(steps), None
    for c in range(0, t_ref.shape[1], PART):
        columns = slice(c, c + PART)
        weights = weights_of(eig_ref, columns)
        t = t_ref[:, columns]
        for i, group in enumerate(x_refs):
            x = (added([ref.at[:, columns] for ref in group]) * weights).astype(BF16)
            part = dot(x, t, ((1,), (1,)))
            p[i] = part if p[i] is None else p[i] + part
        if first:
            tf = t.astype(F32)
            square = tf * tf * weights
            for k in range(0, PART, 128):
                part = square[:, k : k + 128]
                squares = part if squares is None else squares + part
    own = acc.shape[0] // layers
    for i, (step, _) in enumerate(steps):
        acc[...] = choose(order_ref[:, step : step + 1], p[i])
        for by in range(layers):
            start = pl.multiple_of((me_ref[0] ^ by) * own, own)
            outs[by][i * own : (i + 1) * own] = acc[pl.ds(start, own)].astype(outs[by].dtype)
    if first:
        extra = jnp.broadcast_to(jnp.sum(squares.T, axis=0, keepdims=True), (EXTRA, acc.shape[1]))
        for by in range(layers):
            outs[by][len(steps) * own :] = extra


def scores_call(steps, first, layers, me, xs, t, eig, order, sent):
    rows, depth = t.shape
    queries = xs[0].shape[0]
    share = len(steps) * (queries // layers) + (EXTRA if first else 0)
    return pl.pallas_call(
        functools.partial(scores_kernel, steps, first, layers),
        in_specs=[SMEM] + [VMEM] * (len(xs) + 3),
        out_specs=[VMEM] * layers,
        scratch_shapes=[pltpu.VMEM((queries, rows), F32)],
        out_shape=[jax.ShapeDtypeStruct((share, rows), F32 if by == 0 else sent) for by in range(layers)],
        compiler_params=pltpu.CompilerParams(vmem_limit_bytes=12 << 20),
        cost_estimate=pl.CostEstimate(
            flops=2 * len(steps) * queries * rows * depth, bytes_accessed=4 * queries * depth, transcendentals=0
        ),
        name="scores_" + "_".join(str(step) for step, _ in steps),
    )(me, *xs, t, eig, order)


def ordered_kernel(step, layers, me_ref, q_ref, eig_ref, order_ref, *refs):
    outs, hot = refs[:layers], refs[layers]
    queries = q_ref.shape[0]
    own = queries // layers
    for by in range(layers):
        start = pl.multiple_of((me_ref[0] ^ by) * own, own)
        hot[by * own : (by + 1) * own] = one_hot(order_ref[pl.ds(start, own), step : step + 1], queries)
    for c in range(0, q_ref.shape[1], PART):
        columns = slice(c, c + PART)
        x = (q_ref[:, columns].astype(F32) * weights_of(eig_ref, columns)).astype(BF16)
        x = dot(hot[...], x, ((1,), (0,))).astype(BF16)
        for by in range(layers):
            outs[by][:, columns] = x[by * own : (by + 1) * own]


def ordered_call(step, layers, me, q, eig, order):
    queries, depth = q.shape
    return pl.pallas_call(
        functools.partial(ordered_kernel, step, layers),
        in_specs=[SMEM] + [VMEM] * 3,
        out_specs=[VMEM] * layers,
        scratch_shapes=[pltpu.VMEM((queries, queries), BF16)],
        out_shape=[jax.ShapeDtypeStruct((queries // layers, depth), BF16)] * layers,
        compiler_params=pltpu.CompilerParams(vmem_limit_bytes=16 << 20),
        cost_estimate=pl.CostEstimate(
            flops=2 * queries * queries * depth, bytes_accessed=4 * queries * depth, transcendentals=0
        ),
        name="ordered",
    )(me, q, eig, order)


def product_kernel(x_ref, t_ref, out_ref):
    out_ref[...] = dot(x_ref[...], t_ref[...], ((1,), (1,))).astype(out_ref.dtype)


def product_call(x, t, dtype):
    (own, depth), rows = x.shape, t.shape[0]
    return pl.pallas_call(
        product_kernel,
        in_specs=[VMEM] * 2,
        out_specs=VMEM,
        out_shape=jax.ShapeDtypeStruct((own, rows), dtype),
        compiler_params=pltpu.CompilerParams(vmem_limit_bytes=8 << 20),
        cost_estimate=pl.CostEstimate(flops=2 * own * rows * depth, bytes_accessed=2 * rows * depth, transcendentals=0),
        name="product",
    )(x, t)


def base_kernel(layers, *refs):
    ins, (out_ref, rest_ref, inverse_ref) = refs[:-3], refs[-3:]
    own = out_ref.shape[1]
    first, second = added(ins[:layers]), added(ins[layers:])
    inverse = 1.0 / jnp.sqrt(first[own : own + 1])
    inverse_ref[...] = inverse
    out_ref[0] = first[:own] * inverse
    out_ref[1] = second[:own] * inverse
    out_ref[2] = jnp.zeros_like(out_ref[2])
    rest_ref[...] = second[own:]


def base_call(layers, own, sums0, sums1):
    rows = sums1[0].shape[1]
    return pl.pallas_call(
        functools.partial(base_kernel, layers),
        out_shape=[
            jax.ShapeDtypeStruct((STEPS, own, rows), F32),
            jax.ShapeDtypeStruct((own, rows), F32),
            jax.ShapeDtypeStruct((1, rows), F32),
        ],
        compiler_params=pltpu.CompilerParams(vmem_limit_bytes=4 << 20),
        name="base",
    )(*sums0, *sums1)


def per_device(train_grads, query_grads, eigenvalues, order):
    rows, queries = train_grads.shape[0], query_grads.shape[0]
    layers, blks = lax.axis_size("layer"), lax.axis_size("blk")
    me = lax.axis_index("layer").astype(jnp.int32).reshape(1)
    t = train_grads.reshape(rows, -1)
    q = query_grads.reshape(queries, -1)
    columns = order.T
    evens = range(0, blks, 2)
    even_on = [(i, (i + 2) % blks) for i in evens]

    def exchange(pieces):
        bys = [1, *range(layers - 1, 1, -1)]
        got = [lax.ppermute(pieces[by], "layer", [(i, i ^ by) for i in range(layers)]) for by in bys]
        return [pieces[0]] + got

    odd_two = lax.ppermute(q, "blk", [(i + 1, (i + 3) % blks) for i in evens])
    odd_one = lax.ppermute(q, "blk", [(i, i + 1) for i in evens])
    pieces = scores_call(((0, 1),), True, layers, me, [q], t, eigenvalues, columns, F32)
    sums0 = exchange(pieces)

    ordered = ordered_call(2, layers, me, after(q, *pieces), eigenvalues, columns)
    bys = [*range(layers - 1, 0, -1), 0]
    parts = [ordered[by] for by in bys]
    parts[0], parts[1] = lax.optimization_barrier((parts[0], parts[1], *sums0))[:2]
    odd_two = after(odd_two, parts[0], parts[1])
    parts[2] = after(parts[2], odd_two)

    even_one = lax.ppermute(odd_two, "blk", [(i + 1, i) for i in evens])
    xs = [odd_one, even_one, odd_two]
    pieces = scores_call(((1, 2), (2, 1)), False, layers, me, xs, t, eigenvalues, columns, BF16)
    parts[3:] = lax.optimization_barrier((*parts[3:], *pieces))[: layers - 3]
    sums1 = exchange(pieces)
    base, total, inverse = base_call(layers, queries // layers, sums0, sums1)

    got = [lax.ppermute(part, "blk", even_on) for part in parts]
    for by, part in zip(bys[:-1], got):
        mine = product_call(part, t, BF16)
        total = total + lax.ppermute(mine, "layer", [(i, i ^ by) for i in range(layers)]).astype(F32)
    total = total + product_call(got[-1], t, F32)
    return lax.dynamic_update_slice(base, (total * inverse)[None], (STEPS - 1, 0, 0))


def solution(mesh):
    return jax.shard_map(
        per_device,
        mesh=mesh,
        in_specs=(
            P(("groups", "blk"), "layer", None),
            P(("groups", "blk"), "layer", None),
            P("layer", None),
            P("groups", None),
        ),
        out_specs=P(None, "layer", ("groups", "blk")),
        check_vma=False,
    )
```

time: 60.4 us -> 56.3 us (0.932)
  waiting for transfers between devices: 26.4 us -> 5.63 us
  starting transfers between devices: 23.4 us -> 35.3 us
  Pallas kernels: 4.79 us -> 11 us
  local copies, waits for them, and re-layouts: 4.71 us -> 3.13 us
    ppermute x3 -> x10, starting transfers between devices: 6.72 us -> 23.3 us  [the longest x4 13.1 us: per_device(): got = [lax.ppermute(part, 'blk', even_on) for part in parts]]
    ppermute x9 -> x6, waiting for transfers between devices: 17.3 us -> 2.22 us  [exchange(): lax.ppermute(pieces[by], 'layer', [(i, i ^ by) for i in range(layers)])]
    pallas_call x3 -> x7, Pallas kernels: 4.08 us -> 10.2 us  [the longest x2 4.81 us: scores_call(): pl.pallas_call(functools.partial(scores_kernel, steps, first, layers), in...]
    ppermute x3 -> x10, waiting for transfers between devices: 9.12 us -> 3.4 us  [the longest x1 2.43 us: per_device(): even_one = lax.ppermute(odd_two, 'blk', [(i + 1, i) for i in evens])]
    ppermute x9 -> x6, starting transfers between devices: 16.7 us -> 11.9 us  [exchange(): lax.ppermute(pieces[by], 'layer', [(i, i ^ by) for i in range(layers)])]
    unnamed x11 -> x9, local copies, waits for them, and re-layouts: 4.71 us -> 3.13 us
  transfers between devices with their start and end apart: 12 -> 16, of which waited for: 8 -> 4; matrix products, arithmetic and copies ran while one was open for 1% -> 1% of each run, Pallas kernels for 6% -> 20%
where the time goes in v5:
time: 56.3 us; the launch traced here: 55.8 us
  starting transfers between devices  35.3 us (63%)
  Pallas kernels  11 us (20%)
  waiting for transfers between devices  5.63 us (10%)
  local copies, waits for them, and re-layouts  3.13 us (6%)
  other arithmetic  0.65 us (1%)
    ppermute x4, starting transfers between devices, per_device(): got = [lax.ppermute(part, 'blk', even_on) for part in parts]  13.1 us
    ppermute x6, starting transfers between devices, exchange(): lax.ppermute(pieces[by], 'layer', [(i, i ^ by) for i in range(layers)])  11.9 us
    pallas_call x2, Pallas kernels, scores_call(): pl.pallas_call(functools.partial(scores_kernel, steps, first, layers), in...  4.81 us
    ppermute x3, starting transfers between devices, per_device(): lax.ppermute(mine, 'layer', [(i, i ^ by) for i in range(layers)])  4.52 us
    ppermute x1, starting transfers between devices, per_device(): odd_one = lax.ppermute(q, 'blk', [(i, i + 1) for i in evens])  3.63 us
    unnamed x9, local copies, waits for them, and re-layouts  3.13 us
    pallas_call x4, Pallas kernels, product_call(): pl.pallas_call(product_kernel, in_specs=[VMEM] * 2, out_specs=VMEM, out_s...  3.05 us
    ppermute x1, waiting for transfers between devices, per_device(): even_one = lax.ppermute(odd_two, 'blk', [(i + 1, i) for i in evens])  2.43 us
  transfers between devices with their start and end apart: 16, of which 4 were waited for; matrix products, arithmetic and copies ran while one was open for 1% of the time, Pallas kernels for 20%

profile of v5, /device:TPU:0, one launch (start us, length us, event | category | flops | bytes accessed | tf_op | source)
XLA Modules:
  0.0 55.8 jit_solution(13793035775459661555)
XLA Ops:
  0.0 0.8 %collective-permute-start.4 = (bf16[256,4096]{1,0:T(8,128)(2,1)}, bf16[256,4096]{1,0:T(8,128)(2,1)S(1)}, u32[]{:S(2)}, u32[]{:S(2)}) collective-permute-start(bf16[256,4096]{1,0:T(8,128)(2,1)} %bitcast.1.refs_0_.q_ref), channel_id=1, source_target_pairs={{4,12},{12,4},{5,13},{13,5},{6,14},{14,6},{7,15},{15,7},{20,28},{2... | collective-permute-start | bytes 6291464 | tf_op jit(solution)/shard_map/ppermute | solution.py:194
  0.8 0.8 %copy.5 = s32[3,256]{0,1:T(8,128)S(1)} copy(s32[3,256]{1,0:T(4,128)} %param.7) | data formatting | bytes 6144 | tf_op args[3]
  1.6 1.6 %copy-done = bf16[256,1,4096]{2,0,1:T(8,128)(2,1)S(1)} copy-done((bf16[256,1,4096]{2,0,1:T(8,128)(2,1)S(1)}, bf16[256,1,4096]{2,0,1:T(8,128)(2,1)}, u32[]{:S(2)}) %copy-start) | copy-done | bytes 2097176
  3.9 3.1 %scores_0.1 = (f32[72,256]{1,0:T(8,128)S(1)}, f32[72,256]{1,0:T(8,128)S(1)}, f32[72,256]{1,0:T(8,128)S(1)}, f32[72,256]{1,0:T(8,128)S(1)}) custom-call(s32[1]{0:T(128)} %bitcast.me_ref, bf16[256,4096]{1,0:T(8,128)(2,1)} %bitcast.1.refs_0_.q_ref, bf16[256,4096]{1,0:T(8,128)(2,1)S(1)} %bitcast.7, f32[1,4096]{1,0:T(1,128)S(1)} %copy-done.2, s32[256,3]{1,0:T(8,128)S(1)} %bitcast.13), custom_call_target="tpu_custom_call" | custom-call | flops 536870912 | bytes 4194304 | tf_op jit(solution)/shard_map/scores_0/pallas_call | solution.py:91
  7.1 3.1 %collective-permute-start = (f32[72,256]{1,0:T(8,128)S(1)}, f32[72,256]{1,0:T(8,128)S(1)}, u32[]{:S(2)}, u32[]{:S(2)}) collective-permute-start(f32[72,256]{1,0:T(8,128)S(1)} %get-tuple-element.27), channel_id=1, source_target_pairs={{0,1},{1,0},{2,3},{3,2},{4,5},{5,4},{6,7},{7,6},{8,9},{9,8},{10,11... | collective-permute-start | bytes 221192 | tf_op jit(solution)/shard_map/ppermute | solution.py:191
  10.2 2.5 %collective-permute-start.1 = (f32[72,256]{1,0:T(8,128)S(1)}, f32[72,256]{1,0:T(8,128)S(1)}, u32[]{:S(2)}, u32[]{:S(2)}) collective-permute-start(f32[72,256]{1,0:T(8,128)S(1)} %get-tuple-element.28), channel_id=1, source_target_pairs={{0,3},{1,2},{2,1},{3,0},{4,7},{5,6},{6,5},{7,4},{8,11},{9,10},{10,... | collective-permute-start | bytes 221192 | tf_op jit(solution)/shard_map/ppermute | solution.py:191
  12.8 3.6 %collective-permute-start.3 = (bf16[256,4096]{1,0:T(8,128)(2,1)}, bf16[256,4096]{1,0:T(8,128)(2,1)S(1)}, u32[]{:S(2)}, u32[]{:S(2)}) collective-permute-start(bf16[256,4096]{1,0:T(8,128)(2,1)} %bitcast.1.refs_0_.q_ref), channel_id=1, source_target_pairs={{0,4},{8,12},{1,5},{9,13},{2,6},{10,14},{3,7},{11,15},{16,20},{24,... | collective-permute-start | bytes 6291464 | tf_op jit(solution)/shard_map/ppermute | solution.py:195
  16.4 2.4 %ordered.1 = (bf16[64,4096]{1,0:T(8,128)(2,1)S(1)}, bf16[64,4096]{1,0:T(8,128)(2,1)S(1)}, bf16[64,4096]{1,0:T(8,128)(2,1)S(1)}, bf16[64,4096]{1,0:T(8,128)(2,1)S(1)}) custom-call(s32[1]{0:T(128)} %bitcast.me_ref, bf16[256,4096]{1,0:T(8,128)(2,1)} %bitcast.1.refs_0_.q_ref, f32[1,4096]{1,0:T(1,128)S(1)} %copy-done.3, s32[256,3]{1,0:T(8,128)S(1)} %bitcast.14), custom_call_target="tpu_custom_call" | custom-call | flops 536870912 | bytes 4194304 | tf_op jit(solution)/shard_map/ordered/pallas_call | solution.py:122
  18.8 2.2 %collective-permute-done.2.refs_3_ = f32[72,256]{1,0:T(8,128)S(1)} collective-permute-done((f32[72,256]{1,0:T(8,128)S(1)}, f32[72,256]{1,0:T(8,128)S(1)}, u32[]{:S(2)}, u32[]{:S(2)}) %collective-permute-start.2) | collective-permute-done | bytes 73760 | tf_op jit(solution)/shard_map/ppermute | solution.py:191
  21.0 1.3 %collective-permute-start.5 = (bf16[256,4096]{1,0:T(8,128)(2,1)S(1)}, bf16[256,4096]{1,0:T(8,128)(2,1)S(1)}, u32[]{:S(2)}, u32[]{:S(2)}) collective-permute-start(bf16[256,4096]{1,0:T(8,128)(2,1)S(1)} %collective-permute-done.4.refs_2_), channel_id=1, source_target_pairs={{4,0},{12,8},{5,1},{13,9},{6,2},{14,10},{7,3},{15,11},{20,16},{28,... | collective-permute-start | bytes 6291464 | tf_op jit(solution)/shard_map/ppermute | solution.py:206
  22.3 3.0 %collective-permute-start.9 = (bf16[64,4096]{1,0:T(8,128)(2,1)S(1)}, bf16[64,4096]{1,0:T(8,128)(2,1)S(1)}, u32[]{:S(2)}, u32[]{:S(2)}) collective-permute-start(bf16[64,4096]{1,0:T(8,128)(2,1)S(1)} %get-tuple-element.33), channel_id=1, source_target_pairs={{0,8},{8,0},{1,9},{9,1},{2,10},{10,2},{3,11},{11,3},{16,24},{24,16... | collective-permute-start | bytes 1572872 | tf_op jit(solution)/shard_map/ppermute | solution.py:213
  25.3 2.8 %collective-permute-start.11 = (bf16[64,4096]{1,0:T(8,128)(2,1)S(1)}, bf16[64,4096]{1,0:T(8,128)(2,1)S(1)}, u32[]{:S(2)}, u32[]{:S(2)}) collective-permute-start(bf16[64,4096]{1,0:T(8,128)(2,1)S(1)} %get-tuple-element.34), channel_id=1, source_target_pairs={{0,8},{8,0},{1,9},{9,1},{2,10},{10,2},{3,11},{11,3},{16,24},{24,16... | collective-permute-start | bytes 1572872 | tf_op jit(solution)/shard_map/ppermute | solution.py:213
  28.2 3.0 %collective-permute-start.13 = (bf16[64,4096]{1,0:T(8,128)(2,1)S(1)}, bf16[64,4096]{1,0:T(8,128)(2,1)S(1)}, u32[]{:S(2)}, u32[]{:S(2)}) collective-permute-start(bf16[64,4096]{1,0:T(8,128)(2,1)S(1)} %get-tuple-element.43), channel_id=1, source_target_pairs={{0,8},{8,0},{1,9},{9,1},{2,10},{10,2},{3,11},{11,3},{16,24},{24,16... | collective-permute-start | bytes 1572872 | tf_op jit(solution)/shard_map/ppermute | solution.py:213
  31.2 2.4 %collective-permute-done.5.refs_1_ = bf16[256,4096]{1,0:T(8,128)(2,1)S(1)} collective-permute-done((bf16[256,4096]{1,0:T(8,128)(2,1)S(1)}, bf16[256,4096]{1,0:T(8,128)(2,1)S(1)}, u32[]{:S(2)}, u32[]{:S(2)}) %collective-permute-start.5) | collective-permute-done | bytes 2097184 | tf_op jit(solution)/shard_map/ppermute | solution.py:206
  33.6 1.7 %scores_1_2.1 = (f32[128,256]{1,0:T(8,128)S(1)}, bf16[128,256]{1,0:T(8,128)(2,1)S(1)}, bf16[128,256]{1,0:T(8,128)(2,1)S(1)}, bf16[128,256]{1,0:T(8,128)(2,1)S(1)}) custom-call(s32[1]{0:T(128)} %bitcast.me_ref, bf16[256,4096]{1,0:T(8,128)(2,1)S(1)} %collective-permute-done.3.refs_0_, bf16[256,4096]{1,0:T(8,128)(2,1)S(1)} %collective-permute-done.5.refs_1_, ...), custom_call_target="tpu_custom_call" | custom-call | flops 1073741824 | bytes 4194304 | tf_op jit(solution)/shard_map/scores_1_2/pallas_call | solution.py:91
  35.3 4.3 %collective-permute-start.15 = (bf16[64,4096]{1,0:T(8,128)(2,1)S(1)}, bf16[64,4096]{1,0:T(8,128)(2,1)S(1)}, u32[]{:S(2)}, u32[]{:S(2)}) collective-permute-start(bf16[64,4096]{1,0:T(8,128)(2,1)S(1)} %get-tuple-element.45), channel_id=1, source_target_pairs={{0,8},{8,0},{1,9},{9,1},{2,10},{10,2},{3,11},{11,3},{16,24},{24,16... | collective-permute-start | bytes 1572872 | tf_op jit(solution)/shard_map/ppermute | solution.py:213
  39.6 3.1 %collective-permute-start.6 = (bf16[128,256]{1,0:T(8,128)(2,1)S(1)}, bf16[128,256]{1,0:T(8,128)(2,1)S(1)}, u32[]{:S(2)}, u32[]{:S(2)}) collective-permute-start(bf16[128,256]{1,0:T(8,128)(2,1)S(1)} %get-tuple-element.37), channel_id=1, source_target_pairs={{0,1},{1,0},{2,3},{3,2},{4,5},{5,4},{6,7},{7,6},{8,9},{9,8},{10,11... | collective-permute-start | bytes 196616 | tf_op jit(solution)/shard_map/ppermute | solution.py:191
  42.8 3.1 %collective-permute-start.7 = (bf16[128,256]{1,0:T(8,128)(2,1)S(1)}, bf16[128,256]{1,0:T(8,128)(2,1)S(1)}, u32[]{:S(2)}, u32[]{:S(2)}) collective-permute-start(bf16[128,256]{1,0:T(8,128)(2,1)S(1)} %get-tuple-element.38), channel_id=1, source_target_pairs={{0,3},{1,2},{2,1},{3,0},{4,7},{5,6},{6,5},{7,4},{8,11},{9,10},{10,... | collective-permute-start | bytes 196616 | tf_op jit(solution)/shard_map/ppermute | solution.py:191
  45.9 0.8 %product.4 = bf16[64,256]{1,0:T(8,128)(2,1)S(1)} custom-call(bf16[64,4096]{1,0:T(8,128)(2,1)S(1)} %collective-permute-done.9.x_ref, bf16[256,4096]{1,0:T(8,128)(2,1)S(1)} %bitcast.9), custom_call_target="tpu_custom_call" | custom-call | flops 134217728 | bytes 2097152 | tf_op jit(solution)/shard_map/product/pallas_call | solution.py:142
  46.6 0.8 %product.5 = bf16[64,256]{1,0:T(8,128)(2,1)S(1)} custom-call(bf16[64,4096]{1,0:T(8,128)(2,1)S(1)} %collective-permute-done.11.x_ref, bf16[256,4096]{1,0:T(8,128)(2,1)S(1)} %bitcast.10), custom_call_target="tpu_custom_call" | custom-call | flops 134217728 | bytes 2097152 | tf_op jit(solution)/shard_map/product/pallas_call | solution.py:142
  47.4 1.7 %collective-permute-start.10 = (bf16[64,256]{1,0:T(8,128)(2,1)S(1)}, bf16[64,256]{1,0:T(8,128)(2,1)S(1)}, u32[]{:S(2)}, u32[]{:S(2)}) collective-permute-start(bf16[64,256]{1,0:T(8,128)(2,1)S(1)} %product.4), channel_id=1, source_target_pairs={{0,3},{1,2},{2,1},{3,0},{4,7},{5,6},{6,5},{7,4},{8,11},{9,10},{10,... | collective-permute-start | bytes 98312 | tf_op jit(solution)/shard_map/ppermute | solution.py:216
  49.9 1.4 %collective-permute-start.12 = (bf16[64,256]{1,0:T(8,128)(2,1)S(1)}, bf16[64,256]{1,0:T(8,128)(2,1)S(1)}, u32[]{:S(2)}, u32[]{:S(2)}) collective-permute-start(bf16[64,256]{1,0:T(8,128)(2,1)S(1)} %product.5), channel_id=1, source_target_pairs={{0,2},{1,3},{2,0},{3,1},{4,6},{5,7},{6,4},{7,5},{8,10},{9,11},{10,... | collective-permute-start | bytes 98312 | tf_op jit(solution)/shard_map/ppermute | solution.py:216
  51.3 1.5 %collective-permute-start.14 = (bf16[64,256]{1,0:T(8,128)(2,1)S(1)}, bf16[64,256]{1,0:T(8,128)(2,1)S(1)}, u32[]{:S(2)}, u32[]{:S(2)}) collective-permute-start(bf16[64,256]{1,0:T(8,128)(2,1)S(1)} %product.6), channel_id=1, source_target_pairs={{0,1},{1,0},{2,3},{3,2},{4,5},{5,4},{6,7},{7,6},{8,9},{9,8},{10,11... | collective-permute-start | bytes 98312 | tf_op jit(solution)/shard_map/ppermute | solution.py:216
  53.4 0.8 %product.7 = f32[64,256]{1,0:T(8,128)S(1)} custom-call(bf16[64,4096]{1,0:T(8,128)(2,1)S(1)} %collective-permute-done.15.x_ref, bf16[256,4096]{1,0:T(8,128)(2,1)S(1)} %bitcast.12), custom_call_target="tpu_custom_call" | custom-call | flops 134217728 | bytes 2097152 | tf_op jit(solution)/shard_map/product/pallas_call | solution.py:142
  (26 shorter events, 4.0 us)
Async XLA Ops:
  0.0 21.0 %collective-permute-start.4 = (bf16[256,4096]{1,0:T(8,128)(2,1)}, bf16[256,4096]{1,0:T(8,128)(2,1)S(1)}, u32[]{:S(2)}, u32[]{:S(2)}) collective-permute-start(bf16[256,4096]{1,0:T(8,128)(2,1)} %bitcast.1.refs_0_.q_ref), channel_id=1, source_target_pairs={{4,12},{12,4},{5,13},{13,5},{6,14},{14,6},{7,15},{15,7},{20,28},{2... | collective-permute-start | bytes 6291464 | tf_op jit(solution)/shard_map/ppermute | solution.py:194
  1.6 1.6 %copy-start = (bf16[256,1,4096]{2,0,1:T(8,128)(2,1)S(1)}, bf16[256,1,4096]{2,0,1:T(8,128)(2,1)}, u32[]{:S(2)}) copy-start(bf16[256,1,4096]{2,0,1:T(8,128)(2,1)} %param.4) | copy-start | bytes 6291460
  3.2 0.7 %copy-start.2 = (f32[1,4096]{1,0:T(1,128)S(1)}, f32[1,4096]{1,0:T(1,128)}, u32[]{:S(2)}) copy-start(f32[1,4096]{1,0:T(1,128)} %refs_4_.1) | copy-start | bytes 49156
  3.9 12.5 %copy-start.3 = (f32[1,4096]{1,0:T(1,128)S(1)}, f32[1,4096]{1,0:T(1,128)}, u32[]{:S(2)}) copy-start(f32[1,4096]{1,0:T(1,128)} %refs_4_.1) | copy-start | bytes 49156
  7.1 26.6 %copy-start.1 = (bf16[256,1,4096]{2,0,1:T(8,128)(2,1)S(1)}, bf16[256,1,4096]{2,0,1:T(8,128)(2,1)}, u32[]{:S(2)}) copy-start(bf16[256,1,4096]{2,0,1:T(8,128)(2,1)} %param.4) | copy-start | bytes 6291460
  7.1 11.7 %collective-permute-start = (f32[72,256]{1,0:T(8,128)S(1)}, f32[72,256]{1,0:T(8,128)S(1)}, u32[]{:S(2)}, u32[]{:S(2)}) collective-permute-start(f32[72,256]{1,0:T(8,128)S(1)} %get-tuple-element.27), channel_id=1, source_target_pairs={{0,1},{1,0},{2,3},{3,2},{4,5},{5,4},{6,7},{7,6},{8,9},{9,8},{10,11... | collective-permute-start | bytes 221192 | tf_op jit(solution)/shard_map/ppermute | solution.py:191
  10.2 8.6 %collective-permute-start.1 = (f32[72,256]{1,0:T(8,128)S(1)}, f32[72,256]{1,0:T(8,128)S(1)}, u32[]{:S(2)}, u32[]{:S(2)}) collective-permute-start(f32[72,256]{1,0:T(8,128)S(1)} %get-tuple-element.28), channel_id=1, source_target_pairs={{0,3},{1,2},{2,1},{3,0},{4,7},{5,6},{6,5},{7,4},{8,11},{9,10},{10,... | collective-permute-start | bytes 221192 | tf_op jit(solution)/shard_map/ppermute | solution.py:191
  12.6 8.4 %collective-permute-start.2 = (f32[72,256]{1,0:T(8,128)S(1)}, f32[72,256]{1,0:T(8,128)S(1)}, u32[]{:S(2)}, u32[]{:S(2)}) collective-permute-start(f32[72,256]{1,0:T(8,128)S(1)} %get-tuple-element.29), channel_id=1, source_target_pairs={{0,2},{1,3},{2,0},{3,1},{4,6},{5,7},{6,4},{7,5},{8,10},{9,11},{10,... | collective-permute-start | bytes 221192 | tf_op jit(solution)/shard_map/ppermute | solution.py:191
  12.8 18.4 %collective-permute-start.3 = (bf16[256,4096]{1,0:T(8,128)(2,1)}, bf16[256,4096]{1,0:T(8,128)(2,1)S(1)}, u32[]{:S(2)}, u32[]{:S(2)}) collective-permute-start(bf16[256,4096]{1,0:T(8,128)(2,1)} %bitcast.1.refs_0_.q_ref), channel_id=1, source_target_pairs={{0,4},{8,12},{1,5},{9,13},{2,6},{10,14},{3,7},{11,15},{16,20},{24,... | collective-permute-start | bytes 6291464 | tf_op jit(solution)/shard_map/ppermute | solution.py:195
  21.0 12.6 %collective-permute-start.5 = (bf16[256,4096]{1,0:T(8,128)(2,1)S(1)}, bf16[256,4096]{1,0:T(8,128)(2,1)S(1)}, u32[]{:S(2)}, u32[]{:S(2)}) collective-permute-start(bf16[256,4096]{1,0:T(8,128)(2,1)S(1)} %collective-permute-done.4.refs_2_), channel_id=1, source_target_pairs={{4,0},{12,8},{5,1},{13,9},{6,2},{14,10},{7,3},{15,11},{20,16},{28,... | collective-permute-start | bytes 6291464 | tf_op jit(solution)/shard_map/ppermute | solution.py:206
  22.3 20.5 %collective-permute-start.9 = (bf16[64,4096]{1,0:T(8,128)(2,1)S(1)}, bf16[64,4096]{1,0:T(8,128)(2,1)S(1)}, u32[]{:S(2)}, u32[]{:S(2)}) collective-permute-start(bf16[64,4096]{1,0:T(8,128)(2,1)S(1)} %get-tuple-element.33), channel_id=1, source_target_pairs={{0,8},{8,0},{1,9},{9,1},{2,10},{10,2},{3,11},{11,3},{16,24},{24,16... | collective-permute-start | bytes 1572872 | tf_op jit(solution)/shard_map/ppermute | solution.py:213
  25.3 20.6 %collective-permute-start.11 = (bf16[64,4096]{1,0:T(8,128)(2,1)S(1)}, bf16[64,4096]{1,0:T(8,128)(2,1)S(1)}, u32[]{:S(2)}, u32[]{:S(2)}) collective-permute-start(bf16[64,4096]{1,0:T(8,128)(2,1)S(1)} %get-tuple-element.34), channel_id=1, source_target_pairs={{0,8},{8,0},{1,9},{9,1},{2,10},{10,2},{3,11},{11,3},{16,24},{24,16... | collective-permute-start | bytes 1572872 | tf_op jit(solution)/shard_map/ppermute | solution.py:213
  28.2 19.3 %collective-permute-start.13 = (bf16[64,4096]{1,0:T(8,128)(2,1)S(1)}, bf16[64,4096]{1,0:T(8,128)(2,1)S(1)}, u32[]{:S(2)}, u32[]{:S(2)}) collective-permute-start(bf16[64,4096]{1,0:T(8,128)(2,1)S(1)} %get-tuple-element.43), channel_id=1, source_target_pairs={{0,8},{8,0},{1,9},{9,1},{2,10},{10,2},{3,11},{11,3},{16,24},{24,16... | collective-permute-start | bytes 1572872 | tf_op jit(solution)/shard_map/ppermute | solution.py:213
  35.3 18.1 %collective-permute-start.15 = (bf16[64,4096]{1,0:T(8,128)(2,1)S(1)}, bf16[64,4096]{1,0:T(8,128)(2,1)S(1)}, u32[]{:S(2)}, u32[]{:S(2)}) collective-permute-start(bf16[64,4096]{1,0:T(8,128)(2,1)S(1)} %get-tuple-element.45), channel_id=1, source_target_pairs={{0,8},{8,0},{1,9},{9,1},{2,10},{10,2},{3,11},{11,3},{16,24},{24,16... | collective-permute-start | bytes 1572872 | tf_op jit(solution)/shard_map/ppermute | solution.py:213
  39.6 10.3 %collective-permute-start.6 = (bf16[128,256]{1,0:T(8,128)(2,1)S(1)}, bf16[128,256]{1,0:T(8,128)(2,1)S(1)}, u32[]{:S(2)}, u32[]{:S(2)}) collective-permute-start(bf16[128,256]{1,0:T(8,128)(2,1)S(1)} %get-tuple-element.37), channel_id=1, source_target_pairs={{0,1},{1,0},{2,3},{3,2},{4,5},{5,4},{6,7},{7,6},{8,9},{9,8},{10,11... | collective-permute-start | bytes 196616 | tf_op jit(solution)/shard_map/ppermute | solution.py:191
  42.8 8.5 %collective-permute-start.7 = (bf16[128,256]{1,0:T(8,128)(2,1)S(1)}, bf16[128,256]{1,0:T(8,128)(2,1)S(1)}, u32[]{:S(2)}, u32[]{:S(2)}) collective-permute-start(bf16[128,256]{1,0:T(8,128)(2,1)S(1)} %get-tuple-element.38), channel_id=1, source_target_pairs={{0,3},{1,2},{2,1},{3,0},{4,7},{5,6},{6,5},{7,4},{8,11},{9,10},{10,... | collective-permute-start | bytes 196616 | tf_op jit(solution)/shard_map/ppermute | solution.py:191
  45.9 6.8 %collective-permute-start.8 = (bf16[128,256]{1,0:T(8,128)(2,1)S(1)}, bf16[128,256]{1,0:T(8,128)(2,1)S(1)}, u32[]{:S(2)}, u32[]{:S(2)}) collective-permute-start(bf16[128,256]{1,0:T(8,128)(2,1)S(1)} %get-tuple-element.39), channel_id=1, source_target_pairs={{0,2},{1,3},{2,0},{3,1},{4,6},{5,7},{6,4},{7,5},{8,10},{9,11},{10,... | collective-permute-start | bytes 196616 | tf_op jit(solution)/shard_map/ppermute | solution.py:191
  47.4 6.8 %collective-permute-start.10 = (bf16[64,256]{1,0:T(8,128)(2,1)S(1)}, bf16[64,256]{1,0:T(8,128)(2,1)S(1)}, u32[]{:S(2)}, u32[]{:S(2)}) collective-permute-start(bf16[64,256]{1,0:T(8,128)(2,1)S(1)} %product.4), channel_id=1, source_target_pairs={{0,3},{1,2},{2,1},{3,0},{4,7},{5,6},{6,5},{7,4},{8,11},{9,10},{10,... | collective-permute-start | bytes 98312 | tf_op jit(solution)/shard_map/ppermute | solution.py:216
  49.9 4.9 %collective-permute-start.12 = (bf16[64,256]{1,0:T(8,128)(2,1)S(1)}, bf16[64,256]{1,0:T(8,128)(2,1)S(1)}, u32[]{:S(2)}, u32[]{:S(2)}) collective-permute-start(bf16[64,256]{1,0:T(8,128)(2,1)S(1)} %product.5), channel_id=1, source_target_pairs={{0,2},{1,3},{2,0},{3,1},{4,6},{5,7},{6,4},{7,5},{8,10},{9,11},{10,... | collective-permute-start | bytes 98312 | tf_op jit(solution)/shard_map/ppermute | solution.py:216
  51.3 3.9 %collective-permute-start.14 = (bf16[64,256]{1,0:T(8,128)(2,1)S(1)}, bf16[64,256]{1,0:T(8,128)(2,1)S(1)}, u32[]{:S(2)}, u32[]{:S(2)}) collective-permute-start(bf16[64,256]{1,0:T(8,128)(2,1)S(1)} %product.6), channel_id=1, source_target_pairs={{0,1},{1,0},{2,3},{3,2},{4,5},{5,4},{6,7},{7,6},{8,9},{9,8},{10,11... | collective-permute-start | bytes 98312 | tf_op jit(solution)/shard_map/ppermute | solution.py:216

commit v6 on v5

--- a/solution.py
+++ b/solution.py
@@ -133,47 +133,46 @@
     )(me, q, eig, order)
 
 
-def product_kernel(x_ref, t_ref, out_ref):
-    out_ref[...] = dot(x_ref[...], t_ref[...], ((1,), (1,))).astype(out_ref.dtype)
-
-
-def product_call(x, t, dtype):
+def part_kernel(x_ref, t_ref, *refs):
+    pieces, out = refs[:-1], refs[-1]
+    own = x_ref.shape[0]
+    p = dot(x_ref[...], t_ref[...], ((1,), (1,)))
+    total = added(pieces)
+    out[:-own] = total[:-own].astype(out.dtype)
+    out[-own:] = (total[-own:] + p).astype(out.dtype)
+
+
+def part_call(x, t, pieces, dtype):
     (own, depth), rows = x.shape, t.shape[0]
     return pl.pallas_call(
-        product_kernel,
-        in_specs=[VMEM] * 2,
+        part_kernel,
+        in_specs=[VMEM] * (2 + len(pieces)),
         out_specs=VMEM,
-        out_shape=jax.ShapeDtypeStruct((own, rows), dtype),
+        out_shape=jax.ShapeDtypeStruct(pieces[0].shape, dtype),
         compiler_params=pltpu.CompilerParams(vmem_limit_bytes=8 << 20),
         cost_estimate=pl.CostEstimate(flops=2 * own * rows * depth, bytes_accessed=2 * rows * depth, transcendentals=0),
-        name="product",
-    )(x, t)
-
-
-def base_kernel(layers, *refs):
-    ins, (out_ref, rest_ref, inverse_ref) = refs[:-3], refs[-3:]
+        name="part",
+    )(x, t, *pieces)
+
+
+def base_kernel(*refs):
+    ins, (out_ref, inverse_ref) = refs[:-2], refs[-2:]
     own = out_ref.shape[1]
-    first, second = added(ins[:layers]), added(ins[layers:])
+    first = added(ins)
     inverse = 1.0 / jnp.sqrt(first[own : own + 1])
     inverse_ref[...] = inverse
     out_ref[0] = first[:own] * inverse
-    out_ref[1] = second[:own] * inverse
-    out_ref[2] = jnp.zeros_like(out_ref[2])
-    rest_ref[...] = second[own:]
-
-
-def base_call(layers, own, sums0, sums1):
-    rows = sums1[0].shape[1]
-    return pl.pallas_call(
-        functools.partial(base_kernel, layers),
-        out_shape=[
-            jax.ShapeDtypeStruct((STEPS, own, rows), F32),
-            jax.ShapeDtypeStruct((own, rows), F32),
-            jax.ShapeDtypeStruct((1, rows), F32),
-        ],
+    out_ref[1:] = jnp.zeros_like(out_ref[1:])
+
+
+def base_call(own, sums):
+    rows = sums[0].shape[1]
+    return pl.pallas_call(
+        base_kernel,
+        out_shape=[jax.ShapeDtypeStruct((STEPS, own, rows), F32), jax.ShapeDtypeStruct((1, rows), F32)],
         compiler_params=pltpu.CompilerParams(vmem_limit_bytes=4 << 20),
         name="base",
-    )(*sums0, *sums1)
+    )(*sums)
 
 
 def per_device(train_grads, query_grads, eigenvalues, order):
@@ -192,30 +191,30 @@
         return [pieces[0]] + got
 
     odd_two = lax.ppermute(q, "blk", [(i + 1, (i + 3) % blks) for i in evens])
-    odd_one = lax.ppermute(q, "blk", [(i, i + 1) for i in evens])
     pieces = scores_call(((0, 1),), True, layers, me, [q], t, eigenvalues, columns, F32)
     sums0 = exchange(pieces)
 
     ordered = ordered_call(2, layers, me, after(q, *pieces), eigenvalues, columns)
     bys = [*range(layers - 1, 0, -1), 0]
     parts = [ordered[by] for by in bys]
-    parts[0], parts[1] = lax.optimization_barrier((parts[0], parts[1], *sums0))[:2]
-    odd_two = after(odd_two, parts[0], parts[1])
-    parts[2] = after(parts[2], odd_two)
+    odd_one = lax.ppermute(after(q, sums0[1]), "blk", [(i, i + 1) for i in evens])
+    odd_two = after(odd_two, parts[0])
+    parts[1] = after(parts[1], odd_two)
+    parts[2:] = lax.optimization_barrier((*parts[2:], odd_two, *sums0))[: layers - 2]
 
     even_one = lax.ppermute(odd_two, "blk", [(i + 1, i) for i in evens])
     xs = [odd_one, even_one, odd_two]
-    pieces = scores_call(((1, 2), (2, 1)), False, layers, me, xs, t, eigenvalues, columns, BF16)
-    parts[3:] = lax.optimization_barrier((*parts[3:], *pieces))[: layers - 3]
-    sums1 = exchange(pieces)
-    base, total, inverse = base_call(layers, queries // layers, sums0, sums1)
-
-    got = [lax.ppermute(part, "blk", even_on) for part in parts]
-    for by, part in zip(bys[:-1], got):
-        mine = product_call(part, t, BF16)
-        total = total + lax.ppermute(mine, "layer", [(i, i ^ by) for i in range(layers)]).astype(F32)
-    total = total + product_call(got[-1], t, F32)
-    return lax.dynamic_update_slice(base, (total * inverse)[None], (STEPS - 1, 0, 0))
+    pieces = scores_call(((1, 2), (2, 1)), False, layers, me, xs, t, eigenvalues, columns, F32)
+    base, inverse = base_call(queries // layers, sums0)
+
+    parts = [lax.ppermute(part, "blk", even_on) for part in parts]
+    got = []
+    for by, part in zip(bys[:-1], parts):
+        mine = part_call(part, t, [pieces[by]], BF16)
+        got.append(lax.ppermute(mine, "layer", [(i, i ^ by) for i in range(layers)]))
+    total = part_call(parts[-1], t, [pieces[0], *got[:-1]], F32) + got[-1].astype(F32)
+    total = total.reshape(2, queries // layers, rows) * inverse[None]
+    return lax.dynamic_update_slice(base, total, (1, 0, 0))
 
 
 def solution(mesh):

time: 56.3 us -> 53.2 us (0.945)
  starting transfers between devices: 35.3 us -> 30.7 us
  waiting for transfers between devices: 5.63 us -> 7.1 us
    ppermute x6 -> x3, starting transfers between devices: 11.9 us -> 6.76 us  [exchange(): lax.ppermute(pieces[by], 'layer', [(i, i ^ by) for i in range(layers)])]
    ppermute x5, waiting for transfers between devices: 0.01 us -> 4.75 us  [the longest x4 4.75 us: per_device(): parts = [lax.ppermute(part, 'blk', even_on) for part in parts]]
    ppermute x1, waiting for transfers between devices: 2.43 us -> 0.01 us  [per_device(): even_one = lax.ppermute(odd_two, 'blk', [(i + 1, i) for i in evens])]
    ppermute x3, starting transfers between devices: 4.52 us -> 6.69 us  [per_device(): lax.ppermute(mine, 'layer', [(i, i ^ by) for i in range(layers)])]
    ppermute x5, starting transfers between devices: 16.8 us -> 15.2 us  [the longest x4 11.7 us: per_device(): parts = [lax.ppermute(part, 'blk', even_on) for part in parts]]
    ppermute x3, waiting for transfers between devices: 0.96 us -> 0.01 us  [per_device(): lax.ppermute(mine, 'layer', [(i, i ^ by) for i in range(layers)])]
    ppermute x6 -> x3, waiting for transfers between devices: 2.22 us -> 2.34 us  [exchange(): lax.ppermute(pieces[by], 'layer', [(i, i ^ by) for i in range(layers)])]
  transfers between devices with their start and end apart: 16 -> 13, of which waited for: 4 -> 3; matrix products, arithmetic and copies ran while one was open for 1% -> 2% of each run, Pallas kernels for 20% -> 21%
where the time goes in v6:
time: 53.2 us; the launch traced here: 52.7 us
  starting transfers between devices  30.7 us (58%)
  Pallas kernels  11 us (21%)
  waiting for transfers between devices  7.1 us (13%)
  local copies, waits for them, and re-layouts  3.13 us (6%)
  other arithmetic  0.69 us (1%)
    ppermute x4, starting transfers between devices, per_device(): parts = [lax.ppermute(part, 'blk', even_on) for part in parts]  11.7 us
    ppermute x3, starting transfers between devices, exchange(): lax.ppermute(pieces[by], 'layer', [(i, i ^ by) for i in range(layers)])  6.76 us
    ppermute x3, starting transfers between devices, per_device(): lax.ppermute(mine, 'layer', [(i, i ^ by) for i in range(layers)])  6.69 us
    pallas_call x2, Pallas kernels, scores_call(): pl.pallas_call(functools.partial(scores_kernel, steps, first, layers), in...  4.82 us
    ppermute x4, waiting for transfers between devices, per_device(): parts = [lax.ppermute(part, 'blk', even_on) for part in parts]  4.75 us
    ppermute x1, starting transfers between devices, per_device(): lax.ppermute(after(q, sums0[1]), 'blk', [(i, i + 1) for i in evens])  3.48 us
    unnamed x9, local copies, waits for them, and re-layouts  3.13 us
    pallas_call x4, Pallas kernels, part_call(): pl.pallas_call(part_kernel, in_specs=[VMEM] * (2 + len(pieces)), out_spec...  3.05 us
  transfers between devices with their start and end apart: 13, of which 3 were waited for; matrix products, arithmetic and copies ran while one was open for 2% of the time, Pallas kernels for 21%

profile of v6, /device:TPU:0, one launch (start us, length us, event | category | flops | bytes accessed | tf_op | source)
XLA Modules:
  0.0 52.7 jit_solution(8026671218585418647)
XLA Ops:
  0.0 0.8 %collective-permute-start.3 = (bf16[256,4096]{1,0:T(8,128)(2,1)}, bf16[256,4096]{1,0:T(8,128)(2,1)S(1)}, u32[]{:S(2)}, u32[]{:S(2)}) collective-permute-start(bf16[256,4096]{1,0:T(8,128)(2,1)} %bitcast.1.refs_0_.q_ref), channel_id=1, source_target_pairs={{4,12},{12,4},{5,13},{13,5},{6,14},{14,6},{7,15},{15,7},{20,28},{2... | collective-permute-start | bytes 6291464 | tf_op jit(solution)/shard_map/ppermute | solution.py:193
  0.8 0.8 %copy.5 = s32[3,256]{0,1:T(8,128)S(1)} copy(s32[3,256]{1,0:T(4,128)} %param.7) | data formatting | bytes 6144 | tf_op args[3]
  1.6 1.6 %copy-done = bf16[256,1,4096]{2,0,1:T(8,128)(2,1)S(1)} copy-done((bf16[256,1,4096]{2,0,1:T(8,128)(2,1)S(1)}, bf16[256,1,4096]{2,0,1:T(8,128)(2,1)}, u32[]{:S(2)}) %copy-start) | copy-done | bytes 2097176
  3.9 3.1 %scores_0.1 = (f32[72,256]{1,0:T(8,128)S(1)}, f32[72,256]{1,0:T(8,128)S(1)}, f32[72,256]{1,0:T(8,128)S(1)}, f32[72,256]{1,0:T(8,128)S(1)}) custom-call(s32[1]{0:T(128)} %bitcast.me_ref, bf16[256,4096]{1,0:T(8,128)(2,1)} %bitcast.1.refs_0_.q_ref, bf16[256,4096]{1,0:T(8,128)(2,1)S(1)} %bitcast.6, f32[1,4096]{1,0:T(1,128)S(1)} %copy-done.2, s32[256,3]{1,0:T(8,128)S(1)} %bitcast.12), custom_call_target="tpu_custom_call" | custom-call | flops 536870912 | bytes 4194304 | tf_op jit(solution)/shard_map/scores_0/pallas_call | solution.py:91
  7.1 3.1 %collective-permute-start = (f32[72,256]{1,0:T(8,128)S(1)}, f32[72,256]{1,0:T(8,128)S(1)}, u32[]{:S(2)}, u32[]{:S(2)}) collective-permute-start(f32[72,256]{1,0:T(8,128)S(1)} %get-tuple-element.26), channel_id=1, source_target_pairs={{0,1},{1,0},{2,3},{3,2},{4,5},{5,4},{6,7},{7,6},{8,9},{9,8},{10,11... | collective-permute-start | bytes 221192 | tf_op jit(solution)/shard_map/ppermute | solution.py:190
  10.2 2.3 %collective-permute-done.refs_1_ = f32[72,256]{1,0:T(8,128)S(1)} collective-permute-done((f32[72,256]{1,0:T(8,128)S(1)}, f32[72,256]{1,0:T(8,128)S(1)}, u32[]{:S(2)}, u32[]{:S(2)}) %collective-permute-start) | collective-permute-done | bytes 73760 | tf_op jit(solution)/shard_map/ppermute | solution.py:190
  12.5 3.5 %collective-permute-start.5 = (bf16[256,4096]{1,0:T(8,128)(2,1)}, bf16[256,4096]{1,0:T(8,128)(2,1)S(1)}, u32[]{:S(2)}, u32[]{:S(2)}) collective-permute-start(bf16[256,4096]{1,0:T(8,128)(2,1)} %bitcast.1.refs_0_.q_ref), channel_id=1, source_target_pairs={{0,4},{8,12},{1,5},{9,13},{2,6},{10,14},{3,7},{11,15},{16,20},{24,... | collective-permute-start | bytes 6291464 | tf_op jit(solution)/shard_map/ppermute | solution.py:200
  16.0 2.4 %ordered.1 = (bf16[64,4096]{1,0:T(8,128)(2,1)S(1)}, bf16[64,4096]{1,0:T(8,128)(2,1)S(1)}, bf16[64,4096]{1,0:T(8,128)(2,1)S(1)}, bf16[64,4096]{1,0:T(8,128)(2,1)S(1)}) custom-call(s32[1]{0:T(128)} %bitcast.me_ref, bf16[256,4096]{1,0:T(8,128)(2,1)} %bitcast.1.refs_0_.q_ref, f32[1,4096]{1,0:T(1,128)S(1)} %copy-done.3, s32[256,3]{1,0:T(8,128)S(1)} %bitcast.13), custom_call_target="tpu_custom_call" | custom-call | flops 536870912 | bytes 4194304 | tf_op jit(solution)/shard_map/ordered/pallas_call | solution.py:122
  18.4 1.3 %collective-permute-start.6 = (bf16[256,4096]{1,0:T(8,128)(2,1)S(1)}, bf16[256,4096]{1,0:T(8,128)(2,1)S(1)}, u32[]{:S(2)}, u32[]{:S(2)}) collective-permute-start(bf16[256,4096]{1,0:T(8,128)(2,1)S(1)} %collective-permute-done.3.refs_2_), channel_id=1, source_target_pairs={{4,0},{12,8},{5,1},{13,9},{6,2},{14,10},{7,3},{15,11},{20,16},{28,... | collective-permute-start | bytes 6291464 | tf_op jit(solution)/shard_map/ppermute | solution.py:205
  19.7 3.7 %collective-permute-start.1 = (f32[72,256]{1,0:T(8,128)S(1)}, f32[72,256]{1,0:T(8,128)S(1)}, u32[]{:S(2)}, u32[]{:S(2)}) collective-permute-start(f32[72,256]{1,0:T(8,128)S(1)} %get-tuple-element.27), channel_id=1, source_target_pairs={{0,3},{1,2},{2,1},{3,0},{4,7},{5,6},{6,5},{7,4},{8,11},{9,10},{10,... | collective-permute-start | bytes 221192 | tf_op jit(solution)/shard_map/ppermute | solution.py:190
  23.4 3.0 %collective-permute-start.7 = (bf16[64,4096]{1,0:T(8,128)(2,1)S(1)}, bf16[64,4096]{1,0:T(8,128)(2,1)S(1)}, u32[]{:S(2)}, u32[]{:S(2)}) collective-permute-start(bf16[64,4096]{1,0:T(8,128)(2,1)S(1)} %get-tuple-element.33), channel_id=1, source_target_pairs={{0,8},{8,0},{1,9},{9,1},{2,10},{10,2},{3,11},{11,3},{16,24},{24,16... | collective-permute-start | bytes 1572872 | tf_op jit(solution)/shard_map/ppermute | solution.py:210
  26.4 2.8 %collective-permute-start.9 = (bf16[64,4096]{1,0:T(8,128)(2,1)S(1)}, bf16[64,4096]{1,0:T(8,128)(2,1)S(1)}, u32[]{:S(2)}, u32[]{:S(2)}) collective-permute-start(bf16[64,4096]{1,0:T(8,128)(2,1)S(1)} %get-tuple-element.40), channel_id=1, source_target_pairs={{0,8},{8,0},{1,9},{9,1},{2,10},{10,2},{3,11},{11,3},{16,24},{24,16... | collective-permute-start | bytes 1572872 | tf_op jit(solution)/shard_map/ppermute | solution.py:210
  29.2 3.1 %collective-permute-start.11 = (bf16[64,4096]{1,0:T(8,128)(2,1)S(1)}, bf16[64,4096]{1,0:T(8,128)(2,1)S(1)}, u32[]{:S(2)}, u32[]{:S(2)}) collective-permute-start(bf16[64,4096]{1,0:T(8,128)(2,1)S(1)} %get-tuple-element.42), channel_id=1, source_target_pairs={{0,8},{8,0},{1,9},{9,1},{2,10},{10,2},{3,11},{11,3},{16,24},{24,16... | collective-permute-start | bytes 1572872 | tf_op jit(solution)/shard_map/ppermute | solution.py:210
  32.3 2.8 %collective-permute-start.4 = (bf16[64,4096]{1,0:T(8,128)(2,1)S(1)}, bf16[64,4096]{1,0:T(8,128)(2,1)S(1)}, u32[]{:S(2)}, u32[]{:S(2)}) collective-permute-start(bf16[64,4096]{1,0:T(8,128)(2,1)S(1)} %get-tuple-element.35), channel_id=1, source_target_pairs={{0,8},{8,0},{1,9},{9,1},{2,10},{10,2},{3,11},{11,3},{16,24},{24,16... | collective-permute-start | bytes 1572872 | tf_op jit(solution)/shard_map/ppermute | solution.py:210
  35.1 1.7 %scores_1_2.1 = (f32[128,256]{1,0:T(8,128)S(1)}, f32[128,256]{1,0:T(8,128)S(1)}, f32[128,256]{1,0:T(8,128)S(1)}, f32[128,256]{1,0:T(8,128)S(1)}) custom-call(s32[1]{0:T(128)} %bitcast.me_ref, bf16[256,4096]{1,0:T(8,128)(2,1)S(1)} %collective-permute-done.5.refs_0_, bf16[256,4096]{1,0:T(8,128)(2,1)S(1)} %collective-permute-done.6.refs_1_, ...), custom_call_target="tpu_custom_call" | custom-call | flops 1073741824 | bytes 4194304 | tf_op jit(solution)/shard_map/scores_1_2/pallas_call | solution.py:91
  36.8 0.8 %part.4 = bf16[128,256]{1,0:T(8,128)(2,1)S(1)} custom-call(bf16[64,4096]{1,0:T(8,128)(2,1)S(1)} %collective-permute-done.7.x_ref, bf16[256,4096]{1,0:T(8,128)(2,1)S(1)} %bitcast.8, f32[128,256]{1,0:T(8,128)S(1)} %get-tuple-element.38.refs_0_), custom_call_target="tpu_custom_call" | custom-call | flops 134217728 | bytes 2097152 | tf_op jit(solution)/shard_map/part/pallas_call | solution.py:147
  37.6 3.5 %collective-permute-start.8 = (bf16[128,256]{1,0:T(8,128)(2,1)S(1)}, bf16[128,256]{1,0:T(8,128)(2,1)S(1)}, u32[]{:S(2)}, u32[]{:S(2)}) collective-permute-start(bf16[128,256]{1,0:T(8,128)(2,1)S(1)} %part.4), channel_id=1, source_target_pairs={{0,3},{1,2},{2,1},{3,0},{4,7},{5,6},{6,5},{7,4},{8,11},{9,10},{10,... | collective-permute-start | bytes 196616 | tf_op jit(solution)/shard_map/ppermute | solution.py:214
  41.1 0.8 %part.5 = bf16[128,256]{1,0:T(8,128)(2,1)S(1)} custom-call(bf16[64,4096]{1,0:T(8,128)(2,1)S(1)} %collective-permute-done.9.x_ref, bf16[256,4096]{1,0:T(8,128)(2,1)S(1)} %bitcast.9, f32[128,256]{1,0:T(8,128)S(1)} %get-tuple-element.41.refs_0_), custom_call_target="tpu_custom_call" | custom-call | flops 134217728 | bytes 2097152 | tf_op jit(solution)/shard_map/part/pallas_call | solution.py:147
  41.9 1.9 %collective-permute-start.10 = (bf16[128,256]{1,0:T(8,128)(2,1)S(1)}, bf16[128,256]{1,0:T(8,128)(2,1)S(1)}, u32[]{:S(2)}, u32[]{:S(2)}) collective-permute-start(bf16[128,256]{1,0:T(8,128)(2,1)S(1)} %part.5), channel_id=1, source_target_pairs={{0,2},{1,3},{2,0},{3,1},{4,6},{5,7},{6,4},{7,5},{8,10},{9,11},{10,... | collective-permute-start | bytes 196616 | tf_op jit(solution)/shard_map/ppermute | solution.py:214
  43.8 1.9 %collective-permute-done.11.x_ref = bf16[64,4096]{1,0:T(8,128)(2,1)S(1)} collective-permute-done((bf16[64,4096]{1,0:T(8,128)(2,1)S(1)}, bf16[64,4096]{1,0:T(8,128)(2,1)S(1)}, u32[]{:S(2)}, u32[]{:S(2)}) %collective-permute-start.11) | collective-permute-done | bytes 524320 | tf_op jit(solution)/shard_map/ppermute | solution.py:210
  45.7 0.8 %part.7 = bf16[128,256]{1,0:T(8,128)(2,1)S(1)} custom-call(bf16[64,4096]{1,0:T(8,128)(2,1)S(1)} %collective-permute-done.11.x_ref, bf16[256,4096]{1,0:T(8,128)(2,1)S(1)} %bitcast.10, f32[128,256]{1,0:T(8,128)S(1)} %get-tuple-element.43.refs_0_), custom_call_target="tpu_custom_call" | custom-call | flops 134217728 | bytes 2097152 | tf_op jit(solution)/shard_map/part/pallas_call | solution.py:147
  46.4 1.3 %collective-permute-start.12 = (bf16[128,256]{1,0:T(8,128)(2,1)S(1)}, bf16[128,256]{1,0:T(8,128)(2,1)S(1)}, u32[]{:S(2)}, u32[]{:S(2)}) collective-permute-start(bf16[128,256]{1,0:T(8,128)(2,1)S(1)} %part.7), channel_id=1, source_target_pairs={{0,1},{1,0},{2,3},{3,2},{4,5},{5,4},{6,7},{7,6},{8,9},{9,8},{10,11... | collective-permute-start | bytes 196616 | tf_op jit(solution)/shard_map/ppermute | solution.py:214
  48.4 2.9 %collective-permute-done.4.x_ref = bf16[64,4096]{1,0:T(8,128)(2,1)S(1)} collective-permute-done((bf16[64,4096]{1,0:T(8,128)(2,1)S(1)}, bf16[64,4096]{1,0:T(8,128)(2,1)S(1)}, u32[]{:S(2)}, u32[]{:S(2)}) %collective-permute-start.4) | collective-permute-done | bytes 524320 | tf_op jit(solution)/shard_map/ppermute | solution.py:210
  51.3 0.8 %part.6 = f32[128,256]{1,0:T(8,128)S(1)} custom-call(bf16[64,4096]{1,0:T(8,128)(2,1)S(1)} %collective-permute-done.4.x_ref, bf16[256,4096]{1,0:T(8,128)(2,1)S(1)} %bitcast.11, f32[128,256]{1,0:T(8,128)S(1)} %get-tuple-element.37.refs_0_, bf16[128,256]{1,0:T(8,128)(2,1)S(1)} %collective-permute-done.8.refs_1_, ...), custom_call_target="tpu_custom_call" | custom-call | flops 134217728 | bytes 2097152 | tf_op jit(solution)/shard_map/part/pallas_call | solution.py:147
  (21 shorter events, 2.2 us)
Async XLA Ops:
  0.0 18.4 %collective-permute-start.3 = (bf16[256,4096]{1,0:T(8,128)(2,1)}, bf16[256,4096]{1,0:T(8,128)(2,1)S(1)}, u32[]{:S(2)}, u32[]{:S(2)}) collective-permute-start(bf16[256,4096]{1,0:T(8,128)(2,1)} %bitcast.1.refs_0_.q_ref), channel_id=1, source_target_pairs={{4,12},{12,4},{5,13},{13,5},{6,14},{14,6},{7,15},{15,7},{20,28},{2... | collective-permute-start | bytes 6291464 | tf_op jit(solution)/shard_map/ppermute | solution.py:193
  1.6 1.6 %copy-start = (bf16[256,1,4096]{2,0,1:T(8,128)(2,1)S(1)}, bf16[256,1,4096]{2,0,1:T(8,128)(2,1)}, u32[]{:S(2)}) copy-start(bf16[256,1,4096]{2,0,1:T(8,128)(2,1)} %param.4) | copy-start | bytes 6291460
  3.2 0.7 %copy-start.2 = (f32[1,4096]{1,0:T(1,128)S(1)}, f32[1,4096]{1,0:T(1,128)}, u32[]{:S(2)}) copy-start(f32[1,4096]{1,0:T(1,128)} %refs_4_.1) | copy-start | bytes 49156
  3.9 12.1 %copy-start.3 = (f32[1,4096]{1,0:T(1,128)S(1)}, f32[1,4096]{1,0:T(1,128)}, u32[]{:S(2)}) copy-start(f32[1,4096]{1,0:T(1,128)} %refs_4_.1) | copy-start | bytes 49156
  7.1 28.0 %copy-start.1 = (bf16[256,1,4096]{2,0,1:T(8,128)(2,1)S(1)}, bf16[256,1,4096]{2,0,1:T(8,128)(2,1)}, u32[]{:S(2)}) copy-start(bf16[256,1,4096]{2,0,1:T(8,128)(2,1)} %param.4) | copy-start | bytes 6291460
  7.1 5.4 %collective-permute-start = (f32[72,256]{1,0:T(8,128)S(1)}, f32[72,256]{1,0:T(8,128)S(1)}, u32[]{:S(2)}, u32[]{:S(2)}) collective-permute-start(f32[72,256]{1,0:T(8,128)S(1)} %get-tuple-element.26), channel_id=1, source_target_pairs={{0,1},{1,0},{2,3},{3,2},{4,5},{5,4},{6,7},{7,6},{8,9},{9,8},{10,11... | collective-permute-start | bytes 221192 | tf_op jit(solution)/shard_map/ppermute | solution.py:190
  12.5 19.8 %collective-permute-start.5 = (bf16[256,4096]{1,0:T(8,128)(2,1)}, bf16[256,4096]{1,0:T(8,128)(2,1)S(1)}, u32[]{:S(2)}, u32[]{:S(2)}) collective-permute-start(bf16[256,4096]{1,0:T(8,128)(2,1)} %bitcast.1.refs_0_.q_ref), channel_id=1, source_target_pairs={{0,4},{8,12},{1,5},{9,13},{2,6},{10,14},{3,7},{11,15},{16,20},{24,... | collective-permute-start | bytes 6291464 | tf_op jit(solution)/shard_map/ppermute | solution.py:200
  18.4 16.7 %collective-permute-start.6 = (bf16[256,4096]{1,0:T(8,128)(2,1)S(1)}, bf16[256,4096]{1,0:T(8,128)(2,1)S(1)}, u32[]{:S(2)}, u32[]{:S(2)}) collective-permute-start(bf16[256,4096]{1,0:T(8,128)(2,1)S(1)} %collective-permute-done.3.refs_2_), channel_id=1, source_target_pairs={{4,0},{12,8},{5,1},{13,9},{6,2},{14,10},{7,3},{15,11},{20,16},{28,... | collective-permute-start | bytes 6291464 | tf_op jit(solution)/shard_map/ppermute | solution.py:205
  19.7 6.7 %collective-permute-start.1 = (f32[72,256]{1,0:T(8,128)S(1)}, f32[72,256]{1,0:T(8,128)S(1)}, u32[]{:S(2)}, u32[]{:S(2)}) collective-permute-start(f32[72,256]{1,0:T(8,128)S(1)} %get-tuple-element.27), channel_id=1, source_target_pairs={{0,3},{1,2},{2,1},{3,0},{4,7},{5,6},{6,5},{7,4},{8,11},{9,10},{10,... | collective-permute-start | bytes 221192 | tf_op jit(solution)/shard_map/ppermute | solution.py:190
  23.4 5.9 %collective-permute-start.2 = (f32[72,256]{1,0:T(8,128)S(1)}, f32[72,256]{1,0:T(8,128)S(1)}, u32[]{:S(2)}, u32[]{:S(2)}) collective-permute-start(f32[72,256]{1,0:T(8,128)S(1)} %get-tuple-element.28), channel_id=1, source_target_pairs={{0,2},{1,3},{2,0},{3,1},{4,6},{5,7},{6,4},{7,5},{8,10},{9,11},{10,... | collective-permute-start | bytes 221192 | tf_op jit(solution)/shard_map/ppermute | solution.py:190
  23.4 13.5 %collective-permute-start.7 = (bf16[64,4096]{1,0:T(8,128)(2,1)S(1)}, bf16[64,4096]{1,0:T(8,128)(2,1)S(1)}, u32[]{:S(2)}, u32[]{:S(2)}) collective-permute-start(bf16[64,4096]{1,0:T(8,128)(2,1)S(1)} %get-tuple-element.33), channel_id=1, source_target_pairs={{0,8},{8,0},{1,9},{9,1},{2,10},{10,2},{3,11},{11,3},{16,24},{24,16... | collective-permute-start | bytes 1572872 | tf_op jit(solution)/shard_map/ppermute | solution.py:210
  26.4 14.7 %collective-permute-start.9 = (bf16[64,4096]{1,0:T(8,128)(2,1)S(1)}, bf16[64,4096]{1,0:T(8,128)(2,1)S(1)}, u32[]{:S(2)}, u32[]{:S(2)}) collective-permute-start(bf16[64,4096]{1,0:T(8,128)(2,1)S(1)} %get-tuple-element.40), channel_id=1, source_target_pairs={{0,8},{8,0},{1,9},{9,1},{2,10},{10,2},{3,11},{11,3},{16,24},{24,16... | collective-permute-start | bytes 1572872 | tf_op jit(solution)/shard_map/ppermute | solution.py:210
  29.2 16.4 %collective-permute-start.11 = (bf16[64,4096]{1,0:T(8,128)(2,1)S(1)}, bf16[64,4096]{1,0:T(8,128)(2,1)S(1)}, u32[]{:S(2)}, u32[]{:S(2)}) collective-permute-start(bf16[64,4096]{1,0:T(8,128)(2,1)S(1)} %get-tuple-element.42), channel_id=1, source_target_pairs={{0,8},{8,0},{1,9},{9,1},{2,10},{10,2},{3,11},{11,3},{16,24},{24,16... | collective-permute-start | bytes 1572872 | tf_op jit(solution)/shard_map/ppermute | solution.py:210
  32.3 19.0 %collective-permute-start.4 = (bf16[64,4096]{1,0:T(8,128)(2,1)S(1)}, bf16[64,4096]{1,0:T(8,128)(2,1)S(1)}, u32[]{:S(2)}, u32[]{:S(2)}) collective-permute-start(bf16[64,4096]{1,0:T(8,128)(2,1)S(1)} %get-tuple-element.35), channel_id=1, source_target_pairs={{0,8},{8,0},{1,9},{9,1},{2,10},{10,2},{3,11},{11,3},{16,24},{24,16... | collective-permute-start | bytes 1572872 | tf_op jit(solution)/shard_map/ppermute | solution.py:210
  37.6 13.7 %collective-permute-start.8 = (bf16[128,256]{1,0:T(8,128)(2,1)S(1)}, bf16[128,256]{1,0:T(8,128)(2,1)S(1)}, u32[]{:S(2)}, u32[]{:S(2)}) collective-permute-start(bf16[128,256]{1,0:T(8,128)(2,1)S(1)} %part.4), channel_id=1, source_target_pairs={{0,3},{1,2},{2,1},{3,0},{4,7},{5,6},{6,5},{7,4},{8,11},{9,10},{10,... | collective-permute-start | bytes 196616 | tf_op jit(solution)/shard_map/ppermute | solution.py:214
  41.9 9.4 %collective-permute-start.10 = (bf16[128,256]{1,0:T(8,128)(2,1)S(1)}, bf16[128,256]{1,0:T(8,128)(2,1)S(1)}, u32[]{:S(2)}, u32[]{:S(2)}) collective-permute-start(bf16[128,256]{1,0:T(8,128)(2,1)S(1)} %part.5), channel_id=1, source_target_pairs={{0,2},{1,3},{2,0},{3,1},{4,6},{5,7},{6,4},{7,5},{8,10},{9,11},{10,... | collective-permute-start | bytes 196616 | tf_op jit(solution)/shard_map/ppermute | solution.py:214
  46.4 5.6 %collective-permute-start.12 = (bf16[128,256]{1,0:T(8,128)(2,1)S(1)}, bf16[128,256]{1,0:T(8,128)(2,1)S(1)}, u32[]{:S(2)}, u32[]{:S(2)}) collective-permute-start(bf16[128,256]{1,0:T(8,128)(2,1)S(1)} %part.7), channel_id=1, source_target_pairs={{0,1},{1,0},{2,3},{3,2},{4,5},{5,4},{6,7},{7,6},{8,9},{9,8},{10,11... | collective-permute-start | bytes 196616 | tf_op jit(solution)/shard_map/ppermute | solution.py:214

commit v7 on v6

--- a/solution.py
+++ b/solution.py
@@ -197,8 +197,8 @@
     ordered = ordered_call(2, layers, me, after(q, *pieces), eigenvalues, columns)
     bys = [*range(layers - 1, 0, -1), 0]
     parts = [ordered[by] for by in bys]
-    odd_one = lax.ppermute(after(q, sums0[1]), "blk", [(i, i + 1) for i in evens])
-    odd_two = after(odd_two, parts[0])
+    odd_one = lax.ppermute(after(q, *pieces), "blk", [(i, i + 1) for i in evens])
+    odd_two = after(odd_two, parts[0], sums0[1])
     parts[1] = after(parts[1], odd_two)
     parts[2:] = lax.optimization_barrier((*parts[2:], odd_two, *sums0))[: layers - 2]
 

time: 53.2 us -> 52.6 us (0.989)
  waiting for transfers between devices: 7.1 us -> 5.02 us
  starting transfers between devices: 30.7 us -> 32.2 us
    ppermute x1, starting transfers between devices: 3.48 us -> 5.78 us  [per_device(): lax.ppermute(after(q, *pieces), 'blk', [(i, i + 1) for i in evens])]
    ppermute x3, waiting for transfers between devices: 2.34 us -> 0.52 us  [exchange(): lax.ppermute(pieces[by], 'layer', [(i, i ^ by) for i in range(layers)])]
    ppermute x3, starting transfers between devices: 6.76 us -> 5.31 us  [exchange(): lax.ppermute(pieces[by], 'layer', [(i, i ^ by) for i in range(layers)])]
    ppermute x3, starting transfers between devices: 6.69 us -> 7.47 us  [per_device(): lax.ppermute(mine, 'layer', [(i, i ^ by) for i in range(layers)])]
  transfers between devices with their start and end apart: 13 -> 13, of which waited for: 3 -> 5; matrix products, arithmetic and copies ran while one was open for 2% -> 2% of each run, Pallas kernels for 21% -> 21%
where the time goes in v7:
time: 52.6 us; the launch traced here: 52.1 us
  starting transfers between devices  32.2 us (61%)
  Pallas kernels  10.9 us (21%)
  waiting for transfers between devices  5.02 us (10%)
  local copies, waits for them, and re-layouts  3.13 us (6%)
  other arithmetic  0.69 us (1%)
    ppermute x4, starting transfers between devices, per_device(): parts = [lax.ppermute(part, 'blk', even_on) for part in parts]  11.6 us
    ppermute x3, starting transfers between devices, per_device(): lax.ppermute(mine, 'layer', [(i, i ^ by) for i in range(layers)])  7.47 us
    ppermute x1, starting transfers between devices, per_device(): lax.ppermute(after(q, *pieces), 'blk', [(i, i + 1) for i in evens])  5.78 us
    ppermute x3, starting transfers between devices, exchange(): lax.ppermute(pieces[by], 'layer', [(i, i ^ by) for i in range(layers)])  5.31 us
    pallas_call x2, Pallas kernels, scores_call(): pl.pallas_call(functools.partial(scores_kernel, steps, first, layers), in...  4.82 us
    ppermute x4, waiting for transfers between devices, per_device(): parts = [lax.ppermute(part, 'blk', even_on) for part in parts]  4.24 us
    unnamed x9, local copies, waits for them, and re-layouts  3.13 us
    pallas_call x4, Pallas kernels, part_call(): pl.pallas_call(part_kernel, in_specs=[VMEM] * (2 + len(pieces)), out_spec...  3.06 us
  transfers between devices with their start and end apart: 13, of which 5 were waited for; matrix products, arithmetic and copies ran while one was open for 2% of the time, Pallas kernels for 21%

profile of v7, /device:TPU:0, one launch (start us, length us, event | category | flops | bytes accessed | tf_op | source)
XLA Modules:
  0.0 52.1 jit_solution(7356226081644306531)
XLA Ops:
  0.0 0.8 %collective-permute-start.3 = (bf16[256,4096]{1,0:T(8,128)(2,1)}, bf16[256,4096]{1,0:T(8,128)(2,1)S(1)}, u32[]{:S(2)}, u32[]{:S(2)}) collective-permute-start(bf16[256,4096]{1,0:T(8,128)(2,1)} %bitcast.1.refs_0_.q_ref), channel_id=1, source_target_pairs={{4,12},{12,4},{5,13},{13,5},{6,14},{14,6},{7,15},{15,7},{20,28},{2... | collective-permute-start | bytes 6291464 | tf_op jit(solution)/shard_map/ppermute | solution.py:193
  0.8 0.8 %copy.5 = s32[3,256]{0,1:T(8,128)S(1)} copy(s32[3,256]{1,0:T(4,128)} %param.7) | data formatting | bytes 6144 | tf_op args[3]
  1.6 1.6 %copy-done = bf16[256,1,4096]{2,0,1:T(8,128)(2,1)S(1)} copy-done((bf16[256,1,4096]{2,0,1:T(8,128)(2,1)S(1)}, bf16[256,1,4096]{2,0,1:T(8,128)(2,1)}, u32[]{:S(2)}) %copy-start) | copy-done | bytes 2097176
  3.2 0.7 %copy-done.2 = f32[1,4096]{1,0:T(1,128)S(1)} copy-done((f32[1,4096]{1,0:T(1,128)S(1)}, f32[1,4096]{1,0:T(1,128)}, u32[]{:S(2)}) %copy-start.2) | copy-done | bytes 16408
  3.9 3.1 %scores_0.1 = (f32[72,256]{1,0:T(8,128)S(1)}, f32[72,256]{1,0:T(8,128)S(1)}, f32[72,256]{1,0:T(8,128)S(1)}, f32[72,256]{1,0:T(8,128)S(1)}) custom-call(s32[1]{0:T(128)} %bitcast.me_ref, bf16[256,4096]{1,0:T(8,128)(2,1)} %bitcast.1.refs_0_.q_ref, bf16[256,4096]{1,0:T(8,128)(2,1)S(1)} %bitcast.6, f32[1,4096]{1,0:T(1,128)S(1)} %copy-done.2, s32[256,3]{1,0:T(8,128)S(1)} %bitcast.12), custom_call_target="tpu_custom_call" | custom-call | flops 536870912 | bytes 4194304 | tf_op jit(solution)/shard_map/scores_0/pallas_call | solution.py:91
  7.1 5.8 %collective-permute-start.5 = (bf16[256,4096]{1,0:T(8,128)(2,1)}, bf16[256,4096]{1,0:T(8,128)(2,1)S(1)}, u32[]{:S(2)}, u32[]{:S(2)}) collective-permute-start(bf16[256,4096]{1,0:T(8,128)(2,1)} %bitcast.1.refs_0_.q_ref), channel_id=1, source_target_pairs={{0,4},{8,12},{1,5},{9,13},{2,6},{10,14},{3,7},{11,15},{16,20},{24,... | collective-permute-start | bytes 6291464 | tf_op jit(solution)/shard_map/ppermute | solution.py:200
  12.9 1.6 %collective-permute-start = (f32[72,256]{1,0:T(8,128)S(1)}, f32[72,256]{1,0:T(8,128)S(1)}, u32[]{:S(2)}, u32[]{:S(2)}) collective-permute-start(f32[72,256]{1,0:T(8,128)S(1)} %get-tuple-element.25), channel_id=1, source_target_pairs={{0,1},{1,0},{2,3},{3,2},{4,5},{5,4},{6,7},{7,6},{8,9},{9,8},{10,11... | collective-permute-start | bytes 221192 | tf_op jit(solution)/shard_map/ppermute | solution.py:190
  14.5 2.4 %ordered.1 = (bf16[64,4096]{1,0:T(8,128)(2,1)S(1)}, bf16[64,4096]{1,0:T(8,128)(2,1)S(1)}, bf16[64,4096]{1,0:T(8,128)(2,1)S(1)}, bf16[64,4096]{1,0:T(8,128)(2,1)S(1)}) custom-call(s32[1]{0:T(128)} %bitcast.me_ref, bf16[256,4096]{1,0:T(8,128)(2,1)} %bitcast.1.refs_0_.q_ref, f32[1,4096]{1,0:T(1,128)S(1)} %copy-done.3, s32[256,3]{1,0:T(8,128)S(1)} %bitcast.13), custom_call_target="tpu_custom_call" | custom-call | flops 536870912 | bytes 4194304 | tf_op jit(solution)/shard_map/ordered/pallas_call | solution.py:122
  17.3 1.3 %collective-permute-start.6 = (bf16[256,4096]{1,0:T(8,128)(2,1)S(1)}, bf16[256,4096]{1,0:T(8,128)(2,1)S(1)}, u32[]{:S(2)}, u32[]{:S(2)}) collective-permute-start(bf16[256,4096]{1,0:T(8,128)(2,1)S(1)} %collective-permute-done.3.refs_2_), channel_id=1, source_target_pairs={{4,0},{12,8},{5,1},{13,9},{6,2},{14,10},{7,3},{15,11},{20,16},{28,... | collective-permute-start | bytes 6291464 | tf_op jit(solution)/shard_map/ppermute | solution.py:205
  18.6 3.7 %collective-permute-start.1 = (f32[72,256]{1,0:T(8,128)S(1)}, f32[72,256]{1,0:T(8,128)S(1)}, u32[]{:S(2)}, u32[]{:S(2)}) collective-permute-start(f32[72,256]{1,0:T(8,128)S(1)} %get-tuple-element.26), channel_id=1, source_target_pairs={{0,3},{1,2},{2,1},{3,0},{4,7},{5,6},{6,5},{7,4},{8,11},{9,10},{10,... | collective-permute-start | bytes 221192 | tf_op jit(solution)/shard_map/ppermute | solution.py:190
  22.2 2.4 %collective-permute-start.7 = (bf16[64,4096]{1,0:T(8,128)(2,1)S(1)}, bf16[64,4096]{1,0:T(8,128)(2,1)S(1)}, u32[]{:S(2)}, u32[]{:S(2)}) collective-permute-start(bf16[64,4096]{1,0:T(8,128)(2,1)S(1)} %get-tuple-element.32), channel_id=1, source_target_pairs={{0,8},{8,0},{1,9},{9,1},{2,10},{10,2},{3,11},{11,3},{16,24},{24,16... | collective-permute-start | bytes 1572872 | tf_op jit(solution)/shard_map/ppermute | solution.py:210
  24.8 3.3 %collective-permute-start.9 = (bf16[64,4096]{1,0:T(8,128)(2,1)S(1)}, bf16[64,4096]{1,0:T(8,128)(2,1)S(1)}, u32[]{:S(2)}, u32[]{:S(2)}) collective-permute-start(bf16[64,4096]{1,0:T(8,128)(2,1)S(1)} %get-tuple-element.38), channel_id=1, source_target_pairs={{0,8},{8,0},{1,9},{9,1},{2,10},{10,2},{3,11},{11,3},{16,24},{24,16... | collective-permute-start | bytes 1572872 | tf_op jit(solution)/shard_map/ppermute | solution.py:210
  28.1 2.5 %collective-permute-start.11 = (bf16[64,4096]{1,0:T(8,128)(2,1)S(1)}, bf16[64,4096]{1,0:T(8,128)(2,1)S(1)}, u32[]{:S(2)}, u32[]{:S(2)}) collective-permute-start(bf16[64,4096]{1,0:T(8,128)(2,1)S(1)} %get-tuple-element.40), channel_id=1, source_target_pairs={{0,8},{8,0},{1,9},{9,1},{2,10},{10,2},{3,11},{11,3},{16,24},{24,16... | collective-permute-start | bytes 1572872 | tf_op jit(solution)/shard_map/ppermute | solution.py:210
  30.7 3.3 %collective-permute-start.4 = (bf16[64,4096]{1,0:T(8,128)(2,1)S(1)}, bf16[64,4096]{1,0:T(8,128)(2,1)S(1)}, u32[]{:S(2)}, u32[]{:S(2)}) collective-permute-start(bf16[64,4096]{1,0:T(8,128)(2,1)S(1)} %get-tuple-element.34), channel_id=1, source_target_pairs={{0,8},{8,0},{1,9},{9,1},{2,10},{10,2},{3,11},{11,3},{16,24},{24,16... | collective-permute-start | bytes 1572872 | tf_op jit(solution)/shard_map/ppermute | solution.py:210
  34.2 1.7 %scores_1_2.1 = (f32[128,256]{1,0:T(8,128)S(1)}, f32[128,256]{1,0:T(8,128)S(1)}, f32[128,256]{1,0:T(8,128)S(1)}, f32[128,256]{1,0:T(8,128)S(1)}) custom-call(s32[1]{0:T(128)} %bitcast.me_ref, bf16[256,4096]{1,0:T(8,128)(2,1)S(1)} %collective-permute-done.5.refs_0_, bf16[256,4096]{1,0:T(8,128)(2,1)S(1)} %collective-permute-done.6.refs_1_, ...), custom_call_target="tpu_custom_call" | custom-call | flops 1073741824 | bytes 4194304 | tf_op jit(solution)/shard_map/scores_1_2/pallas_call | solution.py:91
  36.0 0.8 %part.4 = bf16[128,256]{1,0:T(8,128)(2,1)S(1)} custom-call(bf16[64,4096]{1,0:T(8,128)(2,1)S(1)} %collective-permute-done.7.x_ref, bf16[256,4096]{1,0:T(8,128)(2,1)S(1)} %bitcast.8, f32[128,256]{1,0:T(8,128)S(1)} %get-tuple-element.36.refs_0_), custom_call_target="tpu_custom_call" | custom-call | flops 134217728 | bytes 2097152 | tf_op jit(solution)/shard_map/part/pallas_call | solution.py:147
  36.7 5.4 %collective-permute-start.8 = (bf16[128,256]{1,0:T(8,128)(2,1)S(1)}, bf16[128,256]{1,0:T(8,128)(2,1)S(1)}, u32[]{:S(2)}, u32[]{:S(2)}) collective-permute-start(bf16[128,256]{1,0:T(8,128)(2,1)S(1)} %part.4), channel_id=1, source_target_pairs={{0,3},{1,2},{2,1},{3,0},{4,7},{5,6},{6,5},{7,4},{8,11},{9,10},{10,... | collective-permute-start | bytes 196616 | tf_op jit(solution)/shard_map/ppermute | solution.py:214
  42.1 0.8 %part.5 = bf16[128,256]{1,0:T(8,128)(2,1)S(1)} custom-call(bf16[64,4096]{1,0:T(8,128)(2,1)S(1)} %collective-permute-done.9.x_ref, bf16[256,4096]{1,0:T(8,128)(2,1)S(1)} %bitcast.9, f32[128,256]{1,0:T(8,128)S(1)} %get-tuple-element.39.refs_0_), custom_call_target="tpu_custom_call" | custom-call | flops 134217728 | bytes 2097152 | tf_op jit(solution)/shard_map/part/pallas_call | solution.py:147
  43.1 2.0 %collective-permute-done.11.x_ref = bf16[64,4096]{1,0:T(8,128)(2,1)S(1)} collective-permute-done((bf16[64,4096]{1,0:T(8,128)(2,1)S(1)}, bf16[64,4096]{1,0:T(8,128)(2,1)S(1)}, u32[]{:S(2)}, u32[]{:S(2)}) %collective-permute-start.11) | collective-permute-done | bytes 524320 | tf_op jit(solution)/shard_map/ppermute | solution.py:210
  45.1 0.8 %part.7 = bf16[128,256]{1,0:T(8,128)(2,1)S(1)} custom-call(bf16[64,4096]{1,0:T(8,128)(2,1)S(1)} %collective-permute-done.11.x_ref, bf16[256,4096]{1,0:T(8,128)(2,1)S(1)} %bitcast.10, f32[128,256]{1,0:T(8,128)S(1)} %get-tuple-element.41.refs_0_), custom_call_target="tpu_custom_call" | custom-call | flops 134217728 | bytes 2097152 | tf_op jit(solution)/shard_map/part/pallas_call | solution.py:147
  45.8 1.9 %collective-permute-start.12 = (bf16[128,256]{1,0:T(8,128)(2,1)S(1)}, bf16[128,256]{1,0:T(8,128)(2,1)S(1)}, u32[]{:S(2)}, u32[]{:S(2)}) collective-permute-start(bf16[128,256]{1,0:T(8,128)(2,1)S(1)} %part.7), channel_id=1, source_target_pairs={{0,1},{1,0},{2,3},{3,2},{4,5},{5,4},{6,7},{7,6},{8,9},{9,8},{10,11... | collective-permute-start | bytes 196616 | tf_op jit(solution)/shard_map/ppermute | solution.py:214
  47.7 0.7 %base.1 = (f32[3,64,256]{2,1,0:T(8,128)}, f32[1,256]{1,0:T(1,128)S(1)}) custom-call(f32[72,256]{1,0:T(8,128)S(1)} %get-tuple-element.24.refs_0_, f32[72,256]{1,0:T(8,128)S(1)} %collective-permute-done.refs_1_, f32[72,256]{1,0:T(8,128)S(1)} %collective-permute-done.1.refs_2_, f32[72,256]{1,0:T(8,128)S(1)} %collective-permute-done.2.refs_3_), custom_call_target="tpu_custom_call" | custom-call | tf_op jit(solution)/shard_map/base/pallas_call | solution.py:170
  48.4 2.3 %collective-permute-done.4.x_ref = bf16[64,4096]{1,0:T(8,128)(2,1)S(1)} collective-permute-done((bf16[64,4096]{1,0:T(8,128)(2,1)S(1)}, bf16[64,4096]{1,0:T(8,128)(2,1)S(1)}, u32[]{:S(2)}, u32[]{:S(2)}) %collective-permute-start.4) | collective-permute-done | bytes 524320 | tf_op jit(solution)/shard_map/ppermute | solution.py:210
  50.7 0.8 %part.6 = f32[128,256]{1,0:T(8,128)S(1)} custom-call(bf16[64,4096]{1,0:T(8,128)(2,1)S(1)} %collective-permute-done.4.x_ref, bf16[256,4096]{1,0:T(8,128)(2,1)S(1)} %bitcast.11, f32[128,256]{1,0:T(8,128)S(1)} %get-tuple-element.35.refs_0_, bf16[128,256]{1,0:T(8,128)(2,1)S(1)} %collective-permute-done.8.refs_1_, ...), custom_call_target="tpu_custom_call" | custom-call | flops 134217728 | bytes 2097152 | tf_op jit(solution)/shard_map/part/pallas_call | solution.py:147
  (21 shorter events, 1.7 us)
Async XLA Ops:
  0.0 17.3 %collective-permute-start.3 = (bf16[256,4096]{1,0:T(8,128)(2,1)}, bf16[256,4096]{1,0:T(8,128)(2,1)S(1)}, u32[]{:S(2)}, u32[]{:S(2)}) collective-permute-start(bf16[256,4096]{1,0:T(8,128)(2,1)} %bitcast.1.refs_0_.q_ref), channel_id=1, source_target_pairs={{4,12},{12,4},{5,13},{13,5},{6,14},{14,6},{7,15},{15,7},{20,28},{2... | collective-permute-start | bytes 6291464 | tf_op jit(solution)/shard_map/ppermute | solution.py:193
  1.6 1.6 %copy-start = (bf16[256,1,4096]{2,0,1:T(8,128)(2,1)S(1)}, bf16[256,1,4096]{2,0,1:T(8,128)(2,1)}, u32[]{:S(2)}) copy-start(bf16[256,1,4096]{2,0,1:T(8,128)(2,1)} %param.4) | copy-start | bytes 6291460
  3.2 0.7 %copy-start.2 = (f32[1,4096]{1,0:T(1,128)S(1)}, f32[1,4096]{1,0:T(1,128)}, u32[]{:S(2)}) copy-start(f32[1,4096]{1,0:T(1,128)} %refs_4_.1) | copy-start | bytes 49156
  3.9 10.6 %copy-start.3 = (f32[1,4096]{1,0:T(1,128)S(1)}, f32[1,4096]{1,0:T(1,128)}, u32[]{:S(2)}) copy-start(f32[1,4096]{1,0:T(1,128)} %refs_4_.1) | copy-start | bytes 49156
  7.1 27.2 %copy-start.1 = (bf16[256,1,4096]{2,0,1:T(8,128)(2,1)S(1)}, bf16[256,1,4096]{2,0,1:T(8,128)(2,1)}, u32[]{:S(2)}) copy-start(bf16[256,1,4096]{2,0,1:T(8,128)(2,1)} %param.4) | copy-start | bytes 6291460
  7.1 23.6 %collective-permute-start.5 = (bf16[256,4096]{1,0:T(8,128)(2,1)}, bf16[256,4096]{1,0:T(8,128)(2,1)S(1)}, u32[]{:S(2)}, u32[]{:S(2)}) collective-permute-start(bf16[256,4096]{1,0:T(8,128)(2,1)} %bitcast.1.refs_0_.q_ref), channel_id=1, source_target_pairs={{0,4},{8,12},{1,5},{9,13},{2,6},{10,14},{3,7},{11,15},{16,20},{24,... | collective-permute-start | bytes 6291464 | tf_op jit(solution)/shard_map/ppermute | solution.py:200
  12.9 4.4 %collective-permute-start = (f32[72,256]{1,0:T(8,128)S(1)}, f32[72,256]{1,0:T(8,128)S(1)}, u32[]{:S(2)}, u32[]{:S(2)}) collective-permute-start(f32[72,256]{1,0:T(8,128)S(1)} %get-tuple-element.25), channel_id=1, source_target_pairs={{0,1},{1,0},{2,3},{3,2},{4,5},{5,4},{6,7},{7,6},{8,9},{9,8},{10,11... | collective-permute-start | bytes 221192 | tf_op jit(solution)/shard_map/ppermute | solution.py:190
  17.3 17.0 %collective-permute-start.6 = (bf16[256,4096]{1,0:T(8,128)(2,1)S(1)}, bf16[256,4096]{1,0:T(8,128)(2,1)S(1)}, u32[]{:S(2)}, u32[]{:S(2)}) collective-permute-start(bf16[256,4096]{1,0:T(8,128)(2,1)S(1)} %collective-permute-done.3.refs_2_), channel_id=1, source_target_pairs={{4,0},{12,8},{5,1},{13,9},{6,2},{14,10},{7,3},{15,11},{20,16},{28,... | collective-permute-start | bytes 6291464 | tf_op jit(solution)/shard_map/ppermute | solution.py:205
  18.6 6.2 %collective-permute-start.1 = (f32[72,256]{1,0:T(8,128)S(1)}, f32[72,256]{1,0:T(8,128)S(1)}, u32[]{:S(2)}, u32[]{:S(2)}) collective-permute-start(f32[72,256]{1,0:T(8,128)S(1)} %get-tuple-element.26), channel_id=1, source_target_pairs={{0,3},{1,2},{2,1},{3,0},{4,7},{5,6},{6,5},{7,4},{8,11},{9,10},{10,... | collective-permute-start | bytes 221192 | tf_op jit(solution)/shard_map/ppermute | solution.py:190
  22.2 5.9 %collective-permute-start.2 = (f32[72,256]{1,0:T(8,128)S(1)}, f32[72,256]{1,0:T(8,128)S(1)}, u32[]{:S(2)}, u32[]{:S(2)}) collective-permute-start(f32[72,256]{1,0:T(8,128)S(1)} %get-tuple-element.27), channel_id=1, source_target_pairs={{0,2},{1,3},{2,0},{3,1},{4,6},{5,7},{6,4},{7,5},{8,10},{9,11},{10,... | collective-permute-start | bytes 221192 | tf_op jit(solution)/shard_map/ppermute | solution.py:190
  22.2 13.7 %collective-permute-start.7 = (bf16[64,4096]{1,0:T(8,128)(2,1)S(1)}, bf16[64,4096]{1,0:T(8,128)(2,1)S(1)}, u32[]{:S(2)}, u32[]{:S(2)}) collective-permute-start(bf16[64,4096]{1,0:T(8,128)(2,1)S(1)} %get-tuple-element.32), channel_id=1, source_target_pairs={{0,8},{8,0},{1,9},{9,1},{2,10},{10,2},{3,11},{11,3},{16,24},{24,16... | collective-permute-start | bytes 1572872 | tf_op jit(solution)/shard_map/ppermute | solution.py:210
  24.8 17.3 %collective-permute-start.9 = (bf16[64,4096]{1,0:T(8,128)(2,1)S(1)}, bf16[64,4096]{1,0:T(8,128)(2,1)S(1)}, u32[]{:S(2)}, u32[]{:S(2)}) collective-permute-start(bf16[64,4096]{1,0:T(8,128)(2,1)S(1)} %get-tuple-element.38), channel_id=1, source_target_pairs={{0,8},{8,0},{1,9},{9,1},{2,10},{10,2},{3,11},{11,3},{16,24},{24,16... | collective-permute-start | bytes 1572872 | tf_op jit(solution)/shard_map/ppermute | solution.py:210
  28.1 16.9 %collective-permute-start.11 = (bf16[64,4096]{1,0:T(8,128)(2,1)S(1)}, bf16[64,4096]{1,0:T(8,128)(2,1)S(1)}, u32[]{:S(2)}, u32[]{:S(2)}) collective-permute-start(bf16[64,4096]{1,0:T(8,128)(2,1)S(1)} %get-tuple-element.40), channel_id=1, source_target_pairs={{0,8},{8,0},{1,9},{9,1},{2,10},{10,2},{3,11},{11,3},{16,24},{24,16... | collective-permute-start | bytes 1572872 | tf_op jit(solution)/shard_map/ppermute | solution.py:210
  30.7 20.0 %collective-permute-start.4 = (bf16[64,4096]{1,0:T(8,128)(2,1)S(1)}, bf16[64,4096]{1,0:T(8,128)(2,1)S(1)}, u32[]{:S(2)}, u32[]{:S(2)}) collective-permute-start(bf16[64,4096]{1,0:T(8,128)(2,1)S(1)} %get-tuple-element.34), channel_id=1, source_target_pairs={{0,8},{8,0},{1,9},{9,1},{2,10},{10,2},{3,11},{11,3},{16,24},{24,16... | collective-permute-start | bytes 1572872 | tf_op jit(solution)/shard_map/ppermute | solution.py:210
  36.7 13.9 %collective-permute-start.8 = (bf16[128,256]{1,0:T(8,128)(2,1)S(1)}, bf16[128,256]{1,0:T(8,128)(2,1)S(1)}, u32[]{:S(2)}, u32[]{:S(2)}) collective-permute-start(bf16[128,256]{1,0:T(8,128)(2,1)S(1)} %part.4), channel_id=1, source_target_pairs={{0,3},{1,2},{2,1},{3,0},{4,7},{5,6},{6,5},{7,4},{8,11},{9,10},{10,... | collective-permute-start | bytes 196616 | tf_op jit(solution)/shard_map/ppermute | solution.py:214
  42.9 7.8 %collective-permute-start.10 = (bf16[128,256]{1,0:T(8,128)(2,1)S(1)}, bf16[128,256]{1,0:T(8,128)(2,1)S(1)}, u32[]{:S(2)}, u32[]{:S(2)}) collective-permute-start(bf16[128,256]{1,0:T(8,128)(2,1)S(1)} %part.5), channel_id=1, source_target_pairs={{0,2},{1,3},{2,0},{3,1},{4,6},{5,7},{6,4},{7,5},{8,10},{9,11},{10,... | collective-permute-start | bytes 196616 | tf_op jit(solution)/shard_map/ppermute | solution.py:214
  45.8 5.6 %collective-permute-start.12 = (bf16[128,256]{1,0:T(8,128)(2,1)S(1)}, bf16[128,256]{1,0:T(8,128)(2,1)S(1)}, u32[]{:S(2)}, u32[]{:S(2)}) collective-permute-start(bf16[128,256]{1,0:T(8,128)(2,1)S(1)} %part.7), channel_id=1, source_target_pairs={{0,1},{1,0},{2,3},{3,2},{4,5},{5,4},{6,7},{7,6},{8,9},{9,8},{10,11... | collective-permute-start | bytes 196616 | tf_op jit(solution)/shard_map/ppermute | solution.py:214
